TPU v7x, 32 devices: a whole 2x2x4 slice. The times are simulated.
32 devices in a mesh: site: 2 (over x), var: 8 (over z, y), sub: 2 (over core).
Axes of the slice: x: 2, y: 2, z: 4, core: 2. Of those that a mesh axis runs over, the one named last changes fastest.
Arguments:
- fault_points: float32 [2, 1024], P(None, 'site'), parts along dimension 1, may hold values from 0 to 40
- hypocenter: int32 [16384], P(('site', 'var')), parts along dimension 0, may hold values from 0 to 511
- velocity: float32 [16384], P(('site', 'var')), parts along dimension 0, may hold values from 2 to 3.5
- rise_time: float32 [16384], P(('site', 'var')), parts along dimension 0, may hold values from 0.2 to 1
- member_mask: int32 [16384, 512], P(('site', 'var'), 'sub'), parts along dimension 0, may hold values 0 or 1
- slip_amount: float32 [16384, 512], P(('site', 'var'), 'sub'), parts along dimension 0, may hold values from 0.3 to 3
- moment_tensor: float32 [6, 1024], P(None, ('site', 'sub')), parts along dimension 1, may hold values from -6 to 6
- strain_green: bfloat16 [4, 6, 2, 256, 16, 128], P('site', None, 'sub', 'var'), parts along dimension 0, may hold values from -0.109375 to 0.109375
- station_ids: int32 [256], P('site'), parts along dimension 0, may hold values from 0 to 127, each once
Outputs:
- spectra: float32 [16, 2, 128, 16384], P(None, None, 'sub', ('site', 'var')), parts along dimension 3
There are 2 independent parts, one for each index of `site`. A program takes and returns all parts, laid end to end along the dimension named above; each array names one. Nothing has to cross between parts.
Inputs may be any that keep to these rules, and one draw needn't show every extreme that they name: `station_ids`: each station once.
All inputs are finite; a program needn't handle non-finite values. No bound on the sum of `member_mask` on one device may be relied on, other than what follows from the above.
Results may differ from a plain program's by a relative error of at most 0.0041.
Values may be sent and summed in bfloat16 or wider, within the bound.
No kernel may reach another device: no remote copies, remote signals or barrier semaphores. Data moves between devices by JAX's collectives and lax.ppermute only.
A program may use at most 192 MiB of HBM per device.

v0:
```python
import math

import jax
import jax.numpy as jnp
from jax import lax
from jax.sharding import PartitionSpec as P


def rotate(green, tensor, station_ids):
    total = green[:, 0].astype(jnp.float32) * tensor[0][None, :, None, None]
    for comp in range(1, 6):
        total = total + green[:, comp].astype(jnp.float32) * tensor[comp][None, :, None, None]
    return jnp.take(total, station_ids, axis=3).astype(jnp.bfloat16)


def slip_spectra(points, focus, velocity, rise_time, amount, omega):
    east_gap = points[0][None, :] - focus[0][:, None]
    north_gap = points[1][None, :] - focus[1][:, None]
    delay = jnp.sqrt(east_gap * east_gap + north_gap * north_gap) / velocity[:, None]

    def at_freq(pulsation):
        phase = pulsation * delay
        damping = (pulsation * rise_time)[:, None]
        scale = amount / (1.0 + damping * damping)
        cosine = jnp.cos(phase)
        sine = jnp.sin(phase)
        real = scale * (cosine - damping * sine)
        imag = -scale * (sine + damping * cosine)
        return jnp.concatenate([real, imag], axis=1).astype(jnp.bfloat16)

    return lax.map(at_freq, omega)


def contract(slips, rotated):
    upper = jnp.concatenate([rotated[0], rotated[1]], axis=2)
    lower = jnp.concatenate([-rotated[1], rotated[0]], axis=2)
    blocks = jnp.concatenate([upper, lower], axis=0)
    sums = jnp.einsum("fvm,mfs->fsv", slips, blocks, preferred_element_type=jnp.float32)
    return sums.reshape((slips.shape[0], 2, rotated.shape[3], slips.shape[1]))


def shards(
    fault_points,
    hypocenter,
    velocity,
    rise_time,
    member_mask,
    slip_amount,
    moment_tensor,
    strain_green,
    station_ids,
):
    half_count = moment_tensor.shape[1]
    freq_count = strain_green.shape[4]
    focus = jnp.take(fault_points, hypocenter, axis=1)
    amount = member_mask.astype(jnp.float32) * slip_amount
    omega = (jnp.arange(freq_count, dtype=jnp.int32) + 1).astype(jnp.float32) * (
        2.0 * math.pi * 0.0625
    )
    rotated = rotate(
        lax.all_gather(strain_green, "var", axis=3, tiled=True)[:, :, 0], moment_tensor, station_ids
    )
    first = lax.axis_index("sub") * half_count
    own = lax.dynamic_slice_in_dim(fault_points, first, half_count, 1)
    slips = slip_spectra(own, focus, velocity, rise_time, amount, omega)
    partial_sums = contract(slips, rotated)
    return lax.psum_scatter(partial_sums, "sub", scatter_dimension=2, tiled=True)


def solution(mesh):
    placed = (
        P(None, "site"),
        P(("site", "var")),
        P(("site", "var")),
        P(("site", "var")),
        P(("site", "var"), "sub"),
        P(("site", "var"), "sub"),
        P(None, ("site", "sub")),
        P("site", None, "sub", "var", None, None),
        P("site"),
    )
    return jax.shard_map(
        shards,
        mesh=mesh,
        in_specs=placed,
        out_specs=P(None, None, "sub", ("site", "var")),
        check_vma=False,
    )
```

profile of v0, /device:TPU:0, one launch (start us, length us, event | category | flops | bytes accessed | tf_op | source)
XLA Modules:
  0.0 260.9 jit_solution(4156482265791068219)
XLA Ops:
  6.6 3.2 %copy.19 = bf16[2,6,1,32,16,128]{5,4,2,1,0,3:T(8,128)(2,1)} copy(bf16[2,6,1,32,16,128]{5,4,3,2,1,0:T(8,128)(2,1)} %param.18) | data formatting | bytes 3145728 | tf_op args[7]
  10.1 2.8 %gather_fusion.1 = f32[1024,2]{1,0:T(8,128)S(1)} fusion(f32[2,512]{0,1:T(8,128)S(1)} %copy.22, s32[1024]{0:T(1024)S(1)} %fusion.21), kind=kCustom, calls=%fused_computation.1 | custom fusion | bytes 20480 | tf_op jit(solution)/shard_map/jit(_take)/gather | solution.py:55
  14.0 136.3 %while.11 = (s32[]{:T(128)}, bf16[16,1024,512]{2,1,0:T(8,128)(2,1)}, f32[16]{0:T(128)S(1)}, f32[1024]{0:T(1024)S(1)}, f32[1024,256]{1,0:T(8,128)S(1)}, /*index=5...) while((s32[]{:T(128)}, ...), condition=%wide.region_1.2_spmd.clone, body=%wide.region_0.1_spmd.clone.sunk | while | flops 6556674 | bytes 4229761 | solution.py:31
  15.3 6.1 %fusion.28 = (bf16[1,1024,256]{2,1,0:T(8,128)(2,1)S(1)}, bf16[1,1024,256]{2,1,0:T(8,128)(2,1)S(1)}) fusion(f32[1024]{0:T(1024)S(1)} %get-tuple-element.166, f32[1024]{0:T(1024)S(1)} %get-tuple-element.201, f32[1024]{0:T(1024)S(1)} %get-tuple-element.199, f32[256]{0:T(256)S(1)} %get-tuple-element.200, f32[1024]{0:T(1024)S(1)} %get-tuple-element.197, ...), kind=kLoop, calls=%fused_computation.7.clone.1 | loop fusion | flops 4456448 | bytes 2119684 | tf_op jit(solution)/shard_map/while/body/eval_jaxpr/concatenate | solution.py:29
  23.8 6.1 %fusion.28 = (bf16[1,1024,256]{2,1,0:T(8,128)(2,1)S(1)}, bf16[1,1024,256]{2,1,0:T(8,128)(2,1)S(1)}) fusion(f32[1024]{0:T(1024)S(1)} %get-tuple-element.166, f32[1024]{0:T(1024)S(1)} %get-tuple-element.201, f32[1024]{0:T(1024)S(1)} %get-tuple-element.199, f32[256]{0:T(256)S(1)} %get-tuple-element.200, f32[1024]{0:T(1024)S(1)} %get-tuple-element.197, ...), kind=kLoop, calls=%fused_computation.7.clone.1 | loop fusion | flops 4456448 | bytes 2119684 | tf_op jit(solution)/shard_map/while/body/eval_jaxpr/concatenate | solution.py:29
  32.3 6.1 %fusion.28 = (bf16[1,1024,256]{2,1,0:T(8,128)(2,1)S(1)}, bf16[1,1024,256]{2,1,0:T(8,128)(2,1)S(1)}) fusion(f32[1024]{0:T(1024)S(1)} %get-tuple-element.166, f32[1024]{0:T(1024)S(1)} %get-tuple-element.201, f32[1024]{0:T(1024)S(1)} %get-tuple-element.199, f32[256]{0:T(256)S(1)} %get-tuple-element.200, f32[1024]{0:T(1024)S(1)} %get-tuple-element.197, ...), kind=kLoop, calls=%fused_computation.7.clone.1 | loop fusion | flops 4456448 | bytes 2119684 | tf_op jit(solution)/shard_map/while/body/eval_jaxpr/concatenate | solution.py:29
  40.8 6.1 %fusion.28 = (bf16[1,1024,256]{2,1,0:T(8,128)(2,1)S(1)}, bf16[1,1024,256]{2,1,0:T(8,128)(2,1)S(1)}) fusion(f32[1024]{0:T(1024)S(1)} %get-tuple-element.166, f32[1024]{0:T(1024)S(1)} %get-tuple-element.201, f32[1024]{0:T(1024)S(1)} %get-tuple-element.199, f32[256]{0:T(256)S(1)} %get-tuple-element.200, f32[1024]{0:T(1024)S(1)} %get-tuple-element.197, ...), kind=kLoop, calls=%fused_computation.7.clone.1 | loop fusion | flops 4456448 | bytes 2119684 | tf_op jit(solution)/shard_map/while/body/eval_jaxpr/concatenate | solution.py:29
  49.4 6.1 %fusion.28 = (bf16[1,1024,256]{2,1,0:T(8,128)(2,1)S(1)}, bf16[1,1024,256]{2,1,0:T(8,128)(2,1)S(1)}) fusion(f32[1024]{0:T(1024)S(1)} %get-tuple-element.166, f32[1024]{0:T(1024)S(1)} %get-tuple-element.201, f32[1024]{0:T(1024)S(1)} %get-tuple-element.199, f32[256]{0:T(256)S(1)} %get-tuple-element.200, f32[1024]{0:T(1024)S(1)} %get-tuple-element.197, ...), kind=kLoop, calls=%fused_computation.7.clone.1 | loop fusion | flops 4456448 | bytes 2119684 | tf_op jit(solution)/shard_map/while/body/eval_jaxpr/concatenate | solution.py:29
  57.8 6.1 %fusion.28 = (bf16[1,1024,256]{2,1,0:T(8,128)(2,1)S(1)}, bf16[1,1024,256]{2,1,0:T(8,128)(2,1)S(1)}) fusion(f32[1024]{0:T(1024)S(1)} %get-tuple-element.166, f32[1024]{0:T(1024)S(1)} %get-tuple-element.201, f32[1024]{0:T(1024)S(1)} %get-tuple-element.199, f32[256]{0:T(256)S(1)} %get-tuple-element.200, f32[1024]{0:T(1024)S(1)} %get-tuple-element.197, ...), kind=kLoop, calls=%fused_computation.7.clone.1 | loop fusion | flops 4456448 | bytes 2119684 | tf_op jit(solution)/shard_map/while/body/eval_jaxpr/concatenate | solution.py:29
  66.4 6.1 %fusion.28 = (bf16[1,1024,256]{2,1,0:T(8,128)(2,1)S(1)}, bf16[1,1024,256]{2,1,0:T(8,128)(2,1)S(1)}) fusion(f32[1024]{0:T(1024)S(1)} %get-tuple-element.166, f32[1024]{0:T(1024)S(1)} %get-tuple-element.201, f32[1024]{0:T(1024)S(1)} %get-tuple-element.199, f32[256]{0:T(256)S(1)} %get-tuple-element.200, f32[1024]{0:T(1024)S(1)} %get-tuple-element.197, ...), kind=kLoop, calls=%fused_computation.7.clone.1 | loop fusion | flops 4456448 | bytes 2119684 | tf_op jit(solution)/shard_map/while/body/eval_jaxpr/concatenate | solution.py:29
  74.9 6.1 %fusion.28 = (bf16[1,1024,256]{2,1,0:T(8,128)(2,1)S(1)}, bf16[1,1024,256]{2,1,0:T(8,128)(2,1)S(1)}) fusion(f32[1024]{0:T(1024)S(1)} %get-tuple-element.166, f32[1024]{0:T(1024)S(1)} %get-tuple-element.201, f32[1024]{0:T(1024)S(1)} %get-tuple-element.199, f32[256]{0:T(256)S(1)} %get-tuple-element.200, f32[1024]{0:T(1024)S(1)} %get-tuple-element.197, ...), kind=kLoop, calls=%fused_computation.7.clone.1 | loop fusion | flops 4456448 | bytes 2119684 | tf_op jit(solution)/shard_map/while/body/eval_jaxpr/concatenate | solution.py:29
  83.4 6.1 %fusion.28 = (bf16[1,1024,256]{2,1,0:T(8,128)(2,1)S(1)}, bf16[1,1024,256]{2,1,0:T(8,128)(2,1)S(1)}) fusion(f32[1024]{0:T(1024)S(1)} %get-tuple-element.166, f32[1024]{0:T(1024)S(1)} %get-tuple-element.201, f32[1024]{0:T(1024)S(1)} %get-tuple-element.199, f32[256]{0:T(256)S(1)} %get-tuple-element.200, f32[1024]{0:T(1024)S(1)} %get-tuple-element.197, ...), kind=kLoop, calls=%fused_computation.7.clone.1 | loop fusion | flops 4456448 | bytes 2119684 | tf_op jit(solution)/shard_map/while/body/eval_jaxpr/concatenate | solution.py:29
  92.0 6.1 %fusion.28 = (bf16[1,1024,256]{2,1,0:T(8,128)(2,1)S(1)}, bf16[1,1024,256]{2,1,0:T(8,128)(2,1)S(1)}) fusion(f32[1024]{0:T(1024)S(1)} %get-tuple-element.166, f32[1024]{0:T(1024)S(1)} %get-tuple-element.201, f32[1024]{0:T(1024)S(1)} %get-tuple-element.199, f32[256]{0:T(256)S(1)} %get-tuple-element.200, f32[1024]{0:T(1024)S(1)} %get-tuple-element.197, ...), kind=kLoop, calls=%fused_computation.7.clone.1 | loop fusion | flops 4456448 | bytes 2119684 | tf_op jit(solution)/shard_map/while/body/eval_jaxpr/concatenate | solution.py:29
  100.5 6.1 %fusion.28 = (bf16[1,1024,256]{2,1,0:T(8,128)(2,1)S(1)}, bf16[1,1024,256]{2,1,0:T(8,128)(2,1)S(1)}) fusion(f32[1024]{0:T(1024)S(1)} %get-tuple-element.166, f32[1024]{0:T(1024)S(1)} %get-tuple-element.201, f32[1024]{0:T(1024)S(1)} %get-tuple-element.199, f32[256]{0:T(256)S(1)} %get-tuple-element.200, f32[1024]{0:T(1024)S(1)} %get-tuple-element.197, ...), kind=kLoop, calls=%fused_computation.7.clone.1 | loop fusion | flops 4456448 | bytes 2119684 | tf_op jit(solution)/shard_map/while/body/eval_jaxpr/concatenate | solution.py:29
  109.0 6.1 %fusion.28 = (bf16[1,1024,256]{2,1,0:T(8,128)(2,1)S(1)}, bf16[1,1024,256]{2,1,0:T(8,128)(2,1)S(1)}) fusion(f32[1024]{0:T(1024)S(1)} %get-tuple-element.166, f32[1024]{0:T(1024)S(1)} %get-tuple-element.201, f32[1024]{0:T(1024)S(1)} %get-tuple-element.199, f32[256]{0:T(256)S(1)} %get-tuple-element.200, f32[1024]{0:T(1024)S(1)} %get-tuple-element.197, ...), kind=kLoop, calls=%fused_computation.7.clone.1 | loop fusion | flops 4456448 | bytes 2119684 | tf_op jit(solution)/shard_map/while/body/eval_jaxpr/concatenate | solution.py:29
  117.5 6.1 %fusion.28 = (bf16[1,1024,256]{2,1,0:T(8,128)(2,1)S(1)}, bf16[1,1024,256]{2,1,0:T(8,128)(2,1)S(1)}) fusion(f32[1024]{0:T(1024)S(1)} %get-tuple-element.166, f32[1024]{0:T(1024)S(1)} %get-tuple-element.201, f32[1024]{0:T(1024)S(1)} %get-tuple-element.199, f32[256]{0:T(256)S(1)} %get-tuple-element.200, f32[1024]{0:T(1024)S(1)} %get-tuple-element.197, ...), kind=kLoop, calls=%fused_computation.7.clone.1 | loop fusion | flops 4456448 | bytes 2119684 | tf_op jit(solution)/shard_map/while/body/eval_jaxpr/concatenate | solution.py:29
  126.1 6.1 %fusion.28 = (bf16[1,1024,256]{2,1,0:T(8,128)(2,1)S(1)}, bf16[1,1024,256]{2,1,0:T(8,128)(2,1)S(1)}) fusion(f32[1024]{0:T(1024)S(1)} %get-tuple-element.166, f32[1024]{0:T(1024)S(1)} %get-tuple-element.201, f32[1024]{0:T(1024)S(1)} %get-tuple-element.199, f32[256]{0:T(256)S(1)} %get-tuple-element.200, f32[1024]{0:T(1024)S(1)} %get-tuple-element.197, ...), kind=kLoop, calls=%fused_computation.7.clone.1 | loop fusion | flops 4456448 | bytes 2119684 | tf_op jit(solution)/shard_map/while/body/eval_jaxpr/concatenate | solution.py:29
  134.6 6.1 %fusion.28 = (bf16[1,1024,256]{2,1,0:T(8,128)(2,1)S(1)}, bf16[1,1024,256]{2,1,0:T(8,128)(2,1)S(1)}) fusion(f32[1024]{0:T(1024)S(1)} %get-tuple-element.166, f32[1024]{0:T(1024)S(1)} %get-tuple-element.201, f32[1024]{0:T(1024)S(1)} %get-tuple-element.199, f32[256]{0:T(256)S(1)} %get-tuple-element.200, f32[1024]{0:T(1024)S(1)} %get-tuple-element.197, ...), kind=kLoop, calls=%fused_computation.7.clone.1 | loop fusion | flops 4456448 | bytes 2119684 | tf_op jit(solution)/shard_map/while/body/eval_jaxpr/concatenate | solution.py:29
  143.1 6.1 %fusion.28 = (bf16[1,1024,256]{2,1,0:T(8,128)(2,1)S(1)}, bf16[1,1024,256]{2,1,0:T(8,128)(2,1)S(1)}) fusion(f32[1024]{0:T(1024)S(1)} %get-tuple-element.166, f32[1024]{0:T(1024)S(1)} %get-tuple-element.201, f32[1024]{0:T(1024)S(1)} %get-tuple-element.199, f32[256]{0:T(256)S(1)} %get-tuple-element.200, f32[1024]{0:T(1024)S(1)} %get-tuple-element.197, ...), kind=kLoop, calls=%fused_computation.7.clone.1 | loop fusion | flops 4456448 | bytes 2119684 | tf_op jit(solution)/shard_map/while/body/eval_jaxpr/concatenate | solution.py:29
  150.3 38.8 %all-gather.2.cloned.1.call-done = bf16[2,6,1,256,16,128]{5,4,2,1,0,3:T(8,128)(2,1)} async-done(((bf16[2,6,1,32,16,128]{5,4,2,1,0,3:T(8,128)(2,1)}), bf16[2,6,1,256,16,128]{5,4,2,1,0,3:T(8,128)(2,1)}) %all-gather.2.cloned.1.call-update) | async-done | bytes 12582928 | tf_op jit(solution)/shard_map/all_gather | solution.py:61
  189.1 18.2 %copy.20 = bf16[2,6,1,256,16,128]{3,4,0,5,1,2:T(8,128)(2,1)} copy(bf16[2,6,1,256,16,128]{5,4,2,1,0,3:T(8,128)(2,1)} %all-gather.2.cloned.1.call-done) | data formatting | bytes 25165824 | tf_op jit(solution)/shard_map/all_gather | solution.py:61
  207.3 6.8 %fusion.14 = bf16[2,256,16,128]{1,2,0,3:T(8,128)(2,1)} fusion(bf16[2,6,256,16,128]{2,3,0,4,1:T(8,128)(2,1)} %bitcast.60, f32[256]{0:T(256)S(1)} %bitcast.68, f32[256]{0:T(256)S(1)} %bitcast.69, f32[256]{0:T(256)S(1)} %bitcast.65, f32[256]{0:T(256)S(1)} %bitcast.66, f32[256]{0:T(256)S(1)} %bitcast.67, f32[256]{0:T(256)S(1)} %bitcast.64), kind=kLoop, calls=%fused_computation.23 | loop fusion | flops 18874368 | bytes 14686208 | tf_op jit(solution)/shard_map/add | solution.py:12
  218.0 11.5 %fusion.6 = f32[16,256,1024]{2,1,0:T(8,128)} fusion(bf16[16,1024,512]{2,1,0:T(8,128)(2,1)} %get-tuple-element.37, bf16[256,16,128]{0,2,1:T(8,128)(2,1)S(1)} %get-tuple-element.92, bf16[256,16,128]{0,2,1:T(8,128)(2,1)S(1)} %fusion.23, bf16[256,16,128]{0,2,1:T(8,128)(2,1)S(1)} %get-tuple-element.91), kind=kOutput, calls=%fused_computation.14 | convolution fusion | flops 4311744512 | bytes 36700160 | tf_op jit(solution)/shard_map/fvm,mfs->fsv/dot_general | solution.py:38
  229.5 24.6 %reduce-scatter.2.cloned.1.call-done = f32[16,2,64,1024]{3,2,1,0:T(8,128)} async-done(((f32[16,2,128,1024]{3,2,1,0:T(8,128)}), f32[16,2,64,1024]{3,2,1,0:T(8,128)}) %reduce-scatter.2.cloned.1.call-update) | async-done | bytes 8388624 | tf_op jit(solution)/shard_map/reduce_scatter | solution.py:67
  (85 shorter events, 43.1 us)
Async XLA Ops:
  6.5 3.3 %copy-start.5 = (f32[2,512]{1,0:T(2,128)S(1)}, f32[2,512]{1,0:T(2,128)}, u32[]{:S(2)}) copy-start(f32[2,512]{1,0:T(2,128)} %param.11) | copy-start | bytes 12292
  6.5 3.5 %copy-start.4 = (s32[1024]{0:T(1024)S(1)}, s32[1024]{0:T(1024)}, u32[]{:S(2)}) copy-start(s32[1024]{0:T(1024)} %param.12) | copy-start | bytes 12292
  6.5 6.4 %copy-start.7 = (s32[128]{0:T(128)S(1)}, s32[128]{0:T(128)}, u32[]{:S(2)}) copy-start(s32[128]{0:T(128)} %param.19) | copy-start | bytes 1540
  6.5 7.2 %copy-start.6 = (f32[6,256]{1,0:T(8,128)S(1)}, f32[6,256]{1,0:T(8,128)}, u32[]{:S(2)}) copy-start(f32[6,256]{1,0:T(8,128)} %param.17) | copy-start | bytes 18436
  6.5 7.2 %copy-start.1 = (s32[1024,256]{1,0:T(8,128)S(1)}, s32[1024,256]{1,0:T(8,128)}, u32[]{:S(2)}) copy-start(s32[1024,256]{1,0:T(8,128)} %param.15) | copy-start | bytes 3145732
  6.5 7.2 %copy-start = (f32[1024,256]{1,0:T(8,128)S(1)}, f32[1024,256]{1,0:T(8,128)}, u32[]{:S(2)}) copy-start(f32[1024,256]{1,0:T(8,128)} %param.16) | copy-start | bytes 3145732
  6.6 182.5 %all-gather.2.cloned.1.call-start = ((), (), s32[]{:S(2)}) async-start(), calls=%async_computation.1 | async-start | bytes 14155776 | tf_op jit(solution)/shard_map/all_gather | solution.py:61
  9.8 4.2 %copy-start.2 = (f32[1024]{0:T(1024)S(1)}, f32[1024]{0:T(1024)}, u32[]{:S(2)}) copy-start(f32[1024]{0:T(1024)} %param.13) | copy-start | bytes 12292
  9.8 4.2 %copy-start.3 = (f32[1024]{0:T(1024)S(1)}, f32[1024]{0:T(1024)}, u32[]{:S(2)}) copy-start(f32[1024]{0:T(1024)} %param.14) | copy-start | bytes 12292
  9.8 244.3 %reduce-scatter.2.cloned.1.call-start = ((), (), s32[]{:S(2)}) async-start(), calls=%async_computation.2 | async-start | bytes 25165824 | tf_op jit(solution)/shard_map/reduce_scatter | solution.py:67
Sparse Core Ops, SparseCore 0:
  9.9 179.1 all-gather.1
  229.6 24.4 reduce-scatter.1
where the time goes:
time: 262 us; the launch traced here: 261 us
  other arithmetic  134 us (51%)
  waiting for transfers between devices  63.4 us (24%)
  local copies, waits for them, and re-layouts  37.8 us (14%)
  between operations  13.6 us (5%)
  matrix products  11.5 us (4%)
    concatenate x16, other arithmetic, at_freq(): return jnp.concatenate([real, imag], axis=1).astype(jnp.bfloat16)  98.1 us
    all_gather x1, waiting for transfers between devices, shards(): lax.all_gather(strain_green, 'var', axis=3, tiled=True)[:, :, 0]  38.8 us
    reduce_scatter x1, waiting for transfers between devices, shards(): lax.psum_scatter(partial_sums, 'sub', scatter_dimension=2, tiled=True)  24.6 us
    all_gather x1, local copies, waits for them, and re-layouts, shards(): lax.all_gather(strain_green, 'var', axis=3, tiled=True)[:, :, 0]  18.2 us
    dynamic_update_slice x16, other arithmetic, slip_spectra(): return lax.map(at_freq, omega)  17.3 us
    dot_general x1, matrix products, contract(): jnp.einsum('fvm,mfs->fsv', slips, blocks, preferred_element_type=jnp.floa...  11.5 us
    dynamic_slice x16, local copies, waits for them, and re-layouts, slip_spectra(): return lax.map(at_freq, omega)  10.4 us
    add x16, other arithmetic, at_freq(): scale = amount / (1.0 + damping * damping)  10.2 us
  transfers between devices with their start and end apart: 2, of which 2 were waited for; matrix products, arithmetic and copies ran while one was open for 54% of the time, Pallas kernels for 0%

commit v1 on v0

v1 whole, which is shorter than its diff:
```python
import functools

import jax
import jax.numpy as jnp
from jax import lax
from jax.experimental import pallas as pl
from jax.experimental.pallas import tpu as pltpu
from jax.sharding import PartitionSpec as P

VMEM = pl.BlockSpec(memory_space=pltpu.VMEM)
SMEM = pl.BlockSpec(memory_space=pltpu.SMEM)
ANY = pl.BlockSpec(memory_space=pl.ANY)
PARAMS = pltpu.CompilerParams(vmem_limit_bytes=56 * 2**20)
BASE_FREQ = 0.0625
LANES = 256


def rotate_kernel(green_ref, tensor_ref, ids_ref, own_ref, other_ref, sums, rows):
    _, comps, count, freqs, stations = green_ref.shape
    half = stations // 2
    first = lax.axis_index("var") * count

    def one_subfault(m, carry):
        for part in range(2):
            total = green_ref[part, 0, m].astype(jnp.float32) * tensor_ref[0, first + m]
            for comp in range(1, comps):
                total = total + green_ref[part, comp, m].astype(jnp.float32) * tensor_ref[comp, first + m]
            at = pl.ds(pl.multiple_of(m * freqs, freqs), freqs)
            sums[at, part * stations : (part + 1) * stations] = total.astype(jnp.bfloat16)
        return carry

    lax.fori_loop(0, count, one_subfault, 0, unroll=4)

    lane = lax.broadcasted_iota(jnp.int32, (1, stations), 1)
    ids = ids_ref[...]
    turned = pltpu.roll(ids, half, 1)
    low = jnp.where(lane < half, ids, turned)
    high = jnp.where(lane < half, turned, ids)
    is_first = lax.axis_index("sub") == 0
    wanted = jnp.concatenate([jnp.where(is_first, low, high), jnp.where(is_first, high, low)], axis=1)
    row = lax.broadcasted_iota(jnp.int32, (2 * stations, 2 * stations), 0)
    column = lax.broadcasted_iota(jnp.int32, (2 * stations, 2 * stations), 1)
    part_of_column = (column // half) % 2
    picks = (row == wanted + part_of_column * stations).astype(jnp.float32).astype(jnp.bfloat16)
    picked = jnp.dot(sums[...], picks, preferred_element_type=jnp.float32)
    rows[0] = picked[:, :stations]
    rows[1] = picked[:, stations:]
    for k in range(freqs):
        at = pl.ds(k, count, stride=freqs)
        own_ref[k] = rows[0, at, :].astype(jnp.bfloat16)
        other_ref[k] = rows[1, at, :].astype(jnp.bfloat16)


def rotate(green, tensor, station_ids):
    _, _, count, freqs, stations = green.shape
    piece = jax.ShapeDtypeStruct((freqs, count, stations), jnp.bfloat16)
    return pl.pallas_call(
        rotate_kernel,
        out_shape=(piece, piece),
        in_specs=[VMEM, SMEM, VMEM],
        out_specs=(VMEM, VMEM),
        scratch_shapes=[
            pltpu.VMEM((count * freqs, 2 * stations), jnp.bfloat16),
            pltpu.VMEM((2, count * freqs, stations), jnp.float32),
        ],
        compiler_params=PARAMS,
        name="rotate",
    )(green, tensor, station_ids.reshape((1, stations)))


def amount_kernel(mask_ref, slip_ref, out_ref):
    out_ref[...] = (mask_ref[...].astype(jnp.float32) * slip_ref[...]).T


def amounts(mask, slip):
    variations, subfaults = mask.shape
    block = pl.BlockSpec((LANES, subfaults), lambda i: (i, 0))
    return pl.pallas_call(
        amount_kernel,
        out_shape=jax.ShapeDtypeStruct((subfaults, variations), jnp.float32),
        grid=(variations // LANES,),
        in_specs=[block, block],
        out_specs=pl.BlockSpec((subfaults, LANES), lambda i: (0, i)),
        compiler_params=PARAMS,
        name="amounts",
    )(mask, slip)


SIN = (3.14159264, -5.16771008, 2.55007751, -0.598291190, 0.0776574420)
COS = (0.999999953, -4.93479283, 4.05841131, -1.33187624, 0.219688854)


def sine_cosine(turns):
    rest = turns - jnp.floor(turns + 0.5)
    square = rest * rest
    sine = SIN[-1]
    for c in SIN[-2::-1]:
        sine = sine * square + c
    sine = sine * rest
    cosine = COS[-1]
    for c in COS[-2::-1]:
        cosine = cosine * square + c
    return 2.0 * sine * cosine, 1.0 - 2.0 * sine * sine


def spectra_kernel(
    first, count, pieces, steps, off_ref, points_ref, focus_ref, velocity_ref, rise_ref, own_ref, other_ref, *refs
):
    piece_refs = refs[:pieces]
    out_ref, rotated, columns = refs[-5], refs[-4], refs[-3]
    slots = (refs[-2], refs[-1])
    half = own_ref.shape[0]
    step = pl.program_id(0)
    chunk = 32
    loops = 2 * half // (2 * chunk)

    @pl.when(step == 0)
    def _():
        for piece, ref in enumerate(piece_refs):
            rows = ref.shape[1] // 2
            at = pl.multiple_of(off_ref[piece], 32)
            rotated[:, pl.ds(at, rows), :] = ref[:, :rows, :]
            rotated[:, pl.ds(half + at, rows), :] = ref[:, rows:, :]
        for axis in range(2):
            wide = jnp.broadcast_to(points_ref[axis : axis + 1, :], (128, 2 * half))
            columns[axis] = wide.T

    def slips_of(row, lanes, source, source_row, slot):
        at = pl.ds(row, chunk)
        east = columns[0, at, :] - focus_ref[0:1, lanes]
        north = columns[1, at, :] - focus_ref[1:2, lanes]
        gap = east * east + north * north
        distance = gap * lax.rsqrt(jnp.maximum(gap, 1e-30))
        turns = distance * (BASE_FREQ / velocity_ref[0:1, lanes])
        sine, cosine = sine_cosine(turns)
        amount = source[pl.ds(source_row, chunk), lanes]
        twice = 2.0 * cosine
        re_last, im_last = amount, None
        re, im = amount * cosine, amount * sine
        for k in range(first + count):
            if k >= first:
                slot[0, k - first, at, lanes] = re.astype(jnp.bfloat16)
                slot[1, k - first, at, lanes] = im.astype(jnp.bfloat16)
            re, re_last = twice * re - re_last, re
            im, im_last = (twice * im if im_last is None else twice * im - im_last), im

    def sums_of(k, slot):
        dims = (((0,), (0,)), ((), ()))
        by_re = lax.dot_general(rotated[k], slot[0, k], dims, preferred_element_type=jnp.float32)
        by_im = lax.dot_general(rotated[k], slot[1, k], dims, preferred_element_type=jnp.float32)
        stations = by_re.shape[0] // 2
        re = by_re[:stations] + by_im[stations:]
        im = by_re[stations:] - by_im[:stations]
        pulsation = (first + k + 1).astype(jnp.float32) * (2.0 * jnp.pi * BASE_FREQ)
        damping = pulsation * rise_ref[0:1, :]
        scale = 1.0 / (1.0 + damping * damping)
        tilt = scale * damping
        out_ref[k, 0] = scale * re + tilt * im
        out_ref[k, 1] = scale * im - tilt * re

    def run(fill, drain):
        def body(j, carry):
            if fill is not None:
                for lane in range(0, LANES, 128):
                    lanes = slice(lane, lane + 128)
                    row = pl.multiple_of(j * chunk, chunk)
                    slips_of(row, lanes, own_ref, row, fill)
                    slips_of(pl.multiple_of(half + j * chunk, chunk), lanes, other_ref, row, fill)
            if drain is not None:
                for k in range(count // loops):
                    sums_of(j * (count // loops) + k, drain)
            return carry

        lax.fori_loop(0, loops, body, 0)

    for i in range(steps + 1):
        pl.when(step == i)(
            functools.partial(run, slots[i % 2] if i < steps else None, slots[(i + 1) % 2] if i > 0 else None)
        )


def spectra(first, count, total, offsets, points, focus, velocity, rise_time, own, other, pieces, so_far):
    half, variations = own.shape
    steps = variations // LANES
    stations = pieces[0].shape[2] // 2
    fill = lambda i: jnp.minimum(i, steps - 1)
    drain = lambda i: jnp.maximum(i - 1, 0)
    row = pl.BlockSpec((1, LANES), lambda i: (0, fill(i)))
    args = [offsets, points, focus, velocity, rise_time, own, other, *pieces]
    specs = [
        SMEM,
        VMEM,
        pl.BlockSpec((2, LANES), lambda i: (0, fill(i))),
        row,
        pl.BlockSpec((1, LANES), lambda i: (0, drain(i))),
        pl.BlockSpec((half, LANES), lambda i: (0, fill(i))),
        pl.BlockSpec((half, LANES), lambda i: (0, fill(i))),
    ]
    for piece in pieces:
        at = first // count if piece.shape[0] == total else 0
        specs.append(pl.BlockSpec((count,) + piece.shape[1:], lambda i, at=at: (at, 0, 0)))
    aliases = {}
    if so_far is not None:
        aliases = {len(args): 0}
        args.append(so_far)
        specs.append(ANY)
    slot = pltpu.VMEM((2, count, 2 * half, LANES), jnp.bfloat16)
    return pl.pallas_call(
        functools.partial(spectra_kernel, first, count, len(pieces), steps),
        out_shape=jax.ShapeDtypeStruct((total, 2, stations, variations), jnp.float32),
        grid=(steps + 1,),
        in_specs=specs,
        out_specs=pl.BlockSpec((count, 2, stations, LANES), lambda i: (first // count, 0, 0, drain(i))),
        scratch_shapes=[
            pltpu.VMEM((count, 2 * half, 2 * stations), jnp.bfloat16),
            pltpu.VMEM((2, 2 * half, 128), jnp.float32),
            slot,
            slot,
        ],
        input_output_aliases=aliases,
        compiler_params=PARAMS,
        name="spectra",
    )(*args)


def swap(array, axis):
    return lax.ppermute(array, axis, [(0, 1), (1, 0)])


def gather(own, received, size):
    place = lax.axis_index("var")
    rows = own.shape[1]
    if size != 8:
        whole = [lax.all_gather(piece, "var", axis=1, tiled=True) for piece in (own, received)]
        return [jnp.concatenate(whole, axis=1)], jnp.zeros((1,), jnp.int32)
    block = jnp.concatenate([own, received], axis=1)
    along = lambda piece, s: lax.ppermute(piece, "var", [(i, (i + 2 * s) % 8) for i in range(8)])
    across = lambda piece: lax.ppermute(piece, "var", [(i, i ^ 1) for i in range(8)])
    pieces = [block] + [along(block, s) for s in (1, 3, 2)]
    pieces += [across(piece) for piece in pieces]
    source = [((place - 2 * s) % 8) ^ flip for flip in (0, 1) for s in (0, 1, 3, 2)]
    return pieces, jnp.stack(source).astype(jnp.int32) * rows


def shards(size, fault_points, hypocenter, velocity, rise_time, member_mask, slip_amount, moment_tensor, strain_green, station_ids):
    half = moment_tensor.shape[1]
    freqs = strain_green.shape[4]
    own_part, other_part = rotate(strain_green[:, :, 0], moment_tensor, station_ids)
    pieces, offsets = gather(own_part, swap(other_part, "sub"), size)
    own = amounts(member_mask, slip_amount)
    other = swap(own, "sub")
    focus = jnp.take(fault_points, hypocenter, axis=1)
    turned = jnp.concatenate([fault_points[:, half:], fault_points[:, :half]], axis=1)
    points = jnp.where(lax.axis_index("sub") == 0, fault_points, turned)
    rows = (velocity[None, :], rise_time[None, :])
    out = None
    for first in (0, freqs // 2):
        out = spectra(first, freqs // 2, freqs, offsets, points, focus, *rows, own, other, pieces, out)
    return out


def solution(mesh):
    placed = (
        P(None, "site"),
        P(("site", "var")),
        P(("site", "var")),
        P(("site", "var")),
        P(("site", "var"), "sub"),
        P(("site", "var"), "sub"),
        P(None, ("site", "sub")),
        P("site", None, "sub", "var", None, None),
        P("site"),
    )
    return jax.shard_map(
        functools.partial(shards, mesh.shape["var"]),
        mesh=mesh,
        in_specs=placed,
        out_specs=P(None, None, "sub", ("site", "var")),
        check_vma=False,
    )
```

time: 262 us -> 79.8 us (0.30)
  the two profiles are of different devices: /device:TPU:0 before, /device:TPU:24 now
where the time goes in v1:
time: 79.8 us; the launch traced here: 79.4 us
  Pallas kernels  35.6 us (45%)
  waiting for transfers between devices  21.2 us (27%)
  starting transfers between devices  9.8 us (12%)
  local copies, waits for them, and re-layouts  8.82 us (11%)
  other arithmetic  3.86 us (5%)
    pallas_call x2, Pallas kernels, spectra(): pl.pallas_call(functools.partial(spectra_kernel, first, count, len(pieces...  28.7 us
    ppermute x3, waiting for transfers between devices, gather(): lax.ppermute(piece, 'var', [(i, (i + 2 * s) % 8) for i in range(8)])  12.6 us
    ppermute x4, waiting for transfers between devices, gather(): lax.ppermute(piece, 'var', [(i, i ^ 1) for i in range(8)])  8.52 us
    gather x2, local copies, waits for them, and re-layouts, shards(): focus = jnp.take(fault_points, hypocenter, axis=1)  5.26 us
    ppermute x4, starting transfers between devices, gather(): lax.ppermute(piece, 'var', [(i, i ^ 1) for i in range(8)])  5.06 us
    ppermute x3, starting transfers between devices, gather(): lax.ppermute(piece, 'var', [(i, (i + 2 * s) % 8) for i in range(8)])  4.23 us
    pallas_call x1, Pallas kernels, amounts(): pl.pallas_call(amount_kernel, out_shape=jax.ShapeDtypeStruct((subfaults,...  3.85 us
    pallas_call x1, Pallas kernels, rotate(): pl.pallas_call(rotate_kernel, out_shape=(piece, piece), in_specs=[VMEM, S...  3.03 us
  transfers between devices with their start and end apart: 9, of which 3 were waited for; matrix products, arithmetic and copies ran while one was open for 15% of the time, Pallas kernels for 5%

profile of v1, /device:TPU:24, one launch (start us, length us, event | category | flops | bytes accessed | tf_op | source)
XLA Modules:
  0.0 79.4 jit_solution(5446236338713054906)
XLA Ops:
  0.0 3.0 %rotate.1 = (bf16[16,32,128]{2,1,0:T(8,128)(2,1)}, bf16[16,32,128]{2,1,0:T(8,128)(2,1)}) custom-call(bf16[2,6,32,16,128]{4,3,2,1,0:T(8,128)(2,1)} %bitcast.14, f32[6,256]{1,0:T(8,128)} %tensor_ref.1, s32[1,128]{1,0:T(1,128)} %bitcast.19), custom_call_target="tpu_custom_call" | custom-call | tf_op jit(solution)/shard_map/rotate/pallas_call | solution.py:57
  3.0 3.8 %amounts.1.own_ref = f32[256,1024]{1,0:T(8,128)} custom-call(s32[1024,256]{1,0:T(8,128)} %mask_ref.1, f32[1024,256]{1,0:T(8,128)} %slip_ref.1), custom_call_target="tpu_custom_call" | custom-call | tf_op jit(solution)/shard_map/amounts/pallas_call | solution.py:78
  6.9 0.5 collective-permute-start
  7.4 0.7 fusion
  8.1 0.7 fusion.1
  8.8 0.9 %constant_dynamic-update-slice_fusion.1 = bf16[16,64,128]{2,1,0:T(8,128)(2,1)S(1)} fusion(bf16[16,32,128]{2,1,0:T(8,128)(2,1)} %get-tuple-element.7), kind=kLoop, calls=%fused_computation.5 | loop fusion | bytes 262144
  10.3 3.6 %collective-permute-start.2 = (bf16[16,64,128]{2,1,0:T(8,128)(2,1)S(1)}, bf16[16,64,128]{2,1,0:T(8,128)(2,1)S(1)}, u32[]{:S(2)}, u32[]{:S(2)}) collective-permute-start(bf16[16,64,128]{2,1,0:T(8,128)(2,1)S(1)} %constant_dynamic-update-slice_fusion.refs_0_), channel_id=1, source_target_pairs={{0,4},{2,6},{4,8},{6,10},{8,12},{10,14},{12,0},{14,2},{1,5},{3,7},... | collective-permute-start | bytes 786440 | tf_op jit(solution)/shard_map/ppermute | solution.py:237
  14.0 0.7 compare_and_fusion
  14.7 1.3 %maximum_select_fusion.points_ref = f32[2,512]{1,0:T(2,128)} fusion(f32[2,512]{1,0:T(2,128)} %param.9, f32[2,256]{1,0:T(2,128)S(1)} %get-tuple-element.10, f32[2,256]{1,0:T(2,128)S(1)} %get-tuple-element.9, pred[]{:T(512)S(6)} %eq.12), kind=kLoop, calls=%fused_computation.3 | loop fusion | flops 2048 | bytes 12289 | tf_op jit(solution)/shard_map/jit(_where)/select_n | solution.py:254
  16.0 1.5 %collective-permute-start.5 = (bf16[16,64,128]{2,1,0:T(8,128)(2,1)S(1)}, bf16[16,64,128]{2,1,0:T(8,128)(2,1)S(1)}, u32[]{:S(2)}, u32[]{:S(2)}) collective-permute-start(bf16[16,64,128]{2,1,0:T(8,128)(2,1)S(1)} %constant_dynamic-update-slice_fusion.refs_0_), channel_id=1, source_target_pairs={{0,2},{2,0},{4,6},{6,4},{8,10},{10,8},{12,14},{14,12},{1,3},{3,1},... | collective-permute-start | bytes 786440 | tf_op jit(solution)/shard_map/ppermute | solution.py:238
  17.6 12.6 %collective-permute-done.4.refs_3_ = bf16[16,64,128]{2,1,0:T(8,128)(2,1)S(1)} collective-permute-done((bf16[16,64,128]{2,1,0:T(8,128)(2,1)S(1)}, bf16[16,64,128]{2,1,0:T(8,128)(2,1)S(1)}, u32[]{:S(2)}, u32[]{:S(2)}) %collective-permute-start.4) | collective-permute-done | bytes 262176 | tf_op jit(solution)/shard_map/ppermute | solution.py:237
  30.2 1.5 %collective-permute-start.8 = (bf16[16,64,128]{2,1,0:T(8,128)(2,1)S(1)}, bf16[16,64,128]{2,1,0:T(8,128)(2,1)S(1)}, u32[]{:S(2)}, u32[]{:S(2)}) collective-permute-start(bf16[16,64,128]{2,1,0:T(8,128)(2,1)S(1)} %collective-permute-done.4.refs_3_), channel_id=1, source_target_pairs={{0,2},{2,0},{4,6},{6,4},{8,10},{10,8},{12,14},{14,12},{1,3},{3,1},... | collective-permute-start | bytes 786440 | tf_op jit(solution)/shard_map/ppermute | solution.py:238
  31.7 0.5 collective-permute-start.7
  32.2 1.5 %collective-permute-start.6 = (bf16[16,64,128]{2,1,0:T(8,128)(2,1)S(1)}, bf16[16,64,128]{2,1,0:T(8,128)(2,1)S(1)}, u32[]{:S(2)}, u32[]{:S(2)}) collective-permute-start(bf16[16,64,128]{2,1,0:T(8,128)(2,1)S(1)} %collective-permute-done.2.refs_1_), channel_id=1, source_target_pairs={{0,2},{2,0},{4,6},{6,4},{8,10},{10,8},{12,14},{14,12},{1,3},{3,1},... | collective-permute-start | bytes 786440 | tf_op jit(solution)/shard_map/ppermute | solution.py:238
  33.7 0.6 broadcast_multiply_fusion.off_ref
  34.3 0.8 %copy.11 = f32[2,512]{0,1:T(8,128)S(1)} copy(f32[2,512]{1,0:T(2,128)} %param.9) | data formatting | bytes 8192 | tf_op args[0]
  35.1 4.0 %gather_fusion = f32[1024,2]{1,0:T(8,128)} fusion(f32[2,512]{0,1:T(8,128)S(1)} %copy.11, s32[1024]{0:T(1024)S(1)} %fusion), kind=kCustom, calls=%fused_computation | custom fusion | bytes 20480 | tf_op jit(solution)/shard_map/jit(_take)/gather | solution.py:252
  39.2 1.2 %copy.12 = f32[1024,2]{0,1:T(2,128)S(1)} copy(f32[1024,2]{1,0:T(8,128)} %gather_fusion) | data formatting | bytes 16384 | tf_op jit(solution)/shard_map/jit(_take)/gather | solution.py:252
  40.4 0.6 select_bitcast_fusion.focus_ref
  41.0 3.9 %collective-permute-done.7.refs_6_ = bf16[16,64,128]{2,1,0:T(8,128)(2,1)S(1)} collective-permute-done((bf16[16,64,128]{2,1,0:T(8,128)(2,1)S(1)}, bf16[16,64,128]{2,1,0:T(8,128)(2,1)S(1)}, u32[]{:S(2)}, u32[]{:S(2)}) %collective-permute-start.7) | collective-permute-done | bytes 262176 | tf_op jit(solution)/shard_map/ppermute | solution.py:238
  45.0 4.6 %collective-permute-done.6.refs_5_ = bf16[16,64,128]{2,1,0:T(8,128)(2,1)S(1)} collective-permute-done((bf16[16,64,128]{2,1,0:T(8,128)(2,1)S(1)}, bf16[16,64,128]{2,1,0:T(8,128)(2,1)S(1)}, u32[]{:S(2)}, u32[]{:S(2)}) %collective-permute-start.6) | collective-permute-done | bytes 262176 | tf_op jit(solution)/shard_map/ppermute | solution.py:238
  49.6 0.6 copy-done.8
  50.6 13.8 %spectra.2.refs_8_ = f32[16,2,64,1024]{3,2,1,0:T(8,128)} custom-call(s32[8]{0:T(128)} %broadcast_multiply_fusion.off_ref, f32[2,512]{1,0:T(2,128)} %maximum_select_fusion.points_ref, f32[2,1024]{1,0:T(2,128)} %select_bitcast_fusion.focus_ref, f32[1,1024]{1,0:T(1,128)} %bitcast.15, f32[1,1024]{1,0:T(1,128)} %bitcast.17, f32[256,1024]{1,0:T(8,128)} %amounts.1.own_ref, ...), custom_call_target="tpu_custom_call" | custom-call | tf_op jit(solution)/shard_map/spectra/pallas_call | solution.py:208
  64.4 14.9 %spectra.3 = f32[16,2,64,1024]{3,2,1,0:T(8,128)} custom-call(s32[8]{0:T(128)} %broadcast_multiply_fusion.off_ref, f32[2,512]{1,0:T(2,128)} %maximum_select_fusion.points_ref, f32[2,1024]{1,0:T(2,128)} %select_bitcast_fusion.focus_ref, f32[1,1024]{1,0:T(1,128)} %bitcast.16, f32[1,1024]{1,0:T(1,128)} %bitcast.18, ...), custom_call_target="tpu_custom_call", output_to_operand_aliasing={{}: (15, {})} | custom-call | tf_op jit(solution)/shard_map/spectra/pallas_call | solution.py:208
  (28 shorter events, 1.1 us)
Async XLA Ops:
  3.0 6.7 %collective-permute-start.1 = (bf16[16,32,128]{2,1,0:T(8,128)(2,1)}, bf16[16,32,128]{2,1,0:T(8,128)(2,1)S(1)}, u32[]{:S(2)}, u32[]{:S(2)}) collective-permute-start(bf16[16,32,128]{2,1,0:T(8,128)(2,1)} %get-tuple-element.8), channel_id=1, source_target_pairs={{0,1},{1,0},{2,3},{3,2},{4,5},{5,4},{6,7},{7,6},{8,9},{9,8},{10,11... | collective-permute-start | bytes 393224 | tf_op jit(solution)/shard_map/ppermute | solution.py:227
  6.9 42.7 %collective-permute-start = (f32[256,1024]{1,0:T(8,128)}, f32[256,1024]{1,0:T(8,128)S(1)}, u32[]{:S(2)}, u32[]{:S(2)}) collective-permute-start(f32[256,1024]{1,0:T(8,128)} %amounts.1.own_ref), channel_id=1, source_target_pairs={{0,1},{1,0},{2,3},{3,2},{4,5},{5,4},{6,7},{7,6},{8,9},{9,8},{10,11... | collective-permute-start | bytes 3145736 | tf_op jit(solution)/shard_map/ppermute | solution.py:227
  9.7 39.8 %copy-start.1 = (bf16[16,64,128]{2,1,0:T(8,128)(2,1)}, bf16[16,64,128]{2,1,0:T(8,128)(2,1)S(1)}, u32[]{:S(2)}) copy-start(bf16[16,64,128]{2,1,0:T(8,128)(2,1)S(1)} %constant_dynamic-update-slice_fusion.refs_0_) | copy-start | bytes 786436
  9.7 20.4 %collective-permute-start.4 = (bf16[16,64,128]{2,1,0:T(8,128)(2,1)S(1)}, bf16[16,64,128]{2,1,0:T(8,128)(2,1)S(1)}, u32[]{:S(2)}, u32[]{:S(2)}) collective-permute-start(bf16[16,64,128]{2,1,0:T(8,128)(2,1)S(1)} %constant_dynamic-update-slice_fusion.refs_0_), channel_id=1, source_target_pairs={{0,8},{2,10},{4,12},{6,14},{8,0},{10,2},{12,4},{14,6},{1,9},{3,11}... | collective-permute-start | bytes 786440 | tf_op jit(solution)/shard_map/ppermute | solution.py:237
  10.1 21.6 %collective-permute-start.3 = (bf16[16,64,128]{2,1,0:T(8,128)(2,1)S(1)}, bf16[16,64,128]{2,1,0:T(8,128)(2,1)S(1)}, u32[]{:S(2)}, u32[]{:S(2)}) collective-permute-start(bf16[16,64,128]{2,1,0:T(8,128)(2,1)S(1)} %constant_dynamic-update-slice_fusion.refs_0_), channel_id=1, source_target_pairs={{0,12},{2,14},{4,0},{6,2},{8,4},{10,6},{12,8},{14,10},{1,13},{3,15... | collective-permute-start | bytes 786440 | tf_op jit(solution)/shard_map/ppermute | solution.py:237
  10.3 21.9 %collective-permute-start.2 = (bf16[16,64,128]{2,1,0:T(8,128)(2,1)S(1)}, bf16[16,64,128]{2,1,0:T(8,128)(2,1)S(1)}, u32[]{:S(2)}, u32[]{:S(2)}) collective-permute-start(bf16[16,64,128]{2,1,0:T(8,128)(2,1)S(1)} %constant_dynamic-update-slice_fusion.refs_0_), channel_id=1, source_target_pairs={{0,4},{2,6},{4,8},{6,10},{8,12},{10,14},{12,0},{14,2},{1,5},{3,7},... | collective-permute-start | bytes 786440 | tf_op jit(solution)/shard_map/ppermute | solution.py:237
  16.0 25.0 %collective-permute-start.5 = (bf16[16,64,128]{2,1,0:T(8,128)(2,1)S(1)}, bf16[16,64,128]{2,1,0:T(8,128)(2,1)S(1)}, u32[]{:S(2)}, u32[]{:S(2)}) collective-permute-start(bf16[16,64,128]{2,1,0:T(8,128)(2,1)S(1)} %constant_dynamic-update-slice_fusion.refs_0_), channel_id=1, source_target_pairs={{0,2},{2,0},{4,6},{6,4},{8,10},{10,8},{12,14},{14,12},{1,3},{3,1},... | collective-permute-start | bytes 786440 | tf_op jit(solution)/shard_map/ppermute | solution.py:238
  30.2 19.4 %copy-start.2 = (bf16[16,64,128]{2,1,0:T(8,128)(2,1)}, bf16[16,64,128]{2,1,0:T(8,128)(2,1)S(1)}, u32[]{:S(2)}) copy-start(bf16[16,64,128]{2,1,0:T(8,128)(2,1)S(1)} %collective-permute-done.4.refs_3_) | copy-start | bytes 786436
  30.2 10.8 %collective-permute-start.8 = (bf16[16,64,128]{2,1,0:T(8,128)(2,1)S(1)}, bf16[16,64,128]{2,1,0:T(8,128)(2,1)S(1)}, u32[]{:S(2)}, u32[]{:S(2)}) collective-permute-start(bf16[16,64,128]{2,1,0:T(8,128)(2,1)S(1)} %collective-permute-done.4.refs_3_), channel_id=1, source_target_pairs={{0,2},{2,0},{4,6},{6,4},{8,10},{10,8},{12,14},{14,12},{1,3},{3,1},... | collective-permute-start | bytes 786440 | tf_op jit(solution)/shard_map/ppermute | solution.py:238
  31.7 17.9 %copy-start.3 = (bf16[16,64,128]{2,1,0:T(8,128)(2,1)}, bf16[16,64,128]{2,1,0:T(8,128)(2,1)S(1)}, u32[]{:S(2)}) copy-start(bf16[16,64,128]{2,1,0:T(8,128)(2,1)S(1)} %collective-permute-done.3.refs_2_) | copy-start | bytes 786436
  31.7 13.3 %collective-permute-start.7 = (bf16[16,64,128]{2,1,0:T(8,128)(2,1)S(1)}, bf16[16,64,128]{2,1,0:T(8,128)(2,1)S(1)}, u32[]{:S(2)}, u32[]{:S(2)}) collective-permute-start(bf16[16,64,128]{2,1,0:T(8,128)(2,1)S(1)} %collective-permute-done.3.refs_2_), channel_id=1, source_target_pairs={{0,2},{2,0},{4,6},{6,4},{8,10},{10,8},{12,14},{14,12},{1,3},{3,1},... | collective-permute-start | bytes 786440 | tf_op jit(solution)/shard_map/ppermute | solution.py:238
  32.2 17.4 %copy-start.4 = (bf16[16,64,128]{2,1,0:T(8,128)(2,1)}, bf16[16,64,128]{2,1,0:T(8,128)(2,1)S(1)}, u32[]{:S(2)}) copy-start(bf16[16,64,128]{2,1,0:T(8,128)(2,1)S(1)} %collective-permute-done.2.refs_1_) | copy-start | bytes 786436
  32.2 17.3 %collective-permute-start.6 = (bf16[16,64,128]{2,1,0:T(8,128)(2,1)S(1)}, bf16[16,64,128]{2,1,0:T(8,128)(2,1)S(1)}, u32[]{:S(2)}, u32[]{:S(2)}) collective-permute-start(bf16[16,64,128]{2,1,0:T(8,128)(2,1)S(1)} %collective-permute-done.2.refs_1_), channel_id=1, source_target_pairs={{0,2},{2,0},{4,6},{6,4},{8,10},{10,8},{12,14},{14,12},{1,3},{3,1},... | collective-permute-start | bytes 786440 | tf_op jit(solution)/shard_map/ppermute | solution.py:238
  41.0 8.6 %copy-start.5 = (bf16[16,64,128]{2,1,0:T(8,128)(2,1)}, bf16[16,64,128]{2,1,0:T(8,128)(2,1)S(1)}, u32[]{:S(2)}) copy-start(bf16[16,64,128]{2,1,0:T(8,128)(2,1)S(1)} %collective-permute-done.5.refs_4_) | copy-start | bytes 786436
  41.0 8.6 %copy-start.6 = (bf16[16,64,128]{2,1,0:T(8,128)(2,1)}, bf16[16,64,128]{2,1,0:T(8,128)(2,1)S(1)}, u32[]{:S(2)}) copy-start(bf16[16,64,128]{2,1,0:T(8,128)(2,1)S(1)} %collective-permute-done.8.refs_7_) | copy-start | bytes 786436
  45.0 4.6 %copy-start.7 = (bf16[16,64,128]{2,1,0:T(8,128)(2,1)}, bf16[16,64,128]{2,1,0:T(8,128)(2,1)S(1)}, u32[]{:S(2)}) copy-start(bf16[16,64,128]{2,1,0:T(8,128)(2,1)S(1)} %collective-permute-done.7.refs_6_) | copy-start | bytes 786436
  49.6 0.7 copy-start.8
  49.6 1.1 %copy-start = (f32[256,1024]{1,0:T(8,128)}, f32[256,1024]{1,0:T(8,128)S(1)}, u32[]{:S(2)}) copy-start(f32[256,1024]{1,0:T(8,128)S(1)} %collective-permute-done.other_ref) | copy-start | bytes 3145732

commit v2 on v1

v2 whole, which is shorter than its diff:
```python
import functools

import jax
import jax.numpy as jnp
from jax import lax
from jax.experimental import pallas as pl
from jax.experimental.pallas import tpu as pltpu
from jax.sharding import PartitionSpec as P

VMEM = pl.BlockSpec(memory_space=pltpu.VMEM)
SMEM = pl.BlockSpec(memory_space=pltpu.SMEM)
ANY = pl.BlockSpec(memory_space=pl.ANY)
PARAMS = pltpu.CompilerParams(vmem_limit_bytes=12 * 2**20)
BASE_FREQ = 0.0625
LANES = 256


def rotate_kernel(green_ref, tensor_ref, ids_ref, own_ref, other_ref, sums, rows):
    _, comps, count, freqs, stations = green_ref.shape
    half = stations // 2
    first = lax.axis_index("var") * count

    def one_subfault(m, carry):
        for part in range(2):
            total = green_ref[part, 0, m].astype(jnp.float32) * tensor_ref[0, first + m]
            for comp in range(1, comps):
                total = total + green_ref[part, comp, m].astype(jnp.float32) * tensor_ref[comp, first + m]
            at = pl.ds(pl.multiple_of(m * freqs, freqs), freqs)
            sums[at, part * stations : (part + 1) * stations] = total.astype(jnp.bfloat16)
        return carry

    lax.fori_loop(0, count, one_subfault, 0, unroll=4)

    lane = lax.broadcasted_iota(jnp.int32, (1, stations), 1)
    ids = ids_ref[...]
    turned = pltpu.roll(ids, half, 1)
    low = jnp.where(lane < half, ids, turned)
    high = jnp.where(lane < half, turned, ids)
    is_first = lax.axis_index("sub") == 0
    wanted = jnp.concatenate([jnp.where(is_first, low, high), jnp.where(is_first, high, low)], axis=1)
    row = lax.broadcasted_iota(jnp.int32, (2 * stations, 2 * stations), 0)
    column = lax.broadcasted_iota(jnp.int32, (2 * stations, 2 * stations), 1)
    part_of_column = (column // half) % 2
    picks = (row == wanted + part_of_column * stations).astype(jnp.float32).astype(jnp.bfloat16)
    picked = jnp.dot(sums[...], picks, preferred_element_type=jnp.float32)
    rows[0] = picked[:, :stations]
    rows[1] = picked[:, stations:]
    for k in range(freqs):
        at = pl.ds(k, count, stride=freqs)
        own_ref[k] = rows[0, at, :].astype(jnp.bfloat16)
        other_ref[k] = rows[1, at, :].astype(jnp.bfloat16)


def rotate(green, tensor, station_ids):
    _, _, count, freqs, stations = green.shape
    piece = jax.ShapeDtypeStruct((freqs, count, stations), jnp.bfloat16)
    return pl.pallas_call(
        rotate_kernel,
        out_shape=(piece, piece),
        in_specs=[VMEM, SMEM, VMEM],
        out_specs=(VMEM, VMEM),
        scratch_shapes=[
            pltpu.VMEM((count * freqs, 2 * stations), jnp.bfloat16),
            pltpu.VMEM((2, count * freqs, stations), jnp.float32),
        ],
        compiler_params=PARAMS,
        name="rotate",
    )(green, tensor, station_ids.reshape((1, stations)))


def amount_kernel(mask_ref, slip_ref, out_ref):
    out_ref[...] = (mask_ref[...].astype(jnp.float32) * slip_ref[...]).T


def amounts(mask, slip):
    variations, subfaults = mask.shape
    block = pl.BlockSpec((LANES, subfaults), lambda i: (i, 0))
    return pl.pallas_call(
        amount_kernel,
        out_shape=jax.ShapeDtypeStruct((subfaults, variations), jnp.float32),
        grid=(variations // LANES,),
        in_specs=[block, block],
        out_specs=pl.BlockSpec((subfaults, LANES), lambda i: (0, i)),
        compiler_params=PARAMS,
        name="amounts",
    )(mask, slip)


SIN = (3.14159264, -5.16771008, 2.55007751, -0.598291190, 0.0776574420)
COS = (0.999999953, -4.93479283, 4.05841131, -1.33187624, 0.219688854)


def sine_cosine(turns):
    rest = turns - jnp.floor(turns + 0.5)
    square = rest * rest
    sine = SIN[-1]
    for c in SIN[-2::-1]:
        sine = sine * square + c
    sine = sine * rest
    cosine = COS[-1]
    for c in COS[-2::-1]:
        cosine = cosine * square + c
    return 2.0 * sine * cosine, 1.0 - 2.0 * sine * sine


def slips_kernel(chunk, rows, sub, points_ref, hypocenter_ref, velocity_ref, own_ref, other_ref, *refs):
    outs, columns, spots = refs[:-2], refs[-2], refs[-1]
    half, variations = own_ref.shape
    subfaults = 2 * half
    first = pl.multiple_of(lax.axis_index(sub) * half, half)
    second = pl.multiple_of(half - first, half)
    for axis in range(2):
        for at, start in ((0, first), (half, second)):
            wide = jnp.broadcast_to(points_ref[axis : axis + 1, pl.ds(start, half)], (128, half))
            columns[axis, at : at + half, :] = wide.T

    rest = points_ref[...]
    thirds = []
    for _ in range(3):
        thirds.append(rest.astype(jnp.bfloat16))
        rest = rest - thirds[-1].astype(jnp.float32)
    thirds = jnp.concatenate([t.astype(jnp.float32) for t in thirds], axis=0).astype(jnp.bfloat16)
    for lane in range(0, variations, LANES):
        lanes = slice(lane, lane + LANES)
        index = lax.broadcasted_iota(jnp.int32, (subfaults, LANES), 0)
        here = (index == hypocenter_ref[0:1, lanes]).astype(jnp.float32).astype(jnp.bfloat16)
        spot = jnp.dot(thirds, here, preferred_element_type=jnp.float32)
        spots[0:2, lanes] = (spot[0:2] + spot[2:4]) + spot[4:6]
        spots[2:3, lanes] = BASE_FREQ / velocity_ref[0:1, lanes]

    def fill(row, source, source_row, place, lanes):
        at = pl.ds(row, chunk)
        east = columns[0, at, :] - spots[0:1, lanes]
        north = columns[1, at, :] - spots[1:2, lanes]
        gap = east * east + north * north
        distance = gap * lax.rsqrt(jnp.maximum(gap, 1e-30))
        sine, cosine = sine_cosine(distance * spots[2:3, lanes])
        amount = source[pl.ds(source_row, chunk), lanes]
        twice = 2.0 * cosine
        re_last, im_last = amount, None
        re, im = amount * cosine, amount * sine
        for out in outs:
            for k in range(out.shape[0]):
                out[k, pl.ds(place, chunk), lanes] = re.astype(jnp.bfloat16)
                out[k, pl.ds(place + 2 * rows, chunk), lanes] = im.astype(jnp.bfloat16)
                re, re_last = twice * re - re_last, re
                im, im_last = (twice * im if im_last is None else twice * im - im_last), im

    def body(j, carry):
        row = pl.multiple_of(j * chunk, chunk)
        place = pl.multiple_of((row // rows) * (4 * rows) + row % rows, chunk)
        for lane in range(0, variations, 128):
            lanes = slice(lane, lane + 128)
            fill(row, own_ref, row, place, lanes)
            fill(half + row, other_ref, row, pl.multiple_of(place + rows, chunk), lanes)
        return carry

    lax.fori_loop(0, half // chunk, body, 0)


def slips(groups, rows, points, hypocenter, velocity, own, other):
    half, variations = own.shape
    return pl.pallas_call(
        functools.partial(slips_kernel, 32, rows, "sub"),
        out_shape=tuple(jax.ShapeDtypeStruct((n, 4 * half, variations), jnp.bfloat16) for n in groups),
        in_specs=[VMEM] * 5,
        out_specs=(VMEM,) * len(groups),
        scratch_shapes=[pltpu.VMEM((2, 2 * half, 128), jnp.float32), pltpu.VMEM((8, variations), jnp.float32)],
        compiler_params=PARAMS,
        name="slips",
    )(points, hypocenter[None, :], velocity[None, :], own, other)


def unit_rows(k, pair, flip, table):
    lane = lax.broadcasted_iota(jnp.int32, (1, pair[0].shape[2]), 1)
    half = pair[0].shape[2] // 2
    rows = pair[0].shape[1]
    for i, ref in enumerate(pair):
        at = pl.multiple_of((i ^ flip) * (2 * rows), 2 * rows) if len(pair) == 2 else 0
        block = ref[k]
        turned = pltpu.roll(block.astype(jnp.float32), half, 1)
        table[pl.ds(at, rows), :] = block
        table[pl.ds(at + rows, rows), :] = jnp.where(lane < half, turned, -turned).astype(jnp.bfloat16)


def unit_sum(k, slip_k, unit, pair, slips_ref, flip, table):
    unit_rows(k, pair, flip, table)
    depth = table.shape[0]
    at = pl.multiple_of(unit * depth, depth)
    return lax.dot_general(
        table[...], slips_ref[slip_k, pl.ds(at, depth), :], (((0,), (0,)), ((), ())), preferred_element_type=jnp.float32
    )


def partial_kernel(units, width, numbers_ref, *refs):
    pairs = [refs[i * width : (i + 1) * width] for i in range(units)]
    rest = refs[units * width :]
    groups = (len(rest) - 1) // 2
    slip_refs, out_refs, tables = rest[:groups], rest[groups : 2 * groups], rest[-1]
    flip = numbers_ref[0]
    first = 0
    for slips_ref, out_ref in zip(slip_refs, out_refs):

        def body(k, carry, slips_ref=slips_ref, out_ref=out_ref, first=first):
            total = 0.0
            for u in range(units):
                total += unit_sum(first + k, k, numbers_ref[1 + u], pairs[u], slips_ref, flip, tables.at[u])
            out_ref[k] = total
            return carry

        lax.fori_loop(0, slips_ref.shape[0], body, 0)
        first += slips_ref.shape[0]


def partial_sums(numbers, pairs, slip_groups):
    width = len(pairs[0])
    rows = pairs[0][0].shape[1]
    lanes = pairs[0][0].shape[2]
    variations = slip_groups[0].shape[2]
    flat = [piece for pair in pairs for piece in pair]
    return pl.pallas_call(
        functools.partial(partial_kernel, len(pairs), width),
        out_shape=tuple(jax.ShapeDtypeStruct((g.shape[0], lanes, variations), jnp.float32) for g in slip_groups),
        in_specs=[SMEM] + [VMEM] * (len(flat) + len(slip_groups)),
        out_specs=(VMEM,) * len(slip_groups),
        scratch_shapes=[pltpu.VMEM((len(pairs), 2 * rows * width, lanes), jnp.bfloat16)],
        compiler_params=PARAMS,
        name="partial_sums",
    )(numbers, *flat, *slip_groups)


BUFFERS = 4


def finish_kernel(first, width, has_sums, has_out, numbers_ref, rise_ref, *refs):
    pair = refs[:width]
    refs = refs[width:]
    slips_ref = refs[0]
    sums_ref = refs[1] if has_sums else None
    out_ref, table, buffers, sems = refs[-4:]
    count = slips_ref.shape[0]

    def copy(k):
        slot = k % BUFFERS
        return pltpu.make_async_copy(buffers.at[slot], out_ref.at[first + k], sems.at[slot])

    def body(k, carry):
        total = unit_sum(k, k, numbers_ref[1], pair, slips_ref, numbers_ref[0], table)
        if has_sums:
            total += sums_ref[k]
        stations = total.shape[0] // 2
        re, im = total[:stations], total[stations:]
        pulsation = (first + k + 1).astype(jnp.float32) * (2.0 * jnp.pi * BASE_FREQ)
        damping = pulsation * rise_ref[...]
        scale = 1.0 / (1.0 + damping * damping)
        tilt = scale * damping

        @pl.when(k >= BUFFERS)
        def _():
            copy(k - BUFFERS).wait()

        buffers[k % BUFFERS, 0] = scale * re + tilt * im
        buffers[k % BUFFERS, 1] = scale * im - tilt * re
        copy(k).start()
        return carry

    lax.fori_loop(0, count, body, 0)
    for k in range(max(0, count - BUFFERS), count):
        copy(k).wait()


def finish(first, total, numbers, rise_time, pair, slip_group, sums, so_far):
    rows, lanes = pair[0].shape[1:]
    stations = lanes // 2
    variations = slip_group.shape[2]
    args = [numbers, rise_time[None, :], *pair, slip_group]
    specs = [SMEM] + [VMEM] * (len(args) - 1)
    if sums is not None:
        args.append(sums)
        specs.append(VMEM)
    aliases = {}
    if so_far is not None:
        aliases = {len(args): 0}
        args.append(so_far)
        specs.append(ANY)
    return pl.pallas_call(
        functools.partial(finish_kernel, first, len(pair), sums is not None, so_far is not None),
        out_shape=jax.ShapeDtypeStruct((total, 2, stations, variations), jnp.float32),
        in_specs=specs,
        out_specs=ANY,
        scratch_shapes=[
            pltpu.VMEM((2 * rows * len(pair), lanes), jnp.bfloat16),
            pltpu.VMEM((BUFFERS, 2, stations, variations), jnp.float32),
            pltpu.SemaphoreType.DMA((BUFFERS,)),
        ],
        input_output_aliases=aliases,
        compiler_params=PARAMS,
        name="finish",
    )(*args)


def swap(array, axis):
    return lax.ppermute(array, axis, [(0, 1), (1, 0)])


def shards(size, fault_points, hypocenter, velocity, rise_time, member_mask, slip_amount, moment_tensor, strain_green, station_ids):
    freqs = strain_green.shape[4]
    half = moment_tensor.shape[1]
    own_part, other_part = rotate(strain_green[:, :, 0], moment_tensor, station_ids)
    received = swap(other_part, "sub")
    if size == 8:
        rows = own_part.shape[1]
        block = jnp.concatenate([own_part, received], axis=1)
        member_mask, slip_amount, block = lax.optimization_barrier((member_mask, slip_amount, block))
    else:
        rows = half
        whole = [lax.all_gather(piece, "var", axis=1, tiled=True) for piece in (own_part, received)]
        block = jnp.concatenate(whole, axis=1)
    own = amounts(member_mask, slip_amount)
    groups = (freqs // 2, freqs - freqs // 2)
    slip_groups = slips(groups, rows, fault_points, hypocenter, velocity, own, swap(own, "sub"))
    place = lax.axis_index("var")
    out = None
    first = 0
    if size != 8:
        numbers = jnp.zeros((2,), jnp.int32)
        for group in slip_groups:
            out = finish(first, freqs, numbers, rise_time, [block[first : first + group.shape[0]]], group, None, out)
            first += group.shape[0]
        return out
    along = lambda piece, s: lax.ppermute(piece, "var", [(i, (i + 2 * s) % 8) for i in range(8)])
    across = lambda piece: lax.ppermute(piece, "var", [(i, i ^ 1) for i in range(8)])
    parts = [along(block, 1), along(block, 3)]
    last = []
    for group in groups:
        last.append(along(block[first : first + group], 2))
        first += group
    flip = place % 2
    unit = lambda s: ((place - 2 * s) % 8) // 2
    numbers = jnp.stack([flip, unit(0), unit(1), unit(3)]).astype(jnp.int32)
    pairs = [(piece, across(piece)) for piece in [block] + parts]
    sums = partial_sums(numbers, pairs, slip_groups)
    numbers = jnp.stack([flip, unit(2)]).astype(jnp.int32)
    first = 0
    for piece, group, total in zip(last, slip_groups, sums):
        out = finish(first, freqs, numbers, rise_time, (piece, across(piece)), group, total, out)
        first += group.shape[0]
    return out


def solution(mesh):
    placed = (
        P(None, "site"),
        P(("site", "var")),
        P(("site", "var")),
        P(("site", "var")),
        P(("site", "var"), "sub"),
        P(("site", "var"), "sub"),
        P(None, ("site", "sub")),
        P("site", None, "sub", "var", None, None),
        P("site"),
    )
    return jax.shard_map(
        functools.partial(shards, mesh.shape["var"]),
        mesh=mesh,
        in_specs=placed,
        out_specs=P(None, None, "sub", ("site", "var")),
        check_vma=False,
    )
```

time: 79.8 us -> 101 us (1.27)
  the two profiles are of different devices: /device:TPU:24 before, /device:TPU:0 now
where the time goes in v2:
time: 101 us; the launch traced here: 100 us
  Pallas kernels  34.3 us (34%)
  local copies, waits for them, and re-layouts  33.2 us (33%)
  waiting for transfers between devices  18.5 us (18%)
  starting transfers between devices  14.2 us (14%)
    unnamed x28, local copies, waits for them, and re-layouts  32.5 us
    ppermute x4, waiting for transfers between devices, shards(): lax.ppermute(piece, 'var', [(i, (i + 2 * s) % 8) for i in range(8)])  17.5 us
    pallas_call x1, Pallas kernels, slips(): pl.pallas_call(functools.partial(slips_kernel, 32, rows, 'sub'), out_shap...  13 us
    pallas_call x2, Pallas kernels, finish(): pl.pallas_call(functools.partial(finish_kernel, first, len(pair), sums is...  10.1 us
    pallas_call x1, Pallas kernels, partial_sums(): pl.pallas_call(functools.partial(partial_kernel, len(pairs), width), out_...  8.91 us
    ppermute x4, starting transfers between devices, shards(): lax.ppermute(piece, 'var', [(i, (i + 2 * s) % 8) for i in range(8)])  7.69 us
    ppermute x5, starting transfers between devices, shards(): lax.ppermute(piece, 'var', [(i, i ^ 1) for i in range(8)])  5.57 us
  transfers between devices with their start and end apart: 11, of which 2 were waited for; matrix products, arithmetic and copies ran while one was open for 1% of the time, Pallas kernels for 27%

profile of v2, /device:TPU:0, one launch (start us, length us, event | category | flops | bytes accessed | tf_op | source)
XLA Modules:
  0.0 100.4 jit_solution(15355309233036538812)
XLA Ops:
  0.0 1.4 %copy-done.5 = bf16[2,6,1,32,16,128]{5,4,3,2,1,0:T(8,128)(2,1)S(1)} copy-done((bf16[2,6,1,32,16,128]{5,4,3,2,1,0:T(8,128)(2,1)S(1)}, bf16[2,6,1,32,16,128]{5,4,3,2,1,0:T(8,128)(2,1)}, u32[]{:S(2)}) %copy-start.5) | copy-done | bytes 1572888
  1.4 0.7 copy-done.9
  2.8 1.6 %rotate.1 = (bf16[16,32,128]{2,1,0:T(8,128)(2,1)S(1)}, bf16[16,32,128]{2,1,0:T(8,128)(2,1)S(1)}) custom-call(bf16[2,6,32,16,128]{4,3,2,1,0:T(8,128)(2,1)S(1)} %bitcast.10, f32[6,256]{1,0:T(8,128)S(1)} %copy-done.9, s32[1,128]{1,0:T(1,128)S(1)} %bitcast.15), custom_call_target="tpu_custom_call" | custom-call | tf_op jit(solution)/shard_map/rotate/pallas_call | solution.py:57
  4.9 1.0 collective-permute-done
  5.9 1.2 %copy-done.6 = s32[1024,256]{1,0:T(8,128)S(1)} copy-done((s32[1024,256]{1,0:T(8,128)S(1)}, s32[1024,256]{1,0:T(8,128)}, u32[]{:S(2)}) %copy-start.6) | copy-done | bytes 1048600
  7.1 1.2 %copy-done.7 = f32[1024,256]{1,0:T(8,128)S(1)} copy-done((f32[1024,256]{1,0:T(8,128)S(1)}, f32[1024,256]{1,0:T(8,128)}, u32[]{:S(2)}) %copy-start.7) | copy-done | bytes 1048600
  8.3 0.7 amounts.1.own_ref
  9.5 2.7 %collective-permute-start.5 = (bf16[16,64,128]{2,1,0:T(8,128)(2,1)S(1)}, bf16[16,64,128]{2,1,0:T(8,128)(2,1)S(1)}, u32[]{:S(2)}, u32[]{:S(2)}) collective-permute-start(bf16[16,64,128]{2,1,0:T(8,128)(2,1)S(1)} %pad_maximum_fusion.refs_0_), channel_id=1, source_target_pairs={{0,4},{2,6},{4,8},{6,10},{8,12},{10,14},{12,0},{14,2},{1,5},{3,7},... | collective-permute-start | bytes 786440 | tf_op jit(solution)/shard_map/ppermute | solution.py:331
  12.2 2.0 %collective-permute-start.7 = (bf16[16,64,128]{2,1,0:T(8,128)(2,1)S(1)}, bf16[16,64,128]{2,1,0:T(8,128)(2,1)S(1)}, u32[]{:S(2)}, u32[]{:S(2)}) collective-permute-start(bf16[16,64,128]{2,1,0:T(8,128)(2,1)S(1)} %pad_maximum_fusion.refs_0_), channel_id=1, source_target_pairs={{0,12},{2,14},{4,0},{6,2},{8,4},{10,6},{12,8},{14,10},{1,13},{3,15... | collective-permute-start | bytes 786440 | tf_op jit(solution)/shard_map/ppermute | solution.py:331
  14.9 1.0 %collective-permute-start.9 = (bf16[8,64,128]{2,1,0:T(8,128)(2,1)S(1)}, bf16[8,64,128]{2,1,0:T(8,128)(2,1)}, u32[]{:S(2)}, u32[]{:S(2)}) collective-permute-start(bf16[8,64,128]{2,1,0:T(8,128)(2,1)S(1)} %get-tuple-element.23), channel_id=1, source_target_pairs={{0,8},{2,10},{4,12},{6,14},{8,0},{10,2},{12,4},{14,6},{1,9},{3,11}... | collective-permute-start | bytes 393224 | tf_op jit(solution)/shard_map/ppermute | solution.py:331
  15.9 1.9 %collective-permute-start.1 = (bf16[8,64,128]{2,1,0:T(8,128)(2,1)}, bf16[8,64,128]{2,1,0:T(8,128)(2,1)S(1)}, u32[]{:S(2)}, u32[]{:S(2)}) collective-permute-start(bf16[8,64,128]{2,1,0:T(8,128)(2,1)} %get-tuple-element.24), channel_id=1, source_target_pairs={{0,8},{2,10},{4,12},{6,14},{8,0},{10,2},{12,4},{14,6},{1,9},{3,11}... | collective-permute-start | bytes 393224 | tf_op jit(solution)/shard_map/ppermute | solution.py:331
  17.9 17.4 %collective-permute-done.9.refs_0_ = bf16[8,64,128]{2,1,0:T(8,128)(2,1)} collective-permute-done((bf16[8,64,128]{2,1,0:T(8,128)(2,1)S(1)}, bf16[8,64,128]{2,1,0:T(8,128)(2,1)}, u32[]{:S(2)}, u32[]{:S(2)}) %collective-permute-start.9) | collective-permute-done | bytes 131104 | tf_op jit(solution)/shard_map/ppermute | solution.py:331
  35.3 1.5 %collective-permute-start.4 = (bf16[16,64,128]{2,1,0:T(8,128)(2,1)S(1)}, bf16[16,64,128]{2,1,0:T(8,128)(2,1)S(1)}, u32[]{:S(2)}, u32[]{:S(2)}) collective-permute-start(bf16[16,64,128]{2,1,0:T(8,128)(2,1)S(1)} %pad_maximum_fusion.refs_0_), channel_id=1, source_target_pairs={{0,2},{2,0},{4,6},{6,4},{8,10},{10,8},{12,14},{14,12},{1,3},{3,1},... | collective-permute-start | bytes 786440 | tf_op jit(solution)/shard_map/ppermute | solution.py:332
  37.3 1.5 %collective-permute-start.8 = (bf16[16,64,128]{2,1,0:T(8,128)(2,1)S(1)}, bf16[16,64,128]{2,1,0:T(8,128)(2,1)}, u32[]{:S(2)}, u32[]{:S(2)}) collective-permute-start(bf16[16,64,128]{2,1,0:T(8,128)(2,1)S(1)} %collective-permute-done.7.refs_4_), channel_id=1, source_target_pairs={{0,2},{2,0},{4,6},{6,4},{8,10},{10,8},{12,14},{14,12},{1,3},{3,1},... | collective-permute-start | bytes 786440 | tf_op jit(solution)/shard_map/ppermute | solution.py:332
  39.4 1.4 %collective-permute-start.2 = (bf16[8,64,128]{2,1,0:T(8,128)(2,1)S(1)}, bf16[8,64,128]{2,1,0:T(8,128)(2,1)}, u32[]{:S(2)}, u32[]{:S(2)}) collective-permute-start(bf16[8,64,128]{2,1,0:T(8,128)(2,1)S(1)} %collective-permute-done.1.refs_0_), channel_id=1, source_target_pairs={{0,2},{2,0},{4,6},{6,4},{8,10},{10,8},{12,14},{14,12},{1,3},{3,1},... | collective-permute-start | bytes 393224 | tf_op jit(solution)/shard_map/ppermute | solution.py:332
  43.1 13.0 %slips.1 = (bf16[8,1024,1024]{2,1,0:T(8,128)(2,1)S(1)}, bf16[8,1024,1024]{2,1,0:T(8,128)(2,1)S(1)}) custom-call(f32[2,512]{1,0:T(2,128)S(1)} %copy-done.10, s32[1,1024]{1,0:T(1,128)S(1)} %bitcast.13, f32[1,1024]{1,0:T(1,128)S(1)} %bitcast.14, f32[256,1024]{1,0:T(8,128)S(1)} %amounts.1.own_ref, f32[256,1024]{1,0:T(8,128)S(1)} %collective-permute-done.3.other_ref), custom_call_target="tpu_custom_call" | custom-call | tf_op jit(solution)/shard_map/slips/pallas_call | solution.py:163
  56.1 5.7 %copy-done = bf16[8,1024,1024]{2,1,0:T(8,128)(2,1)} copy-done((bf16[8,1024,1024]{2,1,0:T(8,128)(2,1)}, bf16[8,1024,1024]{2,1,0:T(8,128)(2,1)S(1)}, u32[]{:S(2)}) %copy-start) | copy-done | bytes 16777240
  61.9 5.7 %copy-done.2 = bf16[8,1024,1024]{2,1,0:T(8,128)(2,1)} copy-done((bf16[8,1024,1024]{2,1,0:T(8,128)(2,1)}, bf16[8,1024,1024]{2,1,0:T(8,128)(2,1)S(1)}, u32[]{:S(2)}) %copy-start.2) | copy-done | bytes 16777240
  67.6 5.8 %copy-done.1 = bf16[8,1024,1024]{2,1,0:T(8,128)(2,1)S(1)} copy-done((bf16[8,1024,1024]{2,1,0:T(8,128)(2,1)S(1)}, bf16[8,1024,1024]{2,1,0:T(8,128)(2,1)}, u32[]{:S(2)}) %copy-start.1) | copy-done | bytes 16777240
  73.4 5.8 %copy-done.3 = bf16[8,1024,1024]{2,1,0:T(8,128)(2,1)S(1)} copy-done((bf16[8,1024,1024]{2,1,0:T(8,128)(2,1)S(1)}, bf16[8,1024,1024]{2,1,0:T(8,128)(2,1)}, u32[]{:S(2)}) %copy-start.3) | copy-done | bytes 16777240
  79.1 8.9 %partial_sums.1 = (f32[8,128,1024]{2,1,0:T(8,128)S(1)}, f32[8,128,1024]{2,1,0:T(8,128)S(1)}) custom-call(s32[4]{0:T(128)S(1)} %pad_add_fusion.1.numbers_ref, bf16[16,64,128]{2,1,0:T(8,128)(2,1)S(1)} %pad_maximum_fusion.refs_0_, bf16[16,64,128]{2,1,0:T(8,128)(2,1)S(1)} %collective-permute-done.4.refs_1_, ...), custom_call_target="tpu_custom_call" | custom-call | tf_op jit(solution)/shard_map/partial_sums/pallas_call | solution.py:221
  88.1 5.1 %finish.2.refs_4_ = f32[16,2,64,1024]{3,2,1,0:T(8,128)} custom-call(s32[2]{0:T(128)S(1)} %pad_add_fusion.numbers_ref, f32[1,1024]{1,0:T(1,128)S(1)} %bitcast.11, bf16[8,64,128]{2,1,0:T(8,128)(2,1)} %collective-permute-done.9.refs_0_, bf16[8,64,128]{2,1,0:T(8,128)(2,1)} %collective-permute-done.10.refs_1_, bf16[8,1024,1024]{2,1,0:T(8,128)(2,1)S(1)} %copy-done.1, ...), custom_call_target="tpu_custom_call" | custom-call | tf_op jit(solution)/shard_map/finish/pallas_call | solution.py:286
  93.2 2.2 %copy-done.4 = bf16[8,1024,1024]{2,1,0:T(8,128)(2,1)S(1)} copy-done((bf16[8,1024,1024]{2,1,0:T(8,128)(2,1)S(1)}, bf16[8,1024,1024]{2,1,0:T(8,128)(2,1)}, u32[]{:S(2)}) %copy-start.4) | copy-done | bytes 16777240
  95.5 4.9 %finish.3 = f32[16,2,64,1024]{3,2,1,0:T(8,128)} custom-call(s32[2]{0:T(128)S(1)} %pad_add_fusion.numbers_ref, f32[1,1024]{1,0:T(1,128)S(1)} %bitcast.12, bf16[8,64,128]{2,1,0:T(8,128)(2,1)S(1)} %collective-permute-done.1.refs_0_, bf16[8,64,128]{2,1,0:T(8,128)(2,1)} %collective-permute-done.2.refs_1_, ...), custom_call_target="tpu_custom_call", output_to_operand_aliasing={{}: (6, {})} | custom-call | tf_op jit(solution)/shard_map/finish/pallas_call | solution.py:286
  (36 shorter events, 5.6 us)
Async XLA Ops:
  0.0 1.4 %copy-start.5 = (bf16[2,6,1,32,16,128]{5,4,3,2,1,0:T(8,128)(2,1)S(1)}, bf16[2,6,1,32,16,128]{5,4,3,2,1,0:T(8,128)(2,1)}, u32[]{:S(2)}) copy-start(bf16[2,6,1,32,16,128]{5,4,3,2,1,0:T(8,128)(2,1)} %param.16) | copy-start | bytes 4718596
  1.4 0.7 copy-start.9
  4.4 1.5 %collective-permute-start = (bf16[16,32,128]{2,1,0:T(8,128)(2,1)S(1)}, bf16[16,32,128]{2,1,0:T(8,128)(2,1)S(1)}, u32[]{:S(2)}, u32[]{:S(2)}) collective-permute-start(bf16[16,32,128]{2,1,0:T(8,128)(2,1)S(1)} %get-tuple-element.15), channel_id=1, source_target_pairs={{0,1},{1,0},{2,3},{3,2},{4,5},{5,4},{6,7},{7,6},{8,9},{9,8},{10,11... | collective-permute-start | bytes 393224 | tf_op jit(solution)/shard_map/ppermute | solution.py:303
  5.9 1.2 %copy-start.6 = (s32[1024,256]{1,0:T(8,128)S(1)}, s32[1024,256]{1,0:T(8,128)}, u32[]{:S(2)}) copy-start(s32[1024,256]{1,0:T(8,128)} %mask_ref) | copy-start | bytes 3145732
  7.1 1.2 %copy-start.7 = (f32[1024,256]{1,0:T(8,128)S(1)}, f32[1024,256]{1,0:T(8,128)}, u32[]{:S(2)}) copy-start(f32[1024,256]{1,0:T(8,128)} %slip_ref) | copy-start | bytes 3145732
  9.1 30.4 %collective-permute-start.3 = (f32[256,1024]{1,0:T(8,128)S(1)}, f32[256,1024]{1,0:T(8,128)S(1)}, u32[]{:S(2)}, u32[]{:S(2)}) collective-permute-start(f32[256,1024]{1,0:T(8,128)S(1)} %amounts.1.own_ref), channel_id=1, source_target_pairs={{0,1},{1,0},{2,3},{3,2},{4,5},{5,4},{6,7},{7,6},{8,9},{9,8},{10,11... | collective-permute-start | bytes 3145736 | tf_op jit(solution)/shard_map/ppermute | solution.py:303
  9.5 27.3 %collective-permute-start.5 = (bf16[16,64,128]{2,1,0:T(8,128)(2,1)S(1)}, bf16[16,64,128]{2,1,0:T(8,128)(2,1)S(1)}, u32[]{:S(2)}, u32[]{:S(2)}) collective-permute-start(bf16[16,64,128]{2,1,0:T(8,128)(2,1)S(1)} %pad_maximum_fusion.refs_0_), channel_id=1, source_target_pairs={{0,4},{2,6},{4,8},{6,10},{8,12},{10,14},{12,0},{14,2},{1,5},{3,7},... | collective-permute-start | bytes 786440 | tf_op jit(solution)/shard_map/ppermute | solution.py:331
  12.2 25.1 %collective-permute-start.7 = (bf16[16,64,128]{2,1,0:T(8,128)(2,1)S(1)}, bf16[16,64,128]{2,1,0:T(8,128)(2,1)S(1)}, u32[]{:S(2)}, u32[]{:S(2)}) collective-permute-start(bf16[16,64,128]{2,1,0:T(8,128)(2,1)S(1)} %pad_maximum_fusion.refs_0_), channel_id=1, source_target_pairs={{0,12},{2,14},{4,0},{6,2},{8,4},{10,6},{12,8},{14,10},{1,13},{3,15... | collective-permute-start | bytes 786440 | tf_op jit(solution)/shard_map/ppermute | solution.py:331
  14.9 20.4 %collective-permute-start.9 = (bf16[8,64,128]{2,1,0:T(8,128)(2,1)S(1)}, bf16[8,64,128]{2,1,0:T(8,128)(2,1)}, u32[]{:S(2)}, u32[]{:S(2)}) collective-permute-start(bf16[8,64,128]{2,1,0:T(8,128)(2,1)S(1)} %get-tuple-element.23), channel_id=1, source_target_pairs={{0,8},{2,10},{4,12},{6,14},{8,0},{10,2},{12,4},{14,6},{1,9},{3,11}... | collective-permute-start | bytes 393224 | tf_op jit(solution)/shard_map/ppermute | solution.py:331
  15.9 22.9 %collective-permute-start.1 = (bf16[8,64,128]{2,1,0:T(8,128)(2,1)}, bf16[8,64,128]{2,1,0:T(8,128)(2,1)S(1)}, u32[]{:S(2)}, u32[]{:S(2)}) collective-permute-start(bf16[8,64,128]{2,1,0:T(8,128)(2,1)} %get-tuple-element.24), channel_id=1, source_target_pairs={{0,8},{2,10},{4,12},{6,14},{8,0},{10,2},{12,4},{14,6},{1,9},{3,11}... | collective-permute-start | bytes 393224 | tf_op jit(solution)/shard_map/ppermute | solution.py:331
  35.3 32.3 %collective-permute-start.4 = (bf16[16,64,128]{2,1,0:T(8,128)(2,1)S(1)}, bf16[16,64,128]{2,1,0:T(8,128)(2,1)S(1)}, u32[]{:S(2)}, u32[]{:S(2)}) collective-permute-start(bf16[16,64,128]{2,1,0:T(8,128)(2,1)S(1)} %pad_maximum_fusion.refs_0_), channel_id=1, source_target_pairs={{0,2},{2,0},{4,6},{6,4},{8,10},{10,8},{12,14},{14,12},{1,3},{3,1},... | collective-permute-start | bytes 786440 | tf_op jit(solution)/shard_map/ppermute | solution.py:332
  36.8 30.8 %collective-permute-start.6 = (bf16[16,64,128]{2,1,0:T(8,128)(2,1)S(1)}, bf16[16,64,128]{2,1,0:T(8,128)(2,1)S(1)}, u32[]{:S(2)}, u32[]{:S(2)}) collective-permute-start(bf16[16,64,128]{2,1,0:T(8,128)(2,1)S(1)} %collective-permute-done.5.refs_2_), channel_id=1, source_target_pairs={{0,2},{2,0},{4,6},{6,4},{8,10},{10,8},{12,14},{14,12},{1,3},{3,1},... | collective-permute-start | bytes 786440 | tf_op jit(solution)/shard_map/ppermute | solution.py:332
  37.3 30.2 %collective-permute-start.8 = (bf16[16,64,128]{2,1,0:T(8,128)(2,1)S(1)}, bf16[16,64,128]{2,1,0:T(8,128)(2,1)}, u32[]{:S(2)}, u32[]{:S(2)}) collective-permute-start(bf16[16,64,128]{2,1,0:T(8,128)(2,1)S(1)} %collective-permute-done.7.refs_4_), channel_id=1, source_target_pairs={{0,2},{2,0},{4,6},{6,4},{8,10},{10,8},{12,14},{14,12},{1,3},{3,1},... | collective-permute-start | bytes 786440 | tf_op jit(solution)/shard_map/ppermute | solution.py:332
  38.9 49.2 %collective-permute-start.10 = (bf16[8,64,128]{2,1,0:T(8,128)(2,1)}, bf16[8,64,128]{2,1,0:T(8,128)(2,1)}, u32[]{:S(2)}, u32[]{:S(2)}) collective-permute-start(bf16[8,64,128]{2,1,0:T(8,128)(2,1)} %collective-permute-done.9.refs_0_), channel_id=1, source_target_pairs={{0,2},{2,0},{4,6},{6,4},{8,10},{10,8},{12,14},{14,12},{1,3},{3,1},... | collective-permute-start | bytes 393224 | tf_op jit(solution)/shard_map/ppermute | solution.py:332
  39.4 53.8 %collective-permute-start.2 = (bf16[8,64,128]{2,1,0:T(8,128)(2,1)S(1)}, bf16[8,64,128]{2,1,0:T(8,128)(2,1)}, u32[]{:S(2)}, u32[]{:S(2)}) collective-permute-start(bf16[8,64,128]{2,1,0:T(8,128)(2,1)S(1)} %collective-permute-done.1.refs_0_), channel_id=1, source_target_pairs={{0,2},{2,0},{4,6},{6,4},{8,10},{10,8},{12,14},{14,12},{1,3},{3,1},... | collective-permute-start | bytes 393224 | tf_op jit(solution)/shard_map/ppermute | solution.py:332
  41.0 0.7 copy-start.10
  41.7 0.7 copy-start.11
  42.4 0.7 copy-start.12
  56.1 5.7 %copy-start = (bf16[8,1024,1024]{2,1,0:T(8,128)(2,1)}, bf16[8,1024,1024]{2,1,0:T(8,128)(2,1)S(1)}, u32[]{:S(2)}) copy-start(bf16[8,1024,1024]{2,1,0:T(8,128)(2,1)S(1)} %get-tuple-element.20.refs_6_.refs_2_) | copy-start | bytes 50331652
  61.9 5.7 %copy-start.2 = (bf16[8,1024,1024]{2,1,0:T(8,128)(2,1)}, bf16[8,1024,1024]{2,1,0:T(8,128)(2,1)S(1)}, u32[]{:S(2)}) copy-start(bf16[8,1024,1024]{2,1,0:T(8,128)(2,1)S(1)} %get-tuple-element.19.refs_7_.refs_2_) | copy-start | bytes 50331652
  67.6 5.8 %copy-start.1 = (bf16[8,1024,1024]{2,1,0:T(8,128)(2,1)S(1)}, bf16[8,1024,1024]{2,1,0:T(8,128)(2,1)}, u32[]{:S(2)}) copy-start(bf16[8,1024,1024]{2,1,0:T(8,128)(2,1)} %copy-done) | copy-start | bytes 50331652
  73.4 5.8 %copy-start.3 = (bf16[8,1024,1024]{2,1,0:T(8,128)(2,1)S(1)}, bf16[8,1024,1024]{2,1,0:T(8,128)(2,1)}, u32[]{:S(2)}) copy-start(bf16[8,1024,1024]{2,1,0:T(8,128)(2,1)} %copy-done.2) | copy-start | bytes 50331652
  79.1 8.9 %copy-start.8 = (f32[1024]{0:T(1024)S(1)}, f32[1024]{0:T(1024)}, u32[]{:S(2)}) copy-start(f32[1024]{0:T(1024)} %param.12) | copy-start | bytes 12292
  88.1 7.4 %copy-start.4 = (bf16[8,1024,1024]{2,1,0:T(8,128)(2,1)S(1)}, bf16[8,1024,1024]{2,1,0:T(8,128)(2,1)}, u32[]{:S(2)}) copy-start(bf16[8,1024,1024]{2,1,0:T(8,128)(2,1)} %copy-done.2) | copy-start | bytes 50331652
  (1 other events, 0.7 us)

commit v3 on v1

v3 whole, which is shorter than its diff:
```python
import functools

import jax
import jax.numpy as jnp
from jax import lax
from jax.experimental import pallas as pl
from jax.experimental.pallas import tpu as pltpu
from jax.sharding import PartitionSpec as P

VMEM = pl.BlockSpec(memory_space=pltpu.VMEM)
SMEM = pl.BlockSpec(memory_space=pltpu.SMEM)
ANY = pl.BlockSpec(memory_space=pl.ANY)
ROOMY = pltpu.CompilerParams(vmem_limit_bytes=56 * 2**20)
SMALL = pltpu.CompilerParams(vmem_limit_bytes=12 * 2**20)
BASE_FREQ = 0.0625
LANES = 256
BLOCK = 128
UNITS = 4


def cost(microseconds):
    return pl.CostEstimate(flops=int(microseconds * 1.1e9), bytes_accessed=int(microseconds * 3e6), transcendentals=0)


def rotate_kernel(green_ref, tensor_ref, ids_ref, own_ref, other_ref, sums, rows):
    _, comps, count, freqs, stations = green_ref.shape
    half = stations // 2
    first = lax.axis_index("var") * count

    def one_subfault(m, carry):
        for part in range(2):
            total = green_ref[part, 0, m].astype(jnp.float32) * tensor_ref[0, first + m]
            for comp in range(1, comps):
                total = total + green_ref[part, comp, m].astype(jnp.float32) * tensor_ref[comp, first + m]
            at = pl.ds(pl.multiple_of(m * freqs, freqs), freqs)
            sums[at, part * stations : (part + 1) * stations] = total.astype(jnp.bfloat16)
        return carry

    lax.fori_loop(0, count, one_subfault, 0, unroll=4)

    lane = lax.broadcasted_iota(jnp.int32, (1, stations), 1)
    ids = ids_ref[...]
    turned = pltpu.roll(ids, half, 1)
    low = jnp.where(lane < half, ids, turned)
    high = jnp.where(lane < half, turned, ids)
    is_first = lax.axis_index("sub") == 0
    wanted = jnp.concatenate([jnp.where(is_first, low, high), jnp.where(is_first, high, low)], axis=1)
    row = lax.broadcasted_iota(jnp.int32, (2 * stations, 2 * stations), 0)
    column = lax.broadcasted_iota(jnp.int32, (2 * stations, 2 * stations), 1)
    part_of_column = (column // half) % 2
    picks = (row == wanted + part_of_column * stations).astype(jnp.float32).astype(jnp.bfloat16)
    picked = jnp.dot(sums[...], picks, preferred_element_type=jnp.float32)
    rows[0] = picked[:, :stations]
    rows[1] = picked[:, stations:]
    for k in range(freqs):
        at = pl.ds(k, count, stride=freqs)
        own_ref[k] = rows[0, at, :].astype(jnp.bfloat16)
        other_ref[k] = rows[1, at, :].astype(jnp.bfloat16)


def rotate(green, tensor, station_ids):
    _, _, count, freqs, stations = green.shape
    piece = jax.ShapeDtypeStruct((freqs, count, stations), jnp.bfloat16)
    return pl.pallas_call(
        rotate_kernel,
        out_shape=(piece, piece),
        in_specs=[VMEM, SMEM, VMEM],
        out_specs=(VMEM, VMEM),
        scratch_shapes=[
            pltpu.VMEM((count * freqs, 2 * stations), jnp.bfloat16),
            pltpu.VMEM((2, count * freqs, stations), jnp.float32),
        ],
        compiler_params=ROOMY,
        cost_estimate=cost(3),
        name="rotate",
    )(green, tensor, station_ids.reshape((1, stations)))


TOKEN = jax.ShapeDtypeStruct((8, 128), jnp.float32)


def prepare_kernel(
    points_ref, hypocenter_ref, velocity_ref, own_mask, own_slip, other_mask, other_slip, after_ref, *outs
):
    own_out, other_out, columns, spots, token = outs
    half, variations = own_out.shape
    subfaults = 2 * half
    token[...] = jnp.zeros_like(token)
    first = pl.multiple_of(lax.axis_index("sub") * half, half)
    second = pl.multiple_of(half - first, half)
    for axis in range(2):
        for at, start in ((0, first), (half, second)):
            wide = jnp.broadcast_to(points_ref[axis : axis + 1, pl.ds(start, half)], (BLOCK, half))
            columns[axis, at : at + half, :] = wide.T

    rest = points_ref[...]
    thirds = []
    for _ in range(3):
        thirds.append(rest.astype(jnp.bfloat16))
        rest = rest - thirds[-1].astype(jnp.float32)
    thirds = jnp.concatenate([t.astype(jnp.float32) for t in thirds], axis=0).astype(jnp.bfloat16)
    for lane in range(0, variations, LANES):
        lanes = slice(lane, lane + LANES)
        index = lax.broadcasted_iota(jnp.int32, (subfaults, LANES), 0)
        here = (index == hypocenter_ref[0:1, lanes]).astype(jnp.float32).astype(jnp.bfloat16)
        spot = jnp.dot(thirds, here, preferred_element_type=jnp.float32)
        spots[0:2, lanes] = (spot[0:2] + spot[2:4]) + spot[4:6]
        spots[2:3, lanes] = BASE_FREQ / velocity_ref[0:1, lanes]

    for mask, slip, out in ((own_mask, own_slip, own_out), (other_mask, other_slip, other_out)):
        for row in range(0, variations, BLOCK):
            rows = slice(row, row + BLOCK)
            out[:, rows] = (mask[rows, :].astype(jnp.float32) * slip[rows, :]).T


def prepare(points, hypocenter, velocity, own_mask, own_slip, other_mask, other_slip, after):
    variations, half = own_mask.shape
    out = jax.ShapeDtypeStruct((half, variations), jnp.float32)
    columns = jax.ShapeDtypeStruct((2, 2 * half, BLOCK), jnp.float32)
    spots = jax.ShapeDtypeStruct((8, variations), jnp.float32)
    return pl.pallas_call(
        prepare_kernel,
        out_shape=(out, out, columns, spots, TOKEN),
        in_specs=[VMEM] * 7 + [ANY],
        out_specs=(VMEM,) * 5,
        compiler_params=SMALL,
        cost_estimate=cost(3),
        name="prepare",
    )(points, hypocenter[None, :], velocity[None, :], own_mask, own_slip, other_mask, other_slip, after)


SIN = (3.14159264, -5.16771008, 2.55007751, -0.598291190, 0.0776574420)
COS = (0.999999953, -4.93479283, 4.05841131, -1.33187624, 0.219688854)


def sine_cosine(turns):
    rest = turns - jnp.floor(turns + 0.5)
    square = rest * rest
    sine = SIN[-1]
    for c in SIN[-2::-1]:
        sine = sine * square + c
    sine = sine * rest
    cosine = COS[-1]
    for c in COS[-2::-1]:
        cosine = cosine * square + c
    return 2.0 * sine * cosine, 1.0 - 2.0 * sine * sine


def fill(slips_ref, numbers_ref, unit, step, columns, spots, own_ref, other_ref):
    freqs, _, depth, _ = slips_ref.shape
    half = own_ref.shape[0]
    rows = depth // 8
    piece, block = step % 2, step // 2
    row = pl.multiple_of((2 * numbers_ref[1 + unit] + (piece ^ numbers_ref[0])) * rows, rows)
    lanes = pl.ds(pl.multiple_of(block * BLOCK, BLOCK), BLOCK)
    for part, source in enumerate((own_ref, other_ref)):
        at = pl.ds(part * half + row, rows)
        east = columns[0, at, :] - spots[0:1, lanes]
        north = columns[1, at, :] - spots[1:2, lanes]
        gap = east * east + north * north
        distance = gap * lax.rsqrt(jnp.maximum(gap, 1e-30))
        sine, cosine = sine_cosine(distance * spots[2:3, lanes])
        amount = source[pl.ds(row, rows), lanes]
        twice = 2.0 * cosine
        re_last, im_last = amount, None
        re, im = amount * cosine, amount * sine
        place = pl.multiple_of((4 * piece + part) * rows, rows)
        for k in range(freqs):
            slips_ref[k, block, pl.ds(place, rows), :] = re.astype(jnp.bfloat16)
            slips_ref[k, block, pl.ds(place + 2 * rows, rows), :] = im.astype(jnp.bfloat16)
            re, re_last = twice * re - re_last, re
            im, im_last = (twice * im if im_last is None else twice * im - im_last), im


def unit_sum(k, first, pair, slips_ref):
    half = pair[0].shape[2] // 2
    lane = lax.broadcasted_iota(jnp.int32, (1, 2 * half), 1)
    table = []
    for ref in pair:
        block = ref[k]
        turned = pltpu.roll(block.astype(jnp.float32), half, 1)
        table += [block, jnp.where(lane < half, turned, -turned).astype(jnp.bfloat16)]
    wide = jnp.concatenate([slips_ref[first + k, block] for block in range(slips_ref.shape[1])], axis=1)
    return lax.dot_general(
        jnp.concatenate(table, axis=0), wide, (((0,), (0,)), ((), ())), preferred_element_type=jnp.float32
    )


def work_kernel(fills, has_sum, has_total, unroll, numbers_ref, *refs):
    refs = list(refs)
    take = lambda n: [refs.pop(0) for _ in range(n)]
    sources = take(4) if fills else None
    pair, (slips_ref,) = (take(2), take(1)) if has_sum else (None, (None,))
    (total_ref,) = take(1) if has_total else (None,)
    token = refs.pop()
    (sum_ref,) = [refs.pop()] if has_sum else (None,)
    outs = refs[len(refs) - len(fills) :]
    token[...] = jnp.zeros_like(token)

    def body(k, carry):
        for unit, out in zip(fills, outs):
            fill(out, numbers_ref, unit, k, *sources)
        if has_sum:
            term = unit_sum(k, 0, pair, slips_ref)
            sum_ref[k] = term + total_ref[k] if has_total else term
        return carry

    lax.fori_loop(0, FREQS, body, 0, unroll=unroll)


FREQS = 16


def work(numbers, sources, fills, pair=None, unit_slips=None, total=None, after=()):
    columns, spots, own, other = sources
    variations = own.shape[1]
    freqs = FREQS
    args, aliases = [numbers], {}
    if fills:
        args += sources
    shapes = [
        jax.ShapeDtypeStruct((freqs, variations // BLOCK, 4 * own.shape[0] // UNITS, BLOCK), jnp.bfloat16)
    ] * len(fills)
    if pair is not None:
        args += [*pair, unit_slips]
        if total is not None:
            aliases = {len(args): len(shapes)}
            args.append(total)
        shapes.append(jax.ShapeDtypeStruct((freqs, pair[0].shape[2], variations), jnp.float32))
    shapes.append(TOKEN)
    return pl.pallas_call(
        functools.partial(work_kernel, fills, pair is not None, total is not None, 1 if len(fills) > 1 else 2),
        out_shape=tuple(shapes),
        in_specs=[SMEM] + [VMEM] * (len(args) - 1) + [ANY] * len(after),
        out_specs=(VMEM,) * len(shapes),
        input_output_aliases=aliases,
        compiler_params=SMALL,
        cost_estimate=cost(3),
        name="work" + "".join(str(u) for u in fills) + ("_sum" if pair is not None else ""),
    )(*args, *after)


def finish_kernel(first, count, rise_ref, *refs):
    pair, slips_ref, sums_ref = refs[:2], refs[2], refs[3]
    out_ref, buffers, sems = refs[-3:]

    def copy(k):
        return pltpu.make_async_copy(buffers.at[k], out_ref.at[first + k], sems.at[k])

    def body(k, carry):
        total = sums_ref[first + k] + unit_sum(k, first, pair, slips_ref)
        stations = total.shape[0] // 2
        re, im = total[:stations], total[stations:]
        pulsation = (first + k + 1).astype(jnp.float32) * (2.0 * jnp.pi * BASE_FREQ)
        damping = pulsation * rise_ref[...]
        scale = 1.0 / (1.0 + damping * damping)
        tilt = scale * damping
        buffers[k, 0] = scale * re + tilt * im
        buffers[k, 1] = scale * im - tilt * re
        copy(k).start()
        return carry

    lax.fori_loop(0, count, body, 0, unroll=2)
    for k in range(count):
        copy(k).wait()


def finish(first, rise_time, pair, unit_slips, sums, so_far):
    count, _, lanes = pair[0].shape
    stations = lanes // 2
    total, _, variations = sums.shape
    args = [rise_time[None, :], *pair, unit_slips, sums]
    specs = [VMEM] * len(args)
    aliases = {}
    if so_far is not None:
        aliases = {len(args): 0}
        args.append(so_far)
        specs.append(ANY)
    return pl.pallas_call(
        functools.partial(finish_kernel, first, count),
        out_shape=jax.ShapeDtypeStruct((total, 2, stations, variations), jnp.float32),
        in_specs=specs,
        out_specs=ANY,
        scratch_shapes=[
            pltpu.VMEM((count, 2, stations, variations), jnp.float32),
            pltpu.SemaphoreType.DMA((count,)),
        ],
        input_output_aliases=aliases,
        compiler_params=SMALL,
        cost_estimate=cost(2),
        name="finish",
    )(*args)


def swap(array, axis):
    return lax.ppermute(array, axis, [(0, 1), (1, 0)])


def along(piece, s):
    return lax.ppermute(piece, "var", [(i, (i + 2 * s) % 8) for i in range(8)])


def across(piece):
    return lax.ppermute(piece, "var", [(i, i ^ 1) for i in range(8)])


def gate_kernel(array_ref, token_ref, out_ref):
    pass


def gate(array, token):
    return pl.pallas_call(
        gate_kernel,
        out_shape=jax.ShapeDtypeStruct(array.shape, array.dtype),
        in_specs=[ANY, ANY],
        out_specs=ANY,
        input_output_aliases={0: 0},
        compiler_params=SMALL,
        name="gate",
    )(array, token)


def shards(size, fault_points, hypocenter, velocity, rise_time, member_mask, slip_amount, moment_tensor, strain_green, station_ids):
    freqs = strain_green.shape[4]
    half = moment_tensor.shape[1]
    rows = half // (2 * UNITS)
    groups = (freqs // 2, freqs - freqs // 2)
    cuts = ((0, groups[0]), (groups[0], freqs))
    swapped = [swap(array, "sub") for array in (member_mask, slip_amount)]
    own_part, other_part = rotate(strain_green[:, :, 0], moment_tensor, station_ids)
    received = swap(other_part, "sub")
    routed = size == 2 * UNITS
    if routed:
        place = lax.axis_index("var")
        block = jnp.concatenate([own_part, received], axis=1)
        pieces = [block, along(block, 1), along(block, 3)]
        numbers = jnp.stack([place % 2] + [((place - 2 * s) % 8) // 2 for s in (0, 1, 3, 2)]).astype(jnp.int32)
    else:
        whole = [lax.all_gather(piece, "var", axis=1, tiled=True) for piece in (own_part, received)]
        pieces = [
            jnp.concatenate([part[:, i * rows : (i + 1) * rows] for part in whole], axis=1) for i in range(2 * UNITS)
        ]
        pairs = [(pieces[2 * i], pieces[2 * i + 1]) for i in range(UNITS)]
        last = [tuple(piece[i:j] for piece in pairs[-1]) for i, j in cuts]
        numbers = jnp.arange(-1, UNITS, dtype=jnp.int32) * (jnp.arange(1 + UNITS, dtype=jnp.int32) > 0)

    own, other, columns, spots, token = prepare(
        fault_points, hypocenter, velocity, member_mask, slip_amount, *swapped, pieces[0]
    )
    step = functools.partial(work, numbers, (columns, spots, own, other))
    if routed:
        parts = [gate(block[i:j], token) for i, j in cuts]
        last = [along(part, 2) for part in parts]
        pairs = [(block, across(block))]
    else:
        parts = (token,)
    slips_0, slips_1, token = step((0, 1), after=parts)
    if routed:
        pieces[1] = gate(pieces[1], token)
        pairs.append((pieces[1], across(pieces[1])))
    slips_3, total, token = step((2,), pairs[0], slips_0, after=pieces[1:2])
    if routed:
        pieces[2] = gate(pieces[2], token)
        pairs.append((pieces[2], across(pieces[2])))
    slips_2, total, token = step((3,), pairs[1], slips_1, total, after=pieces[2:3])
    if routed:
        last = [gate(piece, token) for piece in last]
        last = [(piece, across(piece)) for piece in last]
    total, token = step((), pairs[2], slips_3, total, after=(last[0][0], last[1][0]))
    out = None
    for (first, _), pair in zip(cuts, last):
        out = finish(first, rise_time, pair, slips_2, total, out)
    return out


def solution(mesh):
    placed = (
        P(None, "site"),
        P(("site", "var")),
        P(("site", "var")),
        P(("site", "var")),
        P(("site", "var"), "sub"),
        P(("site", "var"), "sub"),
        P(None, ("site", "sub")),
        P("site", None, "sub", "var", None, None),
        P("site"),
    )
    return jax.shard_map(
        functools.partial(shards, mesh.shape["var"]),
        mesh=mesh,
        in_specs=placed,
        out_specs=P(None, None, "sub", ("site", "var")),
        check_vma=False,
    )
```

time: 79.8 us -> 51.7 us (0.65)
  the two profiles are of different devices: /device:TPU:24 before, /device:TPU:18 now
where the time goes in v3:
time: 51.7 us; the launch traced here: 51.5 us
  Pallas kernels  30.8 us (60%)
  starting transfers between devices  11.4 us (22%)
  waiting for transfers between devices  8.11 us (16%)
  local copies, waits for them, and re-layouts  1.06 us (2%)
    pallas_call x4, Pallas kernels, work(): pl.pallas_call(functools.partial(work_kernel, fills, pair is not None, to...  19.9 us
    ppermute x4, waiting for transfers between devices, along(): return lax.ppermute(piece, 'var', [(i, (i + 2 * s) % 8) for i in range(8)])  7.25 us
    ppermute x5, starting transfers between devices, across(): return lax.ppermute(piece, 'var', [(i, i ^ 1) for i in range(8)])  5.77 us
    pallas_call x2, Pallas kernels, finish(): pl.pallas_call(functools.partial(finish_kernel, first, count), out_shape=...  5.4 us
    ppermute x4, starting transfers between devices, along(): return lax.ppermute(piece, 'var', [(i, (i + 2 * s) % 8) for i in range(8)])  5.02 us
    pallas_call x1, Pallas kernels, rotate(): pl.pallas_call(rotate_kernel, out_shape=(piece, piece), in_specs=[VMEM, S...  3.1 us
    pallas_call x1, Pallas kernels, prepare(): pl.pallas_call(prepare_kernel, out_shape=(out, out, columns, spots, TOKEN...  2.3 us
  transfers between devices with their start and end apart: 12, of which 3 were waited for; matrix products, arithmetic and copies ran while one was open for 2% of the time, Pallas kernels for 54%

profile of v3, /device:TPU:18, one launch (start us, length us, event | category | flops | bytes accessed | tf_op | source)
XLA Modules:
  0.0 51.5 jit_solution(12709376363115112758)
XLA Ops:
  0.0 0.1 collective-permute-start.1
  0.1 0.5 collective-permute-start.2
  0.6 3.1 %rotate.1 = (bf16[16,32,128]{2,1,0:T(8,128)(2,1)}, bf16[16,32,128]{2,1,0:T(8,128)(2,1)}) custom-call(bf16[2,6,32,16,128]{4,3,2,1,0:T(8,128)(2,1)} %bitcast.14, f32[6,256]{1,0:T(8,128)} %tensor_ref.1, s32[1,128]{1,0:T(1,128)} %bitcast.15), custom_call_target="tpu_custom_call" | custom-call | flops 3300000000 | bytes 9000000 | tf_op jit(solution)/shard_map/rotate/pallas_call | solution.py:64
  3.7 0.1 stack.23.numbers_ref
  3.8 0.9 %constant_dynamic-update-slice_fusion.1 = bf16[16,64,128]{2,1,0:T(8,128)(2,1)S(1)} fusion(bf16[16,32,128]{2,1,0:T(8,128)(2,1)} %get-tuple-element.22), kind=kLoop, calls=%fused_computation.1 | loop fusion | bytes 262144
  4.7 0.5 %collective-permute-done = bf16[16,32,128]{2,1,0:T(8,128)(2,1)S(1)} collective-permute-done((bf16[16,32,128]{2,1,0:T(8,128)(2,1)}, bf16[16,32,128]{2,1,0:T(8,128)(2,1)S(1)}, u32[]{:S(2)}, u32[]{:S(2)}) %collective-permute-start) | collective-permute-done | bytes 131104 | tf_op jit(solution)/shard_map/ppermute | solution.py:296
  5.3 1.6 %collective-permute-start.6 = (bf16[16,64,128]{2,1,0:T(8,128)(2,1)S(1)}, bf16[16,64,128]{2,1,0:T(8,128)(2,1)S(1)}, u32[]{:S(2)}, u32[]{:S(2)}) collective-permute-start(bf16[16,64,128]{2,1,0:T(8,128)(2,1)S(1)} %constant_dynamic-update-slice_fusion.after_ref.refs_4_), channel_id=1, source_target_pairs={{0,2},{2,0},{4,6},{6,4},{8,10},{10,8},{12,14},{14,12},{1,3},{3,1},... | collective-permute-start | bytes 786440 | tf_op jit(solution)/shard_map/ppermute | solution.py:304
  6.9 1.6 %collective-permute-start.4 = (bf16[16,64,128]{2,1,0:T(8,128)(2,1)S(1)}, bf16[16,64,128]{2,1,0:T(8,128)(2,1)S(1)}, u32[]{:S(2)}, u32[]{:S(2)}) collective-permute-start(bf16[16,64,128]{2,1,0:T(8,128)(2,1)S(1)} %constant_dynamic-update-slice_fusion.after_ref.refs_4_), channel_id=1, source_target_pairs={{0,4},{2,6},{4,8},{6,10},{8,12},{10,14},{12,0},{14,2},{1,5},{3,7},... | collective-permute-start | bytes 786440 | tf_op jit(solution)/shard_map/ppermute | solution.py:300
  8.5 0.4 collective-permute-start.7
  9.0 2.3 %prepare.1 = (f32[256,1024]{1,0:T(8,128)S(1)}, f32[256,1024]{1,0:T(8,128)S(1)}, f32[2,512,128]{2,1,0:T(8,128)S(1)}, f32[8,1024]{1,0:T(8,128)S(1)}, f32[8,128]{1,0:T(8,128)S(1)}) custom-call(f32[2,512]{1,0:T(2,128)S(1)} %copy-done.3, s32[1,1024]{1,0:T(1,128)S(1)} %bitcast.12, f32[1,1024]{1,0:T(1,128)S(1)} %bitcast.13, s32[1024,256]{1,0:T(8,128)S(1)} %copy-done.1, ...), custom_call_target="tpu_custom_call" | custom-call | flops 3300000000 | bytes 9000000 | tf_op jit(solution)/shard_map/prepare/pallas_call | solution.py:121
  11.3 2.2 %collective-permute-start.3 = (bf16[8,64,128]{2,1,0:T(8,128)(2,1)S(1)}, bf16[8,64,128]{2,1,0:T(8,128)(2,1)S(1)}, u32[]{:S(2)}, u32[]{:S(2)}) collective-permute-start(bf16[8,64,128]{2,1,0:T(8,128)(2,1)S(1)} %gate.6.refs_5_), channel_id=1, source_target_pairs={{0,8},{2,10},{4,12},{6,14},{8,0},{10,2},{12,4},{14,6},{1,9},{3,11}... | collective-permute-start | bytes 393224 | tf_op jit(solution)/shard_map/ppermute | solution.py:300
  13.5 0.8 %collective-permute-start.10 = (bf16[8,64,128]{2,1,0:T(8,128)(2,1)S(1)}, bf16[8,64,128]{2,1,0:T(8,128)(2,1)S(1)}, u32[]{:S(2)}, u32[]{:S(2)}) collective-permute-start(bf16[8,64,128]{2,1,0:T(8,128)(2,1)S(1)} %gate.7.refs_4_), channel_id=1, source_target_pairs={{0,8},{2,10},{4,12},{6,14},{8,0},{10,2},{12,4},{14,6},{1,9},{3,11}... | collective-permute-start | bytes 393224 | tf_op jit(solution)/shard_map/ppermute | solution.py:300
  14.3 5.5 %work01.1 = (bf16[16,8,256,128]{3,2,1,0:T(8,128)(2,1)S(1)}, bf16[16,8,256,128]{3,2,1,0:T(8,128)(2,1)S(1)}, f32[8,128]{1,0:T(8,128)S(1)}) custom-call(s32[5]{0:T(128)S(1)} %stack.23.numbers_ref, f32[2,512,128]{2,1,0:T(8,128)S(1)} %get-tuple-element.25.refs_0_, f32[8,1024]{1,0:T(8,128)S(1)} %get-tuple-element.26.refs_1_, ...), custom_call_target="tpu_custom_call" | custom-call | flops 3300000000 | bytes 9000000 | tf_op jit(solution)/shard_map/work01/pallas_call | solution.py:231
  19.8 7.2 %collective-permute-done.4.array_ref = bf16[16,64,128]{2,1,0:T(8,128)(2,1)S(1)} collective-permute-done((bf16[16,64,128]{2,1,0:T(8,128)(2,1)S(1)}, bf16[16,64,128]{2,1,0:T(8,128)(2,1)S(1)}, u32[]{:S(2)}, u32[]{:S(2)}) %collective-permute-start.4) | collective-permute-done | bytes 262176 | tf_op jit(solution)/shard_map/ppermute | solution.py:300
  27.1 0.5 collective-permute-start.5
  27.6 5.2 %work2_sum.1 = (bf16[16,8,256,128]{3,2,1,0:T(8,128)(2,1)S(1)}, f32[16,128,1024]{2,1,0:T(8,128)S(1)}, f32[8,128]{1,0:T(8,128)S(1)}) custom-call(s32[5]{0:T(128)S(1)} %stack.23.numbers_ref, f32[2,512,128]{2,1,0:T(8,128)S(1)} %get-tuple-element.25.refs_0_, f32[8,1024]{1,0:T(8,128)S(1)} %get-tuple-element.26.refs_1_, f32[256,1024]{1,0:T(8,128)S(1)} %get-tuple-element.27.refs_2_, ...), custom_call_target="tpu_custom_call" | custom-call | flops 3300000000 | bytes 9000000 | tf_op jit(solution)/shard_map/work2_sum/pallas_call | solution.py:231
  32.8 1.6 %collective-permute-start.9 = (bf16[16,64,128]{2,1,0:T(8,128)(2,1)S(1)}, bf16[16,64,128]{2,1,0:T(8,128)(2,1)S(1)}, u32[]{:S(2)}, u32[]{:S(2)}) collective-permute-start(bf16[16,64,128]{2,1,0:T(8,128)(2,1)S(1)} %gate.9.refs_8_.refs_0_), channel_id=1, source_target_pairs={{0,2},{2,0},{4,6},{6,4},{8,10},{10,8},{12,14},{14,12},{1,3},{3,1},... | collective-permute-start | bytes 786440 | tf_op jit(solution)/shard_map/ppermute | solution.py:304
  34.4 5.3 %work3_sum.1 = (bf16[16,8,256,128]{3,2,1,0:T(8,128)(2,1)S(1)}, f32[16,128,1024]{2,1,0:T(8,128)S(1)}, f32[8,128]{1,0:T(8,128)S(1)}) custom-call(s32[5]{0:T(128)S(1)} %stack.23.numbers_ref, f32[2,512,128]{2,1,0:T(8,128)S(1)} %get-tuple-element.25.refs_0_, f32[8,1024]{1,0:T(8,128)S(1)} %get-tuple-element.26.refs_1_, ...), custom_call_target="tpu_custom_call", output_to_operand_aliasing={{1}: (8, {})} | custom-call | flops 3300000000 | bytes 9000000 | tf_op jit(solution)/shard_map/work3_sum/pallas_call | solution.py:231
  39.6 0.6 %collective-permute-start.8 = (bf16[8,64,128]{2,1,0:T(8,128)(2,1)S(1)}, bf16[8,64,128]{2,1,0:T(8,128)(2,1)S(1)}, u32[]{:S(2)}, u32[]{:S(2)}) collective-permute-start(bf16[8,64,128]{2,1,0:T(8,128)(2,1)S(1)} %gate.10.refs_5_.refs_0_), channel_id=1, source_target_pairs={{0,2},{2,0},{4,6},{6,4},{8,10},{10,8},{12,14},{14,12},{1,3},{3,1},... | collective-permute-start | bytes 393224 | tf_op jit(solution)/shard_map/ppermute | solution.py:304
  40.2 1.5 %collective-permute-start.11 = (bf16[8,64,128]{2,1,0:T(8,128)(2,1)S(1)}, bf16[8,64,128]{2,1,0:T(8,128)(2,1)S(1)}, u32[]{:S(2)}, u32[]{:S(2)}) collective-permute-start(bf16[8,64,128]{2,1,0:T(8,128)(2,1)S(1)} %gate.11.refs_4_.refs_0_), channel_id=1, source_target_pairs={{0,2},{2,0},{4,6},{6,4},{8,10},{10,8},{12,14},{14,12},{1,3},{3,1},... | collective-permute-start | bytes 393224 | tf_op jit(solution)/shard_map/ppermute | solution.py:304
  41.7 4.0 %work_sum.1 = (f32[16,128,1024]{2,1,0:T(8,128)S(1)}, f32[8,128]{1,0:T(8,128)}) custom-call(s32[5]{0:T(128)S(1)} %stack.23.numbers_ref, bf16[16,64,128]{2,1,0:T(8,128)(2,1)S(1)} %gate.9.refs_8_.refs_0_, bf16[16,64,128]{2,1,0:T(8,128)(2,1)S(1)} %collective-permute-done.9.refs_1_, ...), custom_call_target="tpu_custom_call", output_to_operand_aliasing={{0}: (4, {})} | custom-call | flops 3300000000 | bytes 9000000 | tf_op jit(solution)/shard_map/work_sum/pallas_call | solution.py:231
  45.8 0.3 collective-permute-done.11.refs_1_
  46.1 2.7 %finish.2.refs_4_ = f32[16,2,64,1024]{3,2,1,0:T(8,128)} custom-call(f32[1,1024]{1,0:T(1,128)S(1)} %bitcast.10, bf16[8,64,128]{2,1,0:T(8,128)(2,1)S(1)} %gate.11.refs_4_.refs_0_, bf16[8,64,128]{2,1,0:T(8,128)(2,1)S(1)} %collective-permute-done.11.refs_1_, bf16[16,8,256,128]{3,2,1,0:T(8,128)(2,1)S(1)} %get-tuple-element.35.refs_2_, ...), custom_call_target="tpu_custom_call" | custom-call | flops 2200000000 | bytes 6000000 | tf_op jit(solution)/shard_map/finish/pallas_call | solution.py:279
  48.8 2.7 %finish.3 = f32[16,2,64,1024]{3,2,1,0:T(8,128)} custom-call(f32[1,1024]{1,0:T(1,128)S(1)} %bitcast.11, bf16[8,64,128]{2,1,0:T(8,128)(2,1)S(1)} %gate.10.refs_5_.refs_0_, bf16[8,64,128]{2,1,0:T(8,128)(2,1)S(1)} %collective-permute-done.8.refs_1_, bf16[16,8,256,128]{3,2,1,0:T(8,128)(2,1)S(1)} %get-tuple-element.35.refs_2_, ...), custom_call_target="tpu_custom_call", output_to_operand_aliasing={{}: (5, {})} | custom-call | flops 2200000000 | bytes 6000000 | tf_op jit(solution)/shard_map/finish/pallas_call | solution.py:279
  (30 shorter events, 0.1 us)
Async XLA Ops:
  0.0 8.9 %copy-start.1 = (s32[1024,256]{1,0:T(8,128)S(1)}, s32[1024,256]{1,0:T(8,128)}, u32[]{:S(2)}) copy-start(s32[1024,256]{1,0:T(8,128)} %own_mask.1) | copy-start | bytes 3145732
  0.0 9.0 %copy-start.2 = (f32[1024,256]{1,0:T(8,128)S(1)}, f32[1024,256]{1,0:T(8,128)}, u32[]{:S(2)}) copy-start(f32[1024,256]{1,0:T(8,128)} %own_slip.1) | copy-start | bytes 3145732
  0.0 9.0 %copy-start.5 = (f32[1024]{0:T(1024)S(1)}, f32[1024]{0:T(1024)}, u32[]{:S(2)}) copy-start(f32[1024]{0:T(1024)} %param.11) | copy-start | bytes 12292
  0.0 9.0 %copy-start.4 = (s32[1024]{0:T(1024)S(1)}, s32[1024]{0:T(1024)}, u32[]{:S(2)}) copy-start(s32[1024]{0:T(1024)} %param.10) | copy-start | bytes 12292
  0.0 9.0 %copy-start.3 = (f32[2,512]{1,0:T(2,128)S(1)}, f32[2,512]{1,0:T(2,128)}, u32[]{:S(2)}) copy-start(f32[2,512]{1,0:T(2,128)} %points_ref.1) | copy-start | bytes 12292
  0.0 8.9 %collective-permute-start.1 = (s32[1024,256]{1,0:T(8,128)}, s32[1024,256]{1,0:T(8,128)}, u32[]{:S(2)}, u32[]{:S(2)}) collective-permute-start(s32[1024,256]{1,0:T(8,128)} %own_mask.1), channel_id=1, source_target_pairs={{0,1},{1,0},{2,3},{3,2},{4,5},{5,4},{6,7},{7,6},{8,9},{9,8},{10,11... | collective-permute-start | bytes 3145736 | tf_op jit(solution)/shard_map/ppermute | solution.py:296
  0.1 8.8 %collective-permute-start.2 = (f32[1024,256]{1,0:T(8,128)}, f32[1024,256]{1,0:T(8,128)}, u32[]{:S(2)}, u32[]{:S(2)}) collective-permute-start(f32[1024,256]{1,0:T(8,128)} %own_slip.1), channel_id=1, source_target_pairs={{0,1},{1,0},{2,3},{3,2},{4,5},{5,4},{6,7},{7,6},{8,9},{9,8},{10,11... | collective-permute-start | bytes 3145736 | tf_op jit(solution)/shard_map/ppermute | solution.py:296
  3.7 1.6 %collective-permute-start = (bf16[16,32,128]{2,1,0:T(8,128)(2,1)}, bf16[16,32,128]{2,1,0:T(8,128)(2,1)S(1)}, u32[]{:S(2)}, u32[]{:S(2)}) collective-permute-start(bf16[16,32,128]{2,1,0:T(8,128)(2,1)} %get-tuple-element.23), channel_id=1, source_target_pairs={{0,1},{1,0},{2,3},{3,2},{4,5},{5,4},{6,7},{7,6},{8,9},{9,8},{10,11... | collective-permute-start | bytes 393224 | tf_op jit(solution)/shard_map/ppermute | solution.py:296
  5.3 22.3 %collective-permute-start.6 = (bf16[16,64,128]{2,1,0:T(8,128)(2,1)S(1)}, bf16[16,64,128]{2,1,0:T(8,128)(2,1)S(1)}, u32[]{:S(2)}, u32[]{:S(2)}) collective-permute-start(bf16[16,64,128]{2,1,0:T(8,128)(2,1)S(1)} %constant_dynamic-update-slice_fusion.after_ref.refs_4_), channel_id=1, source_target_pairs={{0,2},{2,0},{4,6},{6,4},{8,10},{10,8},{12,14},{14,12},{1,3},{3,1},... | collective-permute-start | bytes 786440 | tf_op jit(solution)/shard_map/ppermute | solution.py:304
  6.9 20.2 %collective-permute-start.4 = (bf16[16,64,128]{2,1,0:T(8,128)(2,1)S(1)}, bf16[16,64,128]{2,1,0:T(8,128)(2,1)S(1)}, u32[]{:S(2)}, u32[]{:S(2)}) collective-permute-start(bf16[16,64,128]{2,1,0:T(8,128)(2,1)S(1)} %constant_dynamic-update-slice_fusion.after_ref.refs_4_), channel_id=1, source_target_pairs={{0,4},{2,6},{4,8},{6,10},{8,12},{10,14},{12,0},{14,2},{1,5},{3,7},... | collective-permute-start | bytes 786440 | tf_op jit(solution)/shard_map/ppermute | solution.py:300
  8.5 24.3 %collective-permute-start.7 = (bf16[16,64,128]{2,1,0:T(8,128)(2,1)S(1)}, bf16[16,64,128]{2,1,0:T(8,128)(2,1)S(1)}, u32[]{:S(2)}, u32[]{:S(2)}) collective-permute-start(bf16[16,64,128]{2,1,0:T(8,128)(2,1)S(1)} %constant_dynamic-update-slice_fusion.after_ref.refs_4_), channel_id=1, source_target_pairs={{0,12},{2,14},{4,0},{6,2},{8,4},{10,6},{12,8},{14,10},{1,13},{3,15... | collective-permute-start | bytes 786440 | tf_op jit(solution)/shard_map/ppermute | solution.py:300
  11.3 28.3 %collective-permute-start.3 = (bf16[8,64,128]{2,1,0:T(8,128)(2,1)S(1)}, bf16[8,64,128]{2,1,0:T(8,128)(2,1)S(1)}, u32[]{:S(2)}, u32[]{:S(2)}) collective-permute-start(bf16[8,64,128]{2,1,0:T(8,128)(2,1)S(1)} %gate.6.refs_5_), channel_id=1, source_target_pairs={{0,8},{2,10},{4,12},{6,14},{8,0},{10,2},{12,4},{14,6},{1,9},{3,11}... | collective-permute-start | bytes 393224 | tf_op jit(solution)/shard_map/ppermute | solution.py:300
  13.5 26.7 %collective-permute-start.10 = (bf16[8,64,128]{2,1,0:T(8,128)(2,1)S(1)}, bf16[8,64,128]{2,1,0:T(8,128)(2,1)S(1)}, u32[]{:S(2)}, u32[]{:S(2)}) collective-permute-start(bf16[8,64,128]{2,1,0:T(8,128)(2,1)S(1)} %gate.7.refs_4_), channel_id=1, source_target_pairs={{0,8},{2,10},{4,12},{6,14},{8,0},{10,2},{12,4},{14,6},{1,9},{3,11}... | collective-permute-start | bytes 393224 | tf_op jit(solution)/shard_map/ppermute | solution.py:300
  27.1 7.3 %collective-permute-start.5 = (bf16[16,64,128]{2,1,0:T(8,128)(2,1)S(1)}, bf16[16,64,128]{2,1,0:T(8,128)(2,1)S(1)}, u32[]{:S(2)}, u32[]{:S(2)}) collective-permute-start(bf16[16,64,128]{2,1,0:T(8,128)(2,1)S(1)} %gate.8.refs_7_.refs_4_), channel_id=1, source_target_pairs={{0,2},{2,0},{4,6},{6,4},{8,10},{10,8},{12,14},{14,12},{1,3},{3,1},... | collective-permute-start | bytes 786440 | tf_op jit(solution)/shard_map/ppermute | solution.py:304
  32.8 9.0 %collective-permute-start.9 = (bf16[16,64,128]{2,1,0:T(8,128)(2,1)S(1)}, bf16[16,64,128]{2,1,0:T(8,128)(2,1)S(1)}, u32[]{:S(2)}, u32[]{:S(2)}) collective-permute-start(bf16[16,64,128]{2,1,0:T(8,128)(2,1)S(1)} %gate.9.refs_8_.refs_0_), channel_id=1, source_target_pairs={{0,2},{2,0},{4,6},{6,4},{8,10},{10,8},{12,14},{14,12},{1,3},{3,1},... | collective-permute-start | bytes 786440 | tf_op jit(solution)/shard_map/ppermute | solution.py:304
  39.6 9.1 %collective-permute-start.8 = (bf16[8,64,128]{2,1,0:T(8,128)(2,1)S(1)}, bf16[8,64,128]{2,1,0:T(8,128)(2,1)S(1)}, u32[]{:S(2)}, u32[]{:S(2)}) collective-permute-start(bf16[8,64,128]{2,1,0:T(8,128)(2,1)S(1)} %gate.10.refs_5_.refs_0_), channel_id=1, source_target_pairs={{0,2},{2,0},{4,6},{6,4},{8,10},{10,8},{12,14},{14,12},{1,3},{3,1},... | collective-permute-start | bytes 393224 | tf_op jit(solution)/shard_map/ppermute | solution.py:304
  40.2 5.9 %collective-permute-start.11 = (bf16[8,64,128]{2,1,0:T(8,128)(2,1)S(1)}, bf16[8,64,128]{2,1,0:T(8,128)(2,1)S(1)}, u32[]{:S(2)}, u32[]{:S(2)}) collective-permute-start(bf16[8,64,128]{2,1,0:T(8,128)(2,1)S(1)} %gate.11.refs_4_.refs_0_), channel_id=1, source_target_pairs={{0,2},{2,0},{4,6},{6,4},{8,10},{10,8},{12,14},{14,12},{1,3},{3,1},... | collective-permute-start | bytes 393224 | tf_op jit(solution)/shard_map/ppermute | solution.py:304
  41.7 4.3 %copy-start = (f32[1024]{0:T(1024)S(1)}, f32[1024]{0:T(1024)}, u32[]{:S(2)}) copy-start(f32[1024]{0:T(1024)} %param.12) | copy-start | bytes 12292

commit v4 on v3

--- a/solution.py
+++ b/solution.py
@@ -172,37 +172,44 @@
             im, im_last = (twice * im if im_last is None else twice * im - im_last), im
 
 
-def unit_sum(k, first, pair, slips_ref):
-    half = pair[0].shape[2] // 2
+def sum_of(k, first, pairs, slip_refs):
+    half = pairs[0][0].shape[2] // 2
     lane = lax.broadcasted_iota(jnp.int32, (1, 2 * half), 1)
-    table = []
-    for ref in pair:
-        block = ref[k]
-        turned = pltpu.roll(block.astype(jnp.float32), half, 1)
-        table += [block, jnp.where(lane < half, turned, -turned).astype(jnp.bfloat16)]
-    wide = jnp.concatenate([slips_ref[first + k, block] for block in range(slips_ref.shape[1])], axis=1)
+    table, wide = [], []
+    for pair, slips_ref in zip(pairs, slip_refs):
+        for ref in pair:
+            block = ref[k]
+            turned = pltpu.roll(block.astype(jnp.float32), half, 1)
+            table += [block, jnp.where(lane < half, turned, -turned).astype(jnp.bfloat16)]
+        wide.append(jnp.concatenate([slips_ref[first + k, block] for block in range(slips_ref.shape[1])], axis=1))
     return lax.dot_general(
-        jnp.concatenate(table, axis=0), wide, (((0,), (0,)), ((), ())), preferred_element_type=jnp.float32
+        jnp.concatenate(table, axis=0),
+        jnp.concatenate(wide, axis=0),
+        (((0,), (0,)), ((), ())),
+        preferred_element_type=jnp.float32,
     )
 
 
-def work_kernel(fills, has_sum, has_total, unroll, numbers_ref, *refs):
+def work_kernel(fills, sums, has_total, unroll, numbers_ref, *refs):
     refs = list(refs)
     take = lambda n: [refs.pop(0) for _ in range(n)]
     sources = take(4) if fills else None
-    pair, (slips_ref,) = (take(2), take(1)) if has_sum else (None, (None,))
-    (total_ref,) = take(1) if has_total else (None,)
+    pairs, slip_refs = [], []
+    for _ in range(sums):
+        pairs.append(take(2))
+        slip_refs += take(1)
+    total_ref = take(1)[0] if has_total else None
     token = refs.pop()
-    (sum_ref,) = [refs.pop()] if has_sum else (None,)
+    sum_ref = refs.pop() if sums else None
     outs = refs[len(refs) - len(fills) :]
     token[...] = jnp.zeros_like(token)
 
     def body(k, carry):
+        if sums:
+            term = sum_of(k, 0, pairs, slip_refs)
+            sum_ref[k] = term + total_ref[k] if has_total else term
         for unit, out in zip(fills, outs):
             fill(out, numbers_ref, unit, k, *sources)
-        if has_sum:
-            term = unit_sum(k, 0, pair, slips_ref)
-            sum_ref[k] = term + total_ref[k] if has_total else term
         return carry
 
     lax.fori_loop(0, FREQS, body, 0, unroll=unroll)
@@ -211,32 +218,32 @@
 FREQS = 16
 
 
-def work(numbers, sources, fills, pair=None, unit_slips=None, total=None, after=()):
+def work(numbers, sources, fills, sums=(), total=None, after=(), unroll=2):
     columns, spots, own, other = sources
     variations = own.shape[1]
-    freqs = FREQS
     args, aliases = [numbers], {}
     if fills:
         args += sources
     shapes = [
-        jax.ShapeDtypeStruct((freqs, variations // BLOCK, 4 * own.shape[0] // UNITS, BLOCK), jnp.bfloat16)
+        jax.ShapeDtypeStruct((FREQS, variations // BLOCK, 4 * own.shape[0] // UNITS, BLOCK), jnp.bfloat16)
     ] * len(fills)
-    if pair is not None:
+    for pair, unit_slips in sums:
         args += [*pair, unit_slips]
+    if sums:
         if total is not None:
             aliases = {len(args): len(shapes)}
             args.append(total)
-        shapes.append(jax.ShapeDtypeStruct((freqs, pair[0].shape[2], variations), jnp.float32))
+        shapes.append(jax.ShapeDtypeStruct((FREQS, sums[0][0][0].shape[2], variations), jnp.float32))
     shapes.append(TOKEN)
     return pl.pallas_call(
-        functools.partial(work_kernel, fills, pair is not None, total is not None, 1 if len(fills) > 1 else 2),
+        functools.partial(work_kernel, fills, len(sums), total is not None, unroll),
         out_shape=tuple(shapes),
         in_specs=[SMEM] + [VMEM] * (len(args) - 1) + [ANY] * len(after),
         out_specs=(VMEM,) * len(shapes),
         input_output_aliases=aliases,
         compiler_params=SMALL,
         cost_estimate=cost(3),
-        name="work" + "".join(str(u) for u in fills) + ("_sum" if pair is not None else ""),
+        name="fill" * len(fills) + "sum" * len(sums),
     )(*args, *after)
 
 
@@ -248,7 +255,7 @@
         return pltpu.make_async_copy(buffers.at[k], out_ref.at[first + k], sems.at[k])
 
     def body(k, carry):
-        total = sums_ref[first + k] + unit_sum(k, first, pair, slips_ref)
+        total = sums_ref[first + k] + sum_of(k, first, [pair], [slips_ref])
         stations = total.shape[0] // 2
         re, im = total[:stations], total[stations:]
         pulsation = (first + k + 1).astype(jnp.float32) * (2.0 * jnp.pi * BASE_FREQ)
@@ -260,7 +267,7 @@
         copy(k).start()
         return carry
 
-    lax.fori_loop(0, count, body, 0, unroll=2)
+    lax.fori_loop(0, count, body, 0, unroll=4)
     for k in range(count):
         copy(k).wait()
 
@@ -297,7 +304,7 @@
 
 
 def along(piece, s):
-    return lax.ppermute(piece, "var", [(i, (i + 2 * s) % 8) for i in range(8)])
+    return lax.ppermute(piece, "var", [(i, i ^ (2 * s)) for i in range(8)])
 
 
 def across(piece):
@@ -334,7 +341,7 @@
         place = lax.axis_index("var")
         block = jnp.concatenate([own_part, received], axis=1)
         pieces = [block, along(block, 1), along(block, 3)]
-        numbers = jnp.stack([place % 2] + [((place - 2 * s) % 8) // 2 for s in (0, 1, 3, 2)]).astype(jnp.int32)
+        numbers = jnp.stack([place % 2] + [(place // 2) ^ s for s in (0, 1, 3, 2)]).astype(jnp.int32)
     else:
         whole = [lax.all_gather(piece, "var", axis=1, tiled=True) for piece in (own_part, received)]
         pieces = [
@@ -348,28 +355,23 @@
         fault_points, hypocenter, velocity, member_mask, slip_amount, *swapped, pieces[0]
     )
     step = functools.partial(work, numbers, (columns, spots, own, other))
+    slips_0, token = step((0,), after=(token,))
     if routed:
-        parts = [gate(block[i:j], token) for i, j in cuts]
-        last = [along(part, 2) for part in parts]
-        pairs = [(block, across(block))]
-    else:
-        parts = (token,)
-    slips_0, slips_1, token = step((0, 1), after=parts)
-    if routed:
+        last = [along(gate(block[i:j], token), 2) for i, j in cuts]
         pieces[1] = gate(pieces[1], token)
-        pairs.append((pieces[1], across(pieces[1])))
-    slips_3, total, token = step((2,), pairs[0], slips_0, after=pieces[1:2])
+        pairs = [(piece, across(piece)) for piece in pieces[:2]]
+    slips_1, slips_2, token = step((1, 2), after=pieces[1:2])
     if routed:
         pieces[2] = gate(pieces[2], token)
         pairs.append((pieces[2], across(pieces[2])))
-    slips_2, total, token = step((3,), pairs[1], slips_1, total, after=pieces[2:3])
+    slips_3, total, token = step((3,), ((pairs[0], slips_0), (pairs[1], slips_1)), after=pieces[2:3], unroll=8)
     if routed:
         last = [gate(piece, token) for piece in last]
         last = [(piece, across(piece)) for piece in last]
-    total, token = step((), pairs[2], slips_3, total, after=(last[0][0], last[1][0]))
+    total, token = step((), ((pairs[2], slips_2),), total, after=(last[0][0], last[1][0]), unroll=8)
     out = None
     for (first, _), pair in zip(cuts, last):
-        out = finish(first, rise_time, pair, slips_2, total, out)
+        out = finish(first, rise_time, pair, slips_3, total, out)
     return out
 
 

time: 51.7 us -> 45.6 us (0.88)
  the two profiles are of different devices: /device:TPU:18 before, /device:TPU:8 now
where the time goes in v4:
time: 45.6 us; the launch traced here: 45.4 us
  Pallas kernels  26.7 us (59%)
  starting transfers between devices  15.4 us (34%)
  waiting for transfers between devices  2.01 us (4%)
  local copies, waits for them, and re-layouts  1.06 us (2%)
    pallas_call x4, Pallas kernels, work(): pl.pallas_call(functools.partial(work_kernel, fills, len(sums), total is...  16.7 us
    ppermute x4, starting transfers between devices, along(): return lax.ppermute(piece, 'var', [(i, i ^ 2 * s) for i in range(8)])  10 us
    pallas_call x2, Pallas kernels, finish(): pl.pallas_call(functools.partial(finish_kernel, first, count), out_shape=...  4.96 us
    ppermute x5, starting transfers between devices, across(): return lax.ppermute(piece, 'var', [(i, i ^ 1) for i in range(8)])  4.83 us
    pallas_call x1, Pallas kernels, rotate(): pl.pallas_call(rotate_kernel, out_shape=(piece, piece), in_specs=[VMEM, S...  3.11 us
    pallas_call x1, Pallas kernels, prepare(): pl.pallas_call(prepare_kernel, out_shape=(out, out, columns, spots, TOKEN...  1.99 us
    ppermute x5, waiting for transfers between devices, across(): return lax.ppermute(piece, 'var', [(i, i ^ 1) for i in range(8)])  1.45 us
    unnamed x13, local copies, waits for them, and re-layouts  0.94 us
  transfers between devices with their start and end apart: 12, of which 2 were waited for; matrix products, arithmetic and copies ran while one was open for 2% of the time, Pallas kernels for 53%

profile of v4, /device:TPU:8, one launch (start us, length us, event | category | flops | bytes accessed | tf_op | source)
XLA Modules:
  0.0 45.4 jit_solution(4360384826457691113)
XLA Ops:
  0.0 0.1 collective-permute-start.1
  0.1 0.5 %collective-permute-start.2 = (f32[1024,256]{1,0:T(8,128)}, f32[1024,256]{1,0:T(8,128)}, u32[]{:S(2)}, u32[]{:S(2)}) collective-permute-start(f32[1024,256]{1,0:T(8,128)} %own_slip.1), channel_id=1, source_target_pairs={{0,1},{1,0},{2,3},{3,2},{4,5},{5,4},{6,7},{7,6},{8,9},{9,8},{10,11... | collective-permute-start | bytes 3145736 | tf_op jit(solution)/shard_map/ppermute | solution.py:303
  0.6 3.1 %rotate.1 = (bf16[16,32,128]{2,1,0:T(8,128)(2,1)}, bf16[16,32,128]{2,1,0:T(8,128)(2,1)}) custom-call(bf16[2,6,32,16,128]{4,3,2,1,0:T(8,128)(2,1)} %bitcast.14, f32[6,256]{1,0:T(8,128)} %tensor_ref.1, s32[1,128]{1,0:T(1,128)} %bitcast.15), custom_call_target="tpu_custom_call" | custom-call | flops 3300000000 | bytes 9000000 | tf_op jit(solution)/shard_map/rotate/pallas_call | solution.py:64
  3.7 0.0 collective-permute-start
  3.7 0.1 stack.23.numbers_ref
  3.8 0.9 %constant_dynamic-update-slice_fusion.1 = bf16[16,64,128]{2,1,0:T(8,128)(2,1)S(1)} fusion(bf16[16,32,128]{2,1,0:T(8,128)(2,1)} %get-tuple-element.21), kind=kLoop, calls=%fused_computation.1 | loop fusion | bytes 262144
  4.7 0.6 %collective-permute-done = bf16[16,32,128]{2,1,0:T(8,128)(2,1)S(1)} collective-permute-done((bf16[16,32,128]{2,1,0:T(8,128)(2,1)}, bf16[16,32,128]{2,1,0:T(8,128)(2,1)S(1)}, u32[]{:S(2)}, u32[]{:S(2)}) %collective-permute-start) | collective-permute-done | bytes 131104 | tf_op jit(solution)/shard_map/ppermute | solution.py:303
  5.3 0.1 collective-permute-start.5
  5.4 3.1 %collective-permute-start.7 = (bf16[16,64,128]{2,1,0:T(8,128)(2,1)S(1)}, bf16[16,64,128]{2,1,0:T(8,128)(2,1)S(1)}, u32[]{:S(2)}, u32[]{:S(2)}) collective-permute-start(bf16[16,64,128]{2,1,0:T(8,128)(2,1)S(1)} %constant_dynamic-update-slice_fusion.after_ref.refs_4_), channel_id=1, source_target_pairs={{0,12},{2,14},{4,8},{6,10},{8,4},{10,6},{12,0},{14,2},{1,13},{3,15... | collective-permute-start | bytes 786440 | tf_op jit(solution)/shard_map/ppermute | solution.py:307
  8.5 1.5 %collective-permute-start.4 = (bf16[16,64,128]{2,1,0:T(8,128)(2,1)S(1)}, bf16[16,64,128]{2,1,0:T(8,128)(2,1)S(1)}, u32[]{:S(2)}, u32[]{:S(2)}) collective-permute-start(bf16[16,64,128]{2,1,0:T(8,128)(2,1)S(1)} %constant_dynamic-update-slice_fusion.after_ref.refs_4_), channel_id=1, source_target_pairs={{0,2},{2,0},{4,6},{6,4},{8,10},{10,8},{12,14},{14,12},{1,3},{3,1},... | collective-permute-start | bytes 786440 | tf_op jit(solution)/shard_map/ppermute | solution.py:311
  10.1 2.0 %prepare.1 = (f32[256,1024]{1,0:T(8,128)S(1)}, f32[256,1024]{1,0:T(8,128)S(1)}, f32[2,512,128]{2,1,0:T(8,128)S(1)}, f32[8,1024]{1,0:T(8,128)S(1)}, f32[8,128]{1,0:T(8,128)S(1)}) custom-call(f32[2,512]{1,0:T(2,128)S(1)} %copy-done.3, s32[1,1024]{1,0:T(1,128)S(1)} %bitcast.12, f32[1,1024]{1,0:T(1,128)S(1)} %bitcast.13, s32[1024,256]{1,0:T(8,128)S(1)} %copy-done.1, ...), custom_call_target="tpu_custom_call" | custom-call | flops 3300000000 | bytes 9000000 | tf_op jit(solution)/shard_map/prepare/pallas_call | solution.py:121
  12.1 3.2 %fill.1 = (bf16[16,8,256,128]{3,2,1,0:T(8,128)(2,1)S(1)}, f32[8,128]{1,0:T(8,128)S(1)}) custom-call(s32[5]{0:T(128)S(1)} %stack.23.numbers_ref, f32[2,512,128]{2,1,0:T(8,128)S(1)} %get-tuple-element.23.refs_0_, f32[8,1024]{1,0:T(8,128)S(1)} %get-tuple-element.24.refs_1_, f32[256,1024]{1,0:T(8,128)S(1)} %get-tuple-element.25.refs_2_, ...), custom_call_target="tpu_custom_call" | custom-call | flops 3300000000 | bytes 9000000 | tf_op jit(solution)/shard_map/fill/pallas_call | solution.py:238
  15.4 0.6 %collective-permute-start.6 = (bf16[16,64,128]{2,1,0:T(8,128)(2,1)S(1)}, bf16[16,64,128]{2,1,0:T(8,128)(2,1)S(1)}, u32[]{:S(2)}, u32[]{:S(2)}) collective-permute-start(bf16[16,64,128]{2,1,0:T(8,128)(2,1)S(1)} %gate.7.refs_4_.refs_7_), channel_id=1, source_target_pairs={{0,2},{2,0},{4,6},{6,4},{8,10},{10,8},{12,14},{14,12},{1,3},{3,1},... | collective-permute-start | bytes 786440 | tf_op jit(solution)/shard_map/ppermute | solution.py:311
  16.0 6.8 %collective-permute-start.10 = (bf16[8,64,128]{2,1,0:T(8,128)(2,1)S(1)}, bf16[8,64,128]{2,1,0:T(8,128)(2,1)S(1)}, u32[]{:S(2)}, u32[]{:S(2)}) collective-permute-start(bf16[8,64,128]{2,1,0:T(8,128)(2,1)S(1)} %gate.10), channel_id=1, source_target_pairs={{0,8},{2,10},{4,12},{6,14},{8,0},{10,2},{12,4},{14,6},{1,9},{3,11}... | collective-permute-start | bytes 393224 | tf_op jit(solution)/shard_map/ppermute | solution.py:307
  22.8 0.0 collective-permute-start.3
  22.8 5.5 %fillfill.1 = (bf16[16,8,256,128]{3,2,1,0:T(8,128)(2,1)S(1)}, bf16[16,8,256,128]{3,2,1,0:T(8,128)(2,1)S(1)}, f32[8,128]{1,0:T(8,128)S(1)}) custom-call(s32[5]{0:T(128)S(1)} %stack.23.numbers_ref, f32[2,512,128]{2,1,0:T(8,128)S(1)} %get-tuple-element.23.refs_0_, f32[8,1024]{1,0:T(8,128)S(1)} %get-tuple-element.24.refs_1_, ...), custom_call_target="tpu_custom_call" | custom-call | flops 3300000000 | bytes 9000000 | tf_op jit(solution)/shard_map/fillfill/pallas_call | solution.py:238
  28.3 0.6 %collective-permute-start.9 = (bf16[16,64,128]{2,1,0:T(8,128)(2,1)S(1)}, bf16[16,64,128]{2,1,0:T(8,128)(2,1)S(1)}, u32[]{:S(2)}, u32[]{:S(2)}) collective-permute-start(bf16[16,64,128]{2,1,0:T(8,128)(2,1)S(1)} %gate.8.refs_10_.refs_0_), channel_id=1, source_target_pairs={{0,2},{2,0},{4,6},{6,4},{8,10},{10,8},{12,14},{14,12},{1,3},{3,1},... | collective-permute-start | bytes 786440 | tf_op jit(solution)/shard_map/ppermute | solution.py:311
  28.9 4.9 %fillsumsum.1 = (bf16[16,8,256,128]{3,2,1,0:T(8,128)(2,1)S(1)}, f32[16,128,1024]{2,1,0:T(8,128)S(1)}, f32[8,128]{1,0:T(8,128)S(1)}) custom-call(s32[5]{0:T(128)S(1)} %stack.23.numbers_ref, f32[2,512,128]{2,1,0:T(8,128)S(1)} %get-tuple-element.23.refs_0_, f32[8,1024]{1,0:T(8,128)S(1)} %get-tuple-element.24.refs_1_, ...), custom_call_target="tpu_custom_call" | custom-call | flops 3300000000 | bytes 9000000 | tf_op jit(solution)/shard_map/fillsumsum/pallas_call | solution.py:238
  33.8 1.6 %collective-permute-start.11 = (bf16[8,64,128]{2,1,0:T(8,128)(2,1)S(1)}, bf16[8,64,128]{2,1,0:T(8,128)(2,1)S(1)}, u32[]{:S(2)}, u32[]{:S(2)}) collective-permute-start(bf16[8,64,128]{2,1,0:T(8,128)(2,1)S(1)} %gate.11.refs_4_.refs_0_), channel_id=1, source_target_pairs={{0,2},{2,0},{4,6},{6,4},{8,10},{10,8},{12,14},{14,12},{1,3},{3,1},... | collective-permute-start | bytes 393224 | tf_op jit(solution)/shard_map/ppermute | solution.py:311
  35.4 0.5 %collective-permute-start.8 = (bf16[8,64,128]{2,1,0:T(8,128)(2,1)S(1)}, bf16[8,64,128]{2,1,0:T(8,128)(2,1)S(1)}, u32[]{:S(2)}, u32[]{:S(2)}) collective-permute-start(bf16[8,64,128]{2,1,0:T(8,128)(2,1)S(1)} %gate.9.refs_5_.refs_0_), channel_id=1, source_target_pairs={{0,2},{2,0},{4,6},{6,4},{8,10},{10,8},{12,14},{14,12},{1,3},{3,1},... | collective-permute-start | bytes 393224 | tf_op jit(solution)/shard_map/ppermute | solution.py:311
  35.9 1.4 %collective-permute-done.9.refs_1_ = bf16[16,64,128]{2,1,0:T(8,128)(2,1)S(1)} collective-permute-done((bf16[16,64,128]{2,1,0:T(8,128)(2,1)S(1)}, bf16[16,64,128]{2,1,0:T(8,128)(2,1)S(1)}, u32[]{:S(2)}, u32[]{:S(2)}) %collective-permute-start.9) | collective-permute-done | bytes 262176 | tf_op jit(solution)/shard_map/ppermute | solution.py:311
  37.4 3.1 %sum.1 = (f32[16,128,1024]{2,1,0:T(8,128)S(1)}, f32[8,128]{1,0:T(8,128)}) custom-call(s32[5]{0:T(128)S(1)} %stack.23.numbers_ref, bf16[16,64,128]{2,1,0:T(8,128)(2,1)S(1)} %gate.8.refs_10_.refs_0_, bf16[16,64,128]{2,1,0:T(8,128)(2,1)S(1)} %collective-permute-done.9.refs_1_, ...), custom_call_target="tpu_custom_call", output_to_operand_aliasing={{0}: (4, {})} | custom-call | flops 3300000000 | bytes 9000000 | tf_op jit(solution)/shard_map/sum/pallas_call | solution.py:238
  40.5 2.5 %finish.2.refs_4_ = f32[16,2,64,1024]{3,2,1,0:T(8,128)} custom-call(f32[1,1024]{1,0:T(1,128)S(1)} %bitcast.10, bf16[8,64,128]{2,1,0:T(8,128)(2,1)S(1)} %gate.11.refs_4_.refs_0_, bf16[8,64,128]{2,1,0:T(8,128)(2,1)S(1)} %collective-permute-done.11.refs_1_, bf16[16,8,256,128]{3,2,1,0:T(8,128)(2,1)S(1)} %get-tuple-element.33.refs_2_, ...), custom_call_target="tpu_custom_call" | custom-call | flops 2200000000 | bytes 6000000 | tf_op jit(solution)/shard_map/finish/pallas_call | solution.py:286
  43.0 2.5 %finish.3 = f32[16,2,64,1024]{3,2,1,0:T(8,128)} custom-call(f32[1,1024]{1,0:T(1,128)S(1)} %bitcast.11, bf16[8,64,128]{2,1,0:T(8,128)(2,1)S(1)} %gate.9.refs_5_.refs_0_, bf16[8,64,128]{2,1,0:T(8,128)(2,1)S(1)} %collective-permute-done.8.refs_1_, bf16[16,8,256,128]{3,2,1,0:T(8,128)(2,1)S(1)} %get-tuple-element.33.refs_2_, ...), custom_call_target="tpu_custom_call", output_to_operand_aliasing={{}: (5, {})} | custom-call | flops 2200000000 | bytes 6000000 | tf_op jit(solution)/shard_map/finish/pallas_call | solution.py:286
  (30 shorter events, 0.1 us)
Async XLA Ops:
  0.0 10.1 %copy-start.1 = (s32[1024,256]{1,0:T(8,128)S(1)}, s32[1024,256]{1,0:T(8,128)}, u32[]{:S(2)}) copy-start(s32[1024,256]{1,0:T(8,128)} %own_mask.1) | copy-start | bytes 3145732
  0.0 10.1 %copy-start.2 = (f32[1024,256]{1,0:T(8,128)S(1)}, f32[1024,256]{1,0:T(8,128)}, u32[]{:S(2)}) copy-start(f32[1024,256]{1,0:T(8,128)} %own_slip.1) | copy-start | bytes 3145732
  0.0 10.1 %copy-start.4 = (s32[1024]{0:T(1024)S(1)}, s32[1024]{0:T(1024)}, u32[]{:S(2)}) copy-start(s32[1024]{0:T(1024)} %param.10) | copy-start | bytes 12292
  0.0 10.1 %copy-start.5 = (f32[1024]{0:T(1024)S(1)}, f32[1024]{0:T(1024)}, u32[]{:S(2)}) copy-start(f32[1024]{0:T(1024)} %param.11) | copy-start | bytes 12292
  0.0 10.1 %copy-start.3 = (f32[2,512]{1,0:T(2,128)S(1)}, f32[2,512]{1,0:T(2,128)}, u32[]{:S(2)}) copy-start(f32[2,512]{1,0:T(2,128)} %points_ref.1) | copy-start | bytes 12292
  0.0 10.0 %collective-permute-start.1 = (s32[1024,256]{1,0:T(8,128)}, s32[1024,256]{1,0:T(8,128)S(1)}, u32[]{:S(2)}, u32[]{:S(2)}) collective-permute-start(s32[1024,256]{1,0:T(8,128)} %own_mask.1), channel_id=1, source_target_pairs={{0,1},{1,0},{2,3},{3,2},{4,5},{5,4},{6,7},{7,6},{8,9},{9,8},{10,11... | collective-permute-start | bytes 3145736 | tf_op jit(solution)/shard_map/ppermute | solution.py:303
  0.1 10.0 %collective-permute-start.2 = (f32[1024,256]{1,0:T(8,128)}, f32[1024,256]{1,0:T(8,128)}, u32[]{:S(2)}, u32[]{:S(2)}) collective-permute-start(f32[1024,256]{1,0:T(8,128)} %own_slip.1), channel_id=1, source_target_pairs={{0,1},{1,0},{2,3},{3,2},{4,5},{5,4},{6,7},{7,6},{8,9},{9,8},{10,11... | collective-permute-start | bytes 3145736 | tf_op jit(solution)/shard_map/ppermute | solution.py:303
  3.7 1.6 %collective-permute-start = (bf16[16,32,128]{2,1,0:T(8,128)(2,1)}, bf16[16,32,128]{2,1,0:T(8,128)(2,1)S(1)}, u32[]{:S(2)}, u32[]{:S(2)}) collective-permute-start(bf16[16,32,128]{2,1,0:T(8,128)(2,1)} %get-tuple-element.22), channel_id=1, source_target_pairs={{0,1},{1,0},{2,3},{3,2},{4,5},{5,4},{6,7},{7,6},{8,9},{9,8},{10,11... | collective-permute-start | bytes 393224 | tf_op jit(solution)/shard_map/ppermute | solution.py:303
  5.3 10.1 %collective-permute-start.5 = (bf16[16,64,128]{2,1,0:T(8,128)(2,1)S(1)}, bf16[16,64,128]{2,1,0:T(8,128)(2,1)S(1)}, u32[]{:S(2)}, u32[]{:S(2)}) collective-permute-start(bf16[16,64,128]{2,1,0:T(8,128)(2,1)S(1)} %constant_dynamic-update-slice_fusion.after_ref.refs_4_), channel_id=1, source_target_pairs={{0,4},{2,6},{4,0},{6,2},{8,12},{10,14},{12,8},{14,10},{1,5},{3,7},... | collective-permute-start | bytes 786440 | tf_op jit(solution)/shard_map/ppermute | solution.py:307
  5.4 22.9 %collective-permute-start.7 = (bf16[16,64,128]{2,1,0:T(8,128)(2,1)S(1)}, bf16[16,64,128]{2,1,0:T(8,128)(2,1)S(1)}, u32[]{:S(2)}, u32[]{:S(2)}) collective-permute-start(bf16[16,64,128]{2,1,0:T(8,128)(2,1)S(1)} %constant_dynamic-update-slice_fusion.after_ref.refs_4_), channel_id=1, source_target_pairs={{0,12},{2,14},{4,8},{6,10},{8,4},{10,6},{12,0},{14,2},{1,13},{3,15... | collective-permute-start | bytes 786440 | tf_op jit(solution)/shard_map/ppermute | solution.py:307
  8.5 20.4 %collective-permute-start.4 = (bf16[16,64,128]{2,1,0:T(8,128)(2,1)S(1)}, bf16[16,64,128]{2,1,0:T(8,128)(2,1)S(1)}, u32[]{:S(2)}, u32[]{:S(2)}) collective-permute-start(bf16[16,64,128]{2,1,0:T(8,128)(2,1)S(1)} %constant_dynamic-update-slice_fusion.after_ref.refs_4_), channel_id=1, source_target_pairs={{0,2},{2,0},{4,6},{6,4},{8,10},{10,8},{12,14},{14,12},{1,3},{3,1},... | collective-permute-start | bytes 786440 | tf_op jit(solution)/shard_map/ppermute | solution.py:311
  15.4 13.5 %collective-permute-start.6 = (bf16[16,64,128]{2,1,0:T(8,128)(2,1)S(1)}, bf16[16,64,128]{2,1,0:T(8,128)(2,1)S(1)}, u32[]{:S(2)}, u32[]{:S(2)}) collective-permute-start(bf16[16,64,128]{2,1,0:T(8,128)(2,1)S(1)} %gate.7.refs_4_.refs_7_), channel_id=1, source_target_pairs={{0,2},{2,0},{4,6},{6,4},{8,10},{10,8},{12,14},{14,12},{1,3},{3,1},... | collective-permute-start | bytes 786440 | tf_op jit(solution)/shard_map/ppermute | solution.py:311
  16.0 17.8 %collective-permute-start.10 = (bf16[8,64,128]{2,1,0:T(8,128)(2,1)S(1)}, bf16[8,64,128]{2,1,0:T(8,128)(2,1)S(1)}, u32[]{:S(2)}, u32[]{:S(2)}) collective-permute-start(bf16[8,64,128]{2,1,0:T(8,128)(2,1)S(1)} %gate.10), channel_id=1, source_target_pairs={{0,8},{2,10},{4,12},{6,14},{8,0},{10,2},{12,4},{14,6},{1,9},{3,11}... | collective-permute-start | bytes 393224 | tf_op jit(solution)/shard_map/ppermute | solution.py:307
  22.8 12.6 %collective-permute-start.3 = (bf16[8,64,128]{2,1,0:T(8,128)(2,1)S(1)}, bf16[8,64,128]{2,1,0:T(8,128)(2,1)S(1)}, u32[]{:S(2)}, u32[]{:S(2)}) collective-permute-start(bf16[8,64,128]{2,1,0:T(8,128)(2,1)S(1)} %gate.6), channel_id=1, source_target_pairs={{0,8},{2,10},{4,12},{6,14},{8,0},{10,2},{12,4},{14,6},{1,9},{3,11}... | collective-permute-start | bytes 393224 | tf_op jit(solution)/shard_map/ppermute | solution.py:307
  28.3 9.1 %collective-permute-start.9 = (bf16[16,64,128]{2,1,0:T(8,128)(2,1)S(1)}, bf16[16,64,128]{2,1,0:T(8,128)(2,1)S(1)}, u32[]{:S(2)}, u32[]{:S(2)}) collective-permute-start(bf16[16,64,128]{2,1,0:T(8,128)(2,1)S(1)} %gate.8.refs_10_.refs_0_), channel_id=1, source_target_pairs={{0,2},{2,0},{4,6},{6,4},{8,10},{10,8},{12,14},{14,12},{1,3},{3,1},... | collective-permute-start | bytes 786440 | tf_op jit(solution)/shard_map/ppermute | solution.py:311
  33.8 6.6 %collective-permute-start.11 = (bf16[8,64,128]{2,1,0:T(8,128)(2,1)S(1)}, bf16[8,64,128]{2,1,0:T(8,128)(2,1)S(1)}, u32[]{:S(2)}, u32[]{:S(2)}) collective-permute-start(bf16[8,64,128]{2,1,0:T(8,128)(2,1)S(1)} %gate.11.refs_4_.refs_0_), channel_id=1, source_target_pairs={{0,2},{2,0},{4,6},{6,4},{8,10},{10,8},{12,14},{14,12},{1,3},{3,1},... | collective-permute-start | bytes 393224 | tf_op jit(solution)/shard_map/ppermute | solution.py:311
  35.4 7.5 %collective-permute-start.8 = (bf16[8,64,128]{2,1,0:T(8,128)(2,1)S(1)}, bf16[8,64,128]{2,1,0:T(8,128)(2,1)S(1)}, u32[]{:S(2)}, u32[]{:S(2)}) collective-permute-start(bf16[8,64,128]{2,1,0:T(8,128)(2,1)S(1)} %gate.9.refs_5_.refs_0_), channel_id=1, source_target_pairs={{0,2},{2,0},{4,6},{6,4},{8,10},{10,8},{12,14},{14,12},{1,3},{3,1},... | collective-permute-start | bytes 393224 | tf_op jit(solution)/shard_map/ppermute | solution.py:311
  37.4 3.1 %copy-start = (f32[1024]{0:T(1024)S(1)}, f32[1024]{0:T(1024)}, u32[]{:S(2)}) copy-start(f32[1024]{0:T(1024)} %param.12) | copy-start | bytes 12292

commit v5 on v4

--- a/solution.py
+++ b/solution.py
@@ -22,21 +22,25 @@
     return pl.CostEstimate(flops=int(microseconds * 1.1e9), bytes_accessed=int(microseconds * 3e6), transcendentals=0)
 
 
-def rotate_kernel(green_ref, tensor_ref, ids_ref, own_ref, other_ref, sums, rows):
-    _, comps, count, freqs, stations = green_ref.shape
+def rotate_kernel(green_hbm, tensor_hbm, ids_hbm, own_ref, other_ref, green, tensor_ref, ids_ref, sums, rows, sems, few):
+    _, comps, count, freqs, stations = green.shape
     half = stations // 2
     first = lax.axis_index("var") * count
 
-    def one_subfault(m, carry):
-        for part in range(2):
-            total = green_ref[part, 0, m].astype(jnp.float32) * tensor_ref[0, first + m]
-            for comp in range(1, comps):
-                total = total + green_ref[part, comp, m].astype(jnp.float32) * tensor_ref[comp, first + m]
-            at = pl.ds(pl.multiple_of(m * freqs, freqs), freqs)
-            sums[at, part * stations : (part + 1) * stations] = total.astype(jnp.bfloat16)
-        return carry
-
-    lax.fori_loop(0, count, one_subfault, 0, unroll=4)
+    def load(part, comp):
+        return pltpu.make_async_copy(green_hbm.at[part, comp], green.at[part, comp], sems.at[part, comp])
+
+    small = [
+        pltpu.make_async_copy(ids_hbm, ids_ref, few.at[0]),
+        pltpu.make_async_copy(tensor_hbm, tensor_ref, few.at[1]),
+    ]
+    for copy in small:
+        copy.start()
+    for part in range(2):
+        for comp in range(comps):
+            load(part, comp).start()
+    for copy in small:
+        copy.wait()
 
     lane = lax.broadcasted_iota(jnp.int32, (1, stations), 1)
     ids = ids_ref[...]
@@ -49,6 +53,20 @@
     column = lax.broadcasted_iota(jnp.int32, (2 * stations, 2 * stations), 1)
     part_of_column = (column // half) % 2
     picks = (row == wanted + part_of_column * stations).astype(jnp.float32).astype(jnp.bfloat16)
+
+    for part in range(2):
+        for comp in range(comps):
+            load(part, comp).wait()
+
+        def one_subfault(m, carry, part=part):
+            total = green[part, 0, m].astype(jnp.float32) * tensor_ref[0, first + m]
+            for comp in range(1, comps):
+                total = total + green[part, comp, m].astype(jnp.float32) * tensor_ref[comp, first + m]
+            at = pl.ds(pl.multiple_of(m * freqs, freqs), freqs)
+            sums[at, part * stations : (part + 1) * stations] = total.astype(jnp.bfloat16)
+            return carry
+
+        lax.fori_loop(0, count, one_subfault, 0, unroll=8)
     picked = jnp.dot(sums[...], picks, preferred_element_type=jnp.float32)
     rows[0] = picked[:, :stations]
     rows[1] = picked[:, stations:]
@@ -64,11 +82,16 @@
     return pl.pallas_call(
         rotate_kernel,
         out_shape=(piece, piece),
-        in_specs=[VMEM, SMEM, VMEM],
+        in_specs=[ANY] * 3,
         out_specs=(VMEM, VMEM),
         scratch_shapes=[
+            pltpu.VMEM(green.shape, jnp.bfloat16),
+            pltpu.SMEM(tensor.shape, jnp.float32),
+            pltpu.VMEM((1, stations), jnp.int32),
             pltpu.VMEM((count * freqs, 2 * stations), jnp.bfloat16),
             pltpu.VMEM((2, count * freqs, stations), jnp.float32),
+            pltpu.SemaphoreType.DMA(green.shape[:2]),
+            pltpu.SemaphoreType.DMA((2,)),
         ],
         compiler_params=ROOMY,
         cost_estimate=cost(3),
@@ -172,7 +195,7 @@
             im, im_last = (twice * im if im_last is None else twice * im - im_last), im
 
 
-def sum_of(k, first, pairs, slip_refs):
+def sum_of(k, pairs, slip_refs):
     half = pairs[0][0].shape[2] // 2
     lane = lax.broadcasted_iota(jnp.int32, (1, 2 * half), 1)
     table, wide = [], []
@@ -181,7 +204,7 @@
             block = ref[k]
             turned = pltpu.roll(block.astype(jnp.float32), half, 1)
             table += [block, jnp.where(lane < half, turned, -turned).astype(jnp.bfloat16)]
-        wide.append(jnp.concatenate([slips_ref[first + k, block] for block in range(slips_ref.shape[1])], axis=1))
+        wide.append(jnp.concatenate([slips_ref[k, block] for block in range(slips_ref.shape[1])], axis=1))
     return lax.dot_general(
         jnp.concatenate(table, axis=0),
         jnp.concatenate(wide, axis=0),
@@ -206,8 +229,11 @@
 
     def body(k, carry):
         if sums:
-            term = sum_of(k, 0, pairs, slip_refs)
-            sum_ref[k] = term + total_ref[k] if has_total else term
+            term = sum_of(k, pairs, slip_refs)
+            stations = term.shape[0] // 2
+            for part in range(2):
+                piece = term[part * stations : (part + 1) * stations]
+                sum_ref[k, part] = piece + total_ref[k, part] if has_total else piece
         for unit, out in zip(fills, outs):
             fill(out, numbers_ref, unit, k, *sources)
         return carry
@@ -233,7 +259,7 @@
         if total is not None:
             aliases = {len(args): len(shapes)}
             args.append(total)
-        shapes.append(jax.ShapeDtypeStruct((FREQS, sums[0][0][0].shape[2], variations), jnp.float32))
+        shapes.append(jax.ShapeDtypeStruct((FREQS, 2, sums[0][0][0].shape[2] // 2, variations), jnp.float32))
     shapes.append(TOKEN)
     return pl.pallas_call(
         functools.partial(work_kernel, fills, len(sums), total is not None, unroll),
@@ -247,68 +273,62 @@
     )(*args, *after)
 
 
-def finish_kernel(first, count, rise_ref, *refs):
-    pair, slips_ref, sums_ref = refs[:2], refs[2], refs[3]
-    out_ref, buffers, sems = refs[-3:]
+def finish_kernel(sums, unroll, rise_ref, *refs):
+    pairs = [refs[3 * i : 3 * i + 2] for i in range(sums)]
+    slip_refs = [refs[3 * i + 2] for i in range(sums)]
+    total_ref = refs[3 * sums]
+    out_ref, held, sems = refs[-3:]
 
     def copy(k):
-        return pltpu.make_async_copy(buffers.at[k], out_ref.at[first + k], sems.at[k])
+        return pltpu.make_async_copy(held.at[k], out_ref.at[k], sems.at[k])
 
     def body(k, carry):
-        total = sums_ref[first + k] + sum_of(k, first, [pair], [slips_ref])
-        stations = total.shape[0] // 2
-        re, im = total[:stations], total[stations:]
-        pulsation = (first + k + 1).astype(jnp.float32) * (2.0 * jnp.pi * BASE_FREQ)
+        term = sum_of(k, pairs, slip_refs)
+        stations = term.shape[0] // 2
+        re, im = term[:stations] + total_ref[k, 0], term[stations:] + total_ref[k, 1]
+        pulsation = (k + 1).astype(jnp.float32) * (2.0 * jnp.pi * BASE_FREQ)
         damping = pulsation * rise_ref[...]
         scale = 1.0 / (1.0 + damping * damping)
         tilt = scale * damping
-        buffers[k, 0] = scale * re + tilt * im
-        buffers[k, 1] = scale * im - tilt * re
+        held[k, 0] = scale * re + tilt * im
+        held[k, 1] = scale * im - tilt * re
         copy(k).start()
         return carry
 
-    lax.fori_loop(0, count, body, 0, unroll=4)
-    for k in range(count):
+    lax.fori_loop(0, FREQS, body, 0, unroll=unroll)
+
+    def drain(k, carry):
         copy(k).wait()
-
-
-def finish(first, rise_time, pair, unit_slips, sums, so_far):
-    count, _, lanes = pair[0].shape
-    stations = lanes // 2
-    total, _, variations = sums.shape
-    args = [rise_time[None, :], *pair, unit_slips, sums]
-    specs = [VMEM] * len(args)
-    aliases = {}
-    if so_far is not None:
-        aliases = {len(args): 0}
-        args.append(so_far)
-        specs.append(ANY)
+        return carry
+
+    lax.fori_loop(0, FREQS, drain, 0)
+
+
+def finish(rise_time, sums, total, unroll=4):
+    args = [rise_time[None, :]]
+    for pair, unit_slips in sums:
+        args += [*pair, unit_slips]
+    args.append(total)
+    shape = jax.ShapeDtypeStruct(total.shape, jnp.float32)
     return pl.pallas_call(
-        functools.partial(finish_kernel, first, count),
-        out_shape=jax.ShapeDtypeStruct((total, 2, stations, variations), jnp.float32),
-        in_specs=specs,
-        out_specs=ANY,
-        scratch_shapes=[
-            pltpu.VMEM((count, 2, stations, variations), jnp.float32),
-            pltpu.SemaphoreType.DMA((count,)),
-        ],
-        input_output_aliases=aliases,
+        functools.partial(finish_kernel, len(sums), unroll),
+        out_shape=(shape, shape),
+        in_specs=[VMEM] * len(args),
+        out_specs=(ANY, VMEM),
+        scratch_shapes=[pltpu.SemaphoreType.DMA((FREQS,))],
+        input_output_aliases={len(args) - 1: 1},
         compiler_params=SMALL,
-        cost_estimate=cost(2),
+        cost_estimate=cost(4),
         name="finish",
-    )(*args)
+    )(*args)[0]
 
 
 def swap(array, axis):
     return lax.ppermute(array, axis, [(0, 1), (1, 0)])
 
 
-def along(piece, s):
-    return lax.ppermute(piece, "var", [(i, i ^ (2 * s)) for i in range(8)])
-
-
-def across(piece):
-    return lax.ppermute(piece, "var", [(i, i ^ 1) for i in range(8)])
+def exchange(piece, bits):
+    return lax.ppermute(piece, "var", [(i, i ^ bits) for i in range(2 * UNITS)])
 
 
 def gate_kernel(array_ref, token_ref, out_ref):
@@ -331,8 +351,6 @@
     freqs = strain_green.shape[4]
     half = moment_tensor.shape[1]
     rows = half // (2 * UNITS)
-    groups = (freqs // 2, freqs - freqs // 2)
-    cuts = ((0, groups[0]), (groups[0], freqs))
     swapped = [swap(array, "sub") for array in (member_mask, slip_amount)]
     own_part, other_part = rotate(strain_green[:, :, 0], moment_tensor, station_ids)
     received = swap(other_part, "sub")
@@ -340,7 +358,7 @@
     if routed:
         place = lax.axis_index("var")
         block = jnp.concatenate([own_part, received], axis=1)
-        pieces = [block, along(block, 1), along(block, 3)]
+        pieces = [block, exchange(block, 2), exchange(block, 6)]
         numbers = jnp.stack([place % 2] + [(place // 2) ^ s for s in (0, 1, 3, 2)]).astype(jnp.int32)
     else:
         whole = [lax.all_gather(piece, "var", axis=1, tiled=True) for piece in (own_part, received)]
@@ -348,7 +366,6 @@
             jnp.concatenate([part[:, i * rows : (i + 1) * rows] for part in whole], axis=1) for i in range(2 * UNITS)
         ]
         pairs = [(pieces[2 * i], pieces[2 * i + 1]) for i in range(UNITS)]
-        last = [tuple(piece[i:j] for piece in pairs[-1]) for i, j in cuts]
         numbers = jnp.arange(-1, UNITS, dtype=jnp.int32) * (jnp.arange(1 + UNITS, dtype=jnp.int32) > 0)
 
     own, other, columns, spots, token = prepare(
@@ -357,22 +374,16 @@
     step = functools.partial(work, numbers, (columns, spots, own, other))
     slips_0, token = step((0,), after=(token,))
     if routed:
-        last = [along(gate(block[i:j], token), 2) for i, j in cuts]
         pieces[1] = gate(pieces[1], token)
-        pairs = [(piece, across(piece)) for piece in pieces[:2]]
-    slips_1, slips_2, token = step((1, 2), after=pieces[1:2])
+        pairs = [(piece, exchange(piece, 1)) for piece in pieces[:2]]
+    slips_1, token = step((1,), after=pieces[1:2])
     if routed:
         pieces[2] = gate(pieces[2], token)
-        pairs.append((pieces[2], across(pieces[2])))
-    slips_3, total, token = step((3,), ((pairs[0], slips_0), (pairs[1], slips_1)), after=pieces[2:3], unroll=8)
-    if routed:
-        last = [gate(piece, token) for piece in last]
-        last = [(piece, across(piece)) for piece in last]
-    total, token = step((), ((pairs[2], slips_2),), total, after=(last[0][0], last[1][0]), unroll=8)
-    out = None
-    for (first, _), pair in zip(cuts, last):
-        out = finish(first, rise_time, pair, slips_3, total, out)
-    return out
+        pairs.append((pieces[2], exchange(pieces[2], 1)))
+        pairs.append((exchange(pieces[2], 2), exchange(pieces[2], 3)))
+    slips_2, token = step((2,), after=pieces[2:3])
+    slips_3, total, token = step((3,), ((pairs[0], slips_0), (pairs[1], slips_1)), after=(token,), unroll=8)
+    return finish(rise_time, ((pairs[2], slips_2), (pairs[3], slips_3)), total, unroll=8)
 
 
 def solution(mesh):

time: 45.6 us -> 42.5 us (0.932)
  the two profiles are of different devices: /device:TPU:8 before, /device:TPU:0 now
where the time goes in v5:
time: 42.5 us; the launch traced here: 42.3 us
  Pallas kernels  25.4 us (60%)
  starting transfers between devices  12.2 us (29%)
  waiting for transfers between devices  3.61 us (8%)
  local copies, waits for them, and re-layouts  1.04 us (2%)
    pallas_call x4, Pallas kernels, work(): pl.pallas_call(functools.partial(work_kernel, fills, len(sums), total is...  14.9 us
    ppermute x7, starting transfers between devices, exchange(): return lax.ppermute(piece, 'var', [(i, i ^ bits) for i in range(2 * UNITS)])  11.1 us
    pallas_call x1, Pallas kernels, finish(): pl.pallas_call(functools.partial(finish_kernel, len(sums), unroll), out_s...  5.15 us
    ppermute x7, waiting for transfers between devices, exchange(): return lax.ppermute(piece, 'var', [(i, i ^ bits) for i in range(2 * UNITS)])  3.4 us
    pallas_call x1, Pallas kernels, rotate(): pl.pallas_call(rotate_kernel, out_shape=(piece, piece), in_specs=[ANY] *...  3.01 us
    pallas_call x1, Pallas kernels, prepare(): pl.pallas_call(prepare_kernel, out_shape=(out, out, columns, spots, TOKEN...  2.3 us
    ppermute x3, starting transfers between devices, swap(): return lax.ppermute(array, axis, [(0, 1), (1, 0)])  1.12 us
    unnamed x13, local copies, waits for them, and re-layouts  0.94 us
  transfers between devices with their start and end apart: 10, of which 3 were waited for; matrix products, arithmetic and copies ran while one was open for 2% of the time, Pallas kernels for 48%

profile of v5, /device:TPU:0, one launch (start us, length us, event | category | flops | bytes accessed | tf_op | source)
XLA Modules:
  0.0 42.3 jit_solution(9973718288917046974)
XLA Ops:
  0.0 0.5 %collective-permute-start.2 = (s32[1024,256]{1,0:T(8,128)}, s32[1024,256]{1,0:T(8,128)}, u32[]{:S(2)}, u32[]{:S(2)}) collective-permute-start(s32[1024,256]{1,0:T(8,128)} %own_mask.1), channel_id=1, source_target_pairs={{0,1},{1,0},{2,3},{3,2},{4,5},{5,4},{6,7},{7,6},{8,9},{9,8},{10,11... | collective-permute-start | bytes 3145736 | tf_op jit(solution)/shard_map/ppermute | solution.py:327
  0.5 0.1 collective-permute-start.3
  0.6 3.0 %rotate.1 = (bf16[16,32,128]{2,1,0:T(8,128)(2,1)}, bf16[16,32,128]{2,1,0:T(8,128)(2,1)}) custom-call(bf16[2,6,32,16,128]{4,3,2,1,0:T(8,128)(2,1)} %bitcast.13, f32[6,256]{1,0:T(8,128)} %tensor_hbm.1, s32[1,128]{1,0:T(1,128)} %bitcast.14), custom_call_target="tpu_custom_call" | custom-call | flops 3300000000 | bytes 9000000 | tf_op jit(solution)/shard_map/rotate/pallas_call | solution.py:82
  3.6 0.5 %collective-permute-start = (bf16[16,32,128]{2,1,0:T(8,128)(2,1)}, bf16[16,32,128]{2,1,0:T(8,128)(2,1)S(1)}, u32[]{:S(2)}, u32[]{:S(2)}) collective-permute-start(bf16[16,32,128]{2,1,0:T(8,128)(2,1)} %get-tuple-element.22), channel_id=1, source_target_pairs={{0,1},{1,0},{2,3},{3,2},{4,5},{5,4},{6,7},{7,6},{8,9},{9,8},{10,11... | collective-permute-start | bytes 393224 | tf_op jit(solution)/shard_map/ppermute | solution.py:327
  4.2 0.1 stack.23.numbers_ref
  4.2 0.9 %constant_dynamic-update-slice_fusion.1 = bf16[16,64,128]{2,1,0:T(8,128)(2,1)S(1)} fusion(bf16[16,32,128]{2,1,0:T(8,128)(2,1)} %get-tuple-element.21), kind=kLoop, calls=%fused_computation.1 | loop fusion | bytes 262144
  5.2 0.2 collective-permute-done
  5.4 3.0 %collective-permute-start.4 = (bf16[16,64,128]{2,1,0:T(8,128)(2,1)S(1)}, bf16[16,64,128]{2,1,0:T(8,128)(2,1)S(1)}, u32[]{:S(2)}, u32[]{:S(2)}) collective-permute-start(bf16[16,64,128]{2,1,0:T(8,128)(2,1)S(1)} %constant_dynamic-update-slice_fusion.after_ref.refs_4_), channel_id=1, source_target_pairs={{0,4},{2,6},{4,0},{6,2},{8,12},{10,14},{12,8},{14,10},{1,5},{3,7},... | collective-permute-start | bytes 786440 | tf_op jit(solution)/shard_map/ppermute | solution.py:331
  8.4 2.5 %collective-permute-start.1 = (bf16[16,64,128]{2,1,0:T(8,128)(2,1)S(1)}, bf16[16,64,128]{2,1,0:T(8,128)(2,1)S(1)}, u32[]{:S(2)}, u32[]{:S(2)}) collective-permute-start(bf16[16,64,128]{2,1,0:T(8,128)(2,1)S(1)} %constant_dynamic-update-slice_fusion.after_ref.refs_4_), channel_id=1, source_target_pairs={{0,12},{2,14},{4,8},{6,10},{8,4},{10,6},{12,0},{14,2},{1,13},{3,15... | collective-permute-start | bytes 786440 | tf_op jit(solution)/shard_map/ppermute | solution.py:331
  10.9 1.5 %collective-permute-start.8 = (bf16[16,64,128]{2,1,0:T(8,128)(2,1)S(1)}, bf16[16,64,128]{2,1,0:T(8,128)(2,1)S(1)}, u32[]{:S(2)}, u32[]{:S(2)}) collective-permute-start(bf16[16,64,128]{2,1,0:T(8,128)(2,1)S(1)} %constant_dynamic-update-slice_fusion.after_ref.refs_4_), channel_id=1, source_target_pairs={{0,2},{2,0},{4,6},{6,4},{8,10},{10,8},{12,14},{14,12},{1,3},{3,1},... | collective-permute-start | bytes 786440 | tf_op jit(solution)/shard_map/ppermute | solution.py:331
  12.4 2.3 %prepare.1 = (f32[256,1024]{1,0:T(8,128)S(1)}, f32[256,1024]{1,0:T(8,128)S(1)}, f32[2,512,128]{2,1,0:T(8,128)S(1)}, f32[8,1024]{1,0:T(8,128)S(1)}, f32[8,128]{1,0:T(8,128)S(1)}) custom-call(f32[2,512]{1,0:T(2,128)S(1)} %copy-done.3, s32[1,1024]{1,0:T(1,128)S(1)} %bitcast.11, f32[1,1024]{1,0:T(1,128)S(1)} %bitcast.12, s32[1024,256]{1,0:T(8,128)S(1)} %copy-done.1, ...), custom_call_target="tpu_custom_call" | custom-call | flops 3300000000 | bytes 9000000 | tf_op jit(solution)/shard_map/prepare/pallas_call | solution.py:144
  14.7 3.2 %fill.3 = (bf16[16,8,256,128]{3,2,1,0:T(8,128)(2,1)S(1)}, f32[8,128]{1,0:T(8,128)S(1)}) custom-call(s32[5]{0:T(128)S(1)} %stack.23.numbers_ref, f32[2,512,128]{2,1,0:T(8,128)S(1)} %get-tuple-element.23.refs_0_, f32[8,1024]{1,0:T(8,128)S(1)} %get-tuple-element.24.refs_1_, f32[256,1024]{1,0:T(8,128)S(1)} %get-tuple-element.25.refs_2_, ...), custom_call_target="tpu_custom_call" | custom-call | flops 3300000000 | bytes 9000000 | tf_op jit(solution)/shard_map/fill/pallas_call | solution.py:264
  18.0 0.6 %collective-permute-start.9 = (bf16[16,64,128]{2,1,0:T(8,128)(2,1)S(1)}, bf16[16,64,128]{2,1,0:T(8,128)(2,1)S(1)}, u32[]{:S(2)}, u32[]{:S(2)}) collective-permute-start(bf16[16,64,128]{2,1,0:T(8,128)(2,1)S(1)} %gate.2.refs_4_.refs_7_), channel_id=1, source_target_pairs={{0,2},{2,0},{4,6},{6,4},{8,10},{10,8},{12,14},{14,12},{1,3},{3,1},... | collective-permute-start | bytes 786440 | tf_op jit(solution)/shard_map/ppermute | solution.py:331
  18.6 3.2 %fill.4 = (bf16[16,8,256,128]{3,2,1,0:T(8,128)(2,1)S(1)}, f32[8,128]{1,0:T(8,128)S(1)}) custom-call(s32[5]{0:T(128)S(1)} %stack.23.numbers_ref, f32[2,512,128]{2,1,0:T(8,128)S(1)} %get-tuple-element.23.refs_0_, f32[8,1024]{1,0:T(8,128)S(1)} %get-tuple-element.24.refs_1_, f32[256,1024]{1,0:T(8,128)S(1)} %get-tuple-element.25.refs_2_, ...), custom_call_target="tpu_custom_call" | custom-call | flops 3300000000 | bytes 9000000 | tf_op jit(solution)/shard_map/fill/pallas_call | solution.py:264
  21.8 1.1 %collective-permute-done.1.array_ref = bf16[16,64,128]{2,1,0:T(8,128)(2,1)S(1)} collective-permute-done((bf16[16,64,128]{2,1,0:T(8,128)(2,1)S(1)}, bf16[16,64,128]{2,1,0:T(8,128)(2,1)S(1)}, u32[]{:S(2)}, u32[]{:S(2)}) %collective-permute-start.1) | collective-permute-done | bytes 262176 | tf_op jit(solution)/shard_map/ppermute | solution.py:331
  22.9 1.5 %collective-permute-start.5 = (bf16[16,64,128]{2,1,0:T(8,128)(2,1)S(1)}, bf16[16,64,128]{2,1,0:T(8,128)(2,1)S(1)}, u32[]{:S(2)}, u32[]{:S(2)}) collective-permute-start(bf16[16,64,128]{2,1,0:T(8,128)(2,1)S(1)} %gate.3.refs_4_.refs_0_), channel_id=1, source_target_pairs={{0,2},{2,0},{4,6},{6,4},{8,10},{10,8},{12,14},{14,12},{1,3},{3,1},... | collective-permute-start | bytes 786440 | tf_op jit(solution)/shard_map/ppermute | solution.py:331
  24.4 0.6 %collective-permute-start.6 = (bf16[16,64,128]{2,1,0:T(8,128)(2,1)S(1)}, bf16[16,64,128]{2,1,0:T(8,128)(2,1)S(1)}, u32[]{:S(2)}, u32[]{:S(2)}) collective-permute-start(bf16[16,64,128]{2,1,0:T(8,128)(2,1)S(1)} %gate.3.refs_4_.refs_0_), channel_id=1, source_target_pairs={{0,4},{2,6},{4,0},{6,2},{8,12},{10,14},{12,8},{14,10},{1,5},{3,7},... | collective-permute-start | bytes 786440 | tf_op jit(solution)/shard_map/ppermute | solution.py:331
  25.0 1.4 %collective-permute-start.7 = (bf16[16,64,128]{2,1,0:T(8,128)(2,1)S(1)}, bf16[16,64,128]{2,1,0:T(8,128)(2,1)S(1)}, u32[]{:S(2)}, u32[]{:S(2)}) collective-permute-start(bf16[16,64,128]{2,1,0:T(8,128)(2,1)S(1)} %gate.3.refs_4_.refs_0_), channel_id=1, source_target_pairs={{0,6},{2,4},{4,2},{6,0},{8,14},{10,12},{12,10},{14,8},{1,7},{3,5},... | collective-permute-start | bytes 786440 | tf_op jit(solution)/shard_map/ppermute | solution.py:331
  26.4 3.2 %fill.5 = (bf16[16,8,256,128]{3,2,1,0:T(8,128)(2,1)S(1)}, f32[8,128]{1,0:T(8,128)S(1)}) custom-call(s32[5]{0:T(128)S(1)} %stack.23.numbers_ref, f32[2,512,128]{2,1,0:T(8,128)S(1)} %get-tuple-element.23.refs_0_, f32[8,1024]{1,0:T(8,128)S(1)} %get-tuple-element.24.refs_1_, f32[256,1024]{1,0:T(8,128)S(1)} %get-tuple-element.25.refs_2_, ...), custom_call_target="tpu_custom_call" | custom-call | flops 3300000000 | bytes 9000000 | tf_op jit(solution)/shard_map/fill/pallas_call | solution.py:264
  29.6 0.0 collective-permute-done.8.refs_5_
  29.7 0.0 copy-start
  29.7 5.2 %fillsumsum.1 = (bf16[16,8,256,128]{3,2,1,0:T(8,128)(2,1)S(1)}, f32[16,2,64,1024]{3,2,1,0:T(8,128)S(1)}, f32[8,128]{1,0:T(8,128)}) custom-call(s32[5]{0:T(128)S(1)} %stack.23.numbers_ref, f32[2,512,128]{2,1,0:T(8,128)S(1)} %get-tuple-element.23.refs_0_, f32[8,1024]{1,0:T(8,128)S(1)} %get-tuple-element.24.refs_1_, f32[256,1024]{1,0:T(8,128)S(1)} %get-tuple-element.25.refs_2_, ...), custom_call_target="tpu_custom_call" | custom-call | flops 3300000000 | bytes 9000000 | tf_op jit(solution)/shard_map/fillsumsum/pallas_call | solution.py:264
  34.9 2.3 %collective-permute-done.7.refs_4_ = bf16[16,64,128]{2,1,0:T(8,128)(2,1)S(1)} collective-permute-done((bf16[16,64,128]{2,1,0:T(8,128)(2,1)S(1)}, bf16[16,64,128]{2,1,0:T(8,128)(2,1)S(1)}, u32[]{:S(2)}, u32[]{:S(2)}) %collective-permute-start.7) | collective-permute-done | bytes 262176 | tf_op jit(solution)/shard_map/ppermute | solution.py:331
  37.2 5.2 %finish.1 = (f32[16,2,64,1024]{3,2,1,0:T(8,128)}, f32[16,2,64,1024]{3,2,1,0:T(8,128)S(1)}) custom-call(f32[1,1024]{1,0:T(1,128)S(1)} %bitcast.10, bf16[16,64,128]{2,1,0:T(8,128)(2,1)S(1)} %gate.3.refs_4_.refs_0_, bf16[16,64,128]{2,1,0:T(8,128)(2,1)S(1)} %collective-permute-done.5.refs_1_, ...), custom_call_target="tpu_custom_call", output_to_operand_aliasing={{1}: (7, {})} | custom-call | flops 4400000000 | bytes 12000000 | tf_op jit(solution)/shard_map/finish/pallas_call | solution.py:313
  (20 shorter events, 0.1 us)
Async XLA Ops:
  0.0 12.4 %copy-start.1 = (s32[1024,256]{1,0:T(8,128)S(1)}, s32[1024,256]{1,0:T(8,128)}, u32[]{:S(2)}) copy-start(s32[1024,256]{1,0:T(8,128)} %own_mask.1) | copy-start | bytes 3145732
  0.0 12.4 %copy-start.2 = (f32[1024,256]{1,0:T(8,128)S(1)}, f32[1024,256]{1,0:T(8,128)}, u32[]{:S(2)}) copy-start(f32[1024,256]{1,0:T(8,128)} %own_slip.1) | copy-start | bytes 3145732
  0.0 12.4 %copy-start.4 = (s32[1024]{0:T(1024)S(1)}, s32[1024]{0:T(1024)}, u32[]{:S(2)}) copy-start(s32[1024]{0:T(1024)} %param.10) | copy-start | bytes 12292
  0.0 12.4 %copy-start.5 = (f32[1024]{0:T(1024)S(1)}, f32[1024]{0:T(1024)}, u32[]{:S(2)}) copy-start(f32[1024]{0:T(1024)} %param.11) | copy-start | bytes 12292
  0.0 12.4 %copy-start.3 = (f32[2,512]{1,0:T(2,128)S(1)}, f32[2,512]{1,0:T(2,128)}, u32[]{:S(2)}) copy-start(f32[2,512]{1,0:T(2,128)} %points_ref.1) | copy-start | bytes 12292
  0.0 12.4 %collective-permute-start.2 = (s32[1024,256]{1,0:T(8,128)}, s32[1024,256]{1,0:T(8,128)}, u32[]{:S(2)}, u32[]{:S(2)}) collective-permute-start(s32[1024,256]{1,0:T(8,128)} %own_mask.1), channel_id=1, source_target_pairs={{0,1},{1,0},{2,3},{3,2},{4,5},{5,4},{6,7},{7,6},{8,9},{9,8},{10,11... | collective-permute-start | bytes 3145736 | tf_op jit(solution)/shard_map/ppermute | solution.py:327
  0.5 11.8 %collective-permute-start.3 = (f32[1024,256]{1,0:T(8,128)}, f32[1024,256]{1,0:T(8,128)}, u32[]{:S(2)}, u32[]{:S(2)}) collective-permute-start(f32[1024,256]{1,0:T(8,128)} %own_slip.1), channel_id=1, source_target_pairs={{0,1},{1,0},{2,3},{3,2},{4,5},{5,4},{6,7},{7,6},{8,9},{9,8},{10,11... | collective-permute-start | bytes 3145736 | tf_op jit(solution)/shard_map/ppermute | solution.py:327
  3.6 1.7 %collective-permute-start = (bf16[16,32,128]{2,1,0:T(8,128)(2,1)}, bf16[16,32,128]{2,1,0:T(8,128)(2,1)S(1)}, u32[]{:S(2)}, u32[]{:S(2)}) collective-permute-start(bf16[16,32,128]{2,1,0:T(8,128)(2,1)} %get-tuple-element.22), channel_id=1, source_target_pairs={{0,1},{1,0},{2,3},{3,2},{4,5},{5,4},{6,7},{7,6},{8,9},{9,8},{10,11... | collective-permute-start | bytes 393224 | tf_op jit(solution)/shard_map/ppermute | solution.py:327
  5.4 12.6 %collective-permute-start.4 = (bf16[16,64,128]{2,1,0:T(8,128)(2,1)S(1)}, bf16[16,64,128]{2,1,0:T(8,128)(2,1)S(1)}, u32[]{:S(2)}, u32[]{:S(2)}) collective-permute-start(bf16[16,64,128]{2,1,0:T(8,128)(2,1)S(1)} %constant_dynamic-update-slice_fusion.after_ref.refs_4_), channel_id=1, source_target_pairs={{0,4},{2,6},{4,0},{6,2},{8,12},{10,14},{12,8},{14,10},{1,5},{3,7},... | collective-permute-start | bytes 786440 | tf_op jit(solution)/shard_map/ppermute | solution.py:331
  8.4 14.5 %collective-permute-start.1 = (bf16[16,64,128]{2,1,0:T(8,128)(2,1)S(1)}, bf16[16,64,128]{2,1,0:T(8,128)(2,1)S(1)}, u32[]{:S(2)}, u32[]{:S(2)}) collective-permute-start(bf16[16,64,128]{2,1,0:T(8,128)(2,1)S(1)} %constant_dynamic-update-slice_fusion.after_ref.refs_4_), channel_id=1, source_target_pairs={{0,12},{2,14},{4,8},{6,10},{8,4},{10,6},{12,0},{14,2},{1,13},{3,15... | collective-permute-start | bytes 786440 | tf_op jit(solution)/shard_map/ppermute | solution.py:331
  10.9 18.8 %collective-permute-start.8 = (bf16[16,64,128]{2,1,0:T(8,128)(2,1)S(1)}, bf16[16,64,128]{2,1,0:T(8,128)(2,1)S(1)}, u32[]{:S(2)}, u32[]{:S(2)}) collective-permute-start(bf16[16,64,128]{2,1,0:T(8,128)(2,1)S(1)} %constant_dynamic-update-slice_fusion.after_ref.refs_4_), channel_id=1, source_target_pairs={{0,2},{2,0},{4,6},{6,4},{8,10},{10,8},{12,14},{14,12},{1,3},{3,1},... | collective-permute-start | bytes 786440 | tf_op jit(solution)/shard_map/ppermute | solution.py:331
  18.0 11.6 %collective-permute-start.9 = (bf16[16,64,128]{2,1,0:T(8,128)(2,1)S(1)}, bf16[16,64,128]{2,1,0:T(8,128)(2,1)S(1)}, u32[]{:S(2)}, u32[]{:S(2)}) collective-permute-start(bf16[16,64,128]{2,1,0:T(8,128)(2,1)S(1)} %gate.2.refs_4_.refs_7_), channel_id=1, source_target_pairs={{0,2},{2,0},{4,6},{6,4},{8,10},{10,8},{12,14},{14,12},{1,3},{3,1},... | collective-permute-start | bytes 786440 | tf_op jit(solution)/shard_map/ppermute | solution.py:331
  22.9 12.0 %collective-permute-start.5 = (bf16[16,64,128]{2,1,0:T(8,128)(2,1)S(1)}, bf16[16,64,128]{2,1,0:T(8,128)(2,1)S(1)}, u32[]{:S(2)}, u32[]{:S(2)}) collective-permute-start(bf16[16,64,128]{2,1,0:T(8,128)(2,1)S(1)} %gate.3.refs_4_.refs_0_), channel_id=1, source_target_pairs={{0,2},{2,0},{4,6},{6,4},{8,10},{10,8},{12,14},{14,12},{1,3},{3,1},... | collective-permute-start | bytes 786440 | tf_op jit(solution)/shard_map/ppermute | solution.py:331
  24.4 10.5 %collective-permute-start.6 = (bf16[16,64,128]{2,1,0:T(8,128)(2,1)S(1)}, bf16[16,64,128]{2,1,0:T(8,128)(2,1)S(1)}, u32[]{:S(2)}, u32[]{:S(2)}) collective-permute-start(bf16[16,64,128]{2,1,0:T(8,128)(2,1)S(1)} %gate.3.refs_4_.refs_0_), channel_id=1, source_target_pairs={{0,4},{2,6},{4,0},{6,2},{8,12},{10,14},{12,8},{14,10},{1,5},{3,7},... | collective-permute-start | bytes 786440 | tf_op jit(solution)/shard_map/ppermute | solution.py:331
  25.0 12.2 %collective-permute-start.7 = (bf16[16,64,128]{2,1,0:T(8,128)(2,1)S(1)}, bf16[16,64,128]{2,1,0:T(8,128)(2,1)S(1)}, u32[]{:S(2)}, u32[]{:S(2)}) collective-permute-start(bf16[16,64,128]{2,1,0:T(8,128)(2,1)S(1)} %gate.3.refs_4_.refs_0_), channel_id=1, source_target_pairs={{0,6},{2,4},{4,2},{6,0},{8,14},{10,12},{12,10},{14,8},{1,7},{3,5},... | collective-permute-start | bytes 786440 | tf_op jit(solution)/shard_map/ppermute | solution.py:331
  29.7 7.5 %copy-start = (f32[1024]{0:T(1024)S(1)}, f32[1024]{0:T(1024)}, u32[]{:S(2)}) copy-start(f32[1024]{0:T(1024)} %param.12) | copy-start | bytes 12292

commit v6 on v5

--- a/solution.py
+++ b/solution.py
@@ -11,7 +11,8 @@
 SMEM = pl.BlockSpec(memory_space=pltpu.SMEM)
 ANY = pl.BlockSpec(memory_space=pl.ANY)
 ROOMY = pltpu.CompilerParams(vmem_limit_bytes=56 * 2**20)
-SMALL = pltpu.CompilerParams(vmem_limit_bytes=12 * 2**20)
+LARGE = pltpu.CompilerParams(vmem_limit_bytes=12 * 2**20)
+SMALL = pltpu.CompilerParams(vmem_limit_bytes=4 * 2**20)
 BASE_FREQ = 0.0625
 LANES = 256
 BLOCK = 128
@@ -103,11 +104,20 @@
 
 
 def prepare_kernel(
-    points_ref, hypocenter_ref, velocity_ref, own_mask, own_slip, other_mask, other_slip, after_ref, *outs
+    points_ref, hypocenter_ref, velocity_ref, own_mask, own_slip, mask_hbm, slip_hbm, after_ref, *refs
 ):
-    own_out, other_out, columns, spots, token = outs
+    own_out, other_out, columns, spots, token, other_mask, other_slip, sems = refs
     half, variations = own_out.shape
     subfaults = 2 * half
+
+    def load(i, part):
+        rows = pl.ds(part * LANES, LANES)
+        source, target = ((mask_hbm, other_mask), (slip_hbm, other_slip))[i]
+        return pltpu.make_async_copy(source.at[rows], target.at[rows], sems.at[i, part])
+
+    for part in range(variations // LANES):
+        for i in range(2):
+            load(i, part).start()
     token[...] = jnp.zeros_like(token)
     first = pl.multiple_of(lax.axis_index("sub") * half, half)
     second = pl.multiple_of(half - first, half)
@@ -132,6 +142,9 @@
 
     for mask, slip, out in ((own_mask, own_slip, own_out), (other_mask, other_slip, other_out)):
         for row in range(0, variations, BLOCK):
+            if mask is other_mask and row % LANES == 0:
+                load(0, row // LANES).wait()
+                load(1, row // LANES).wait()
             rows = slice(row, row + BLOCK)
             out[:, rows] = (mask[rows, :].astype(jnp.float32) * slip[rows, :]).T
 
@@ -144,8 +157,13 @@
     return pl.pallas_call(
         prepare_kernel,
         out_shape=(out, out, columns, spots, TOKEN),
-        in_specs=[VMEM] * 7 + [ANY],
+        in_specs=[VMEM] * 5 + [ANY] * 3,
         out_specs=(VMEM,) * 5,
+        scratch_shapes=[
+            pltpu.VMEM(other_mask.shape, jnp.int32),
+            pltpu.VMEM(other_slip.shape, jnp.float32),
+            pltpu.SemaphoreType.DMA((2, variations // LANES)),
+        ],
         compiler_params=SMALL,
         cost_estimate=cost(3),
         name="prepare",
@@ -213,7 +231,34 @@
     )
 
 
-def work_kernel(fills, sums, has_total, unroll, numbers_ref, *refs):
+def late_fill_kernel(unit, numbers_ref, columns, spots, own_ref, other_ref, kept_ref, *refs):
+    out_ref, token = refs[-2:]
+    token[...] = jnp.zeros_like(token)
+
+    @pl.when(numbers_ref[1 + UNITS] == 0)
+    def _():
+        def body(k, carry):
+            fill(out_ref, numbers_ref, unit, k, columns, spots, own_ref, other_ref)
+            return carry
+
+        lax.fori_loop(0, FREQS, body, 0, unroll=4)
+
+
+def late_fill(numbers, sources, unit, kept, after=()):
+    args = [numbers, *sources, kept]
+    return pl.pallas_call(
+        functools.partial(late_fill_kernel, unit),
+        out_shape=(jax.ShapeDtypeStruct(kept.shape, kept.dtype), TOKEN),
+        in_specs=[SMEM] + [VMEM] * 5 + [ANY] * len(after),
+        out_specs=(VMEM, VMEM),
+        input_output_aliases={5: 0},
+        compiler_params=SMALL,
+        cost_estimate=cost(3),
+        name="late_fill",
+    )(*args, *after)
+
+
+def work_kernel(fills, sums, has_total, unroll, guarded, numbers_ref, *refs):
     refs = list(refs)
     take = lambda n: [refs.pop(0) for _ in range(n)]
     sources = take(4) if fills else None
@@ -238,13 +283,27 @@
             fill(out, numbers_ref, unit, k, *sources)
         return carry
 
-    lax.fori_loop(0, FREQS, body, 0, unroll=unroll)
+    if guarded:
+        for unit, out in zip(fills, outs):
+
+            def only(k, carry, unit=unit, out=out):
+                fill(out, numbers_ref, unit, k, *sources)
+                return carry
+
+            steps = FREQS if unit == fills[0] else numbers_ref[1 + UNITS] * FREQS // 2
+
+            if unit == fills[0]:
+                lax.fori_loop(0, FREQS, only, 0, unroll=unroll)
+            else:
+                lax.fori_loop(0, steps, lambda k, carry: only(2 * k + 1, only(2 * k, carry)), 0)
+    else:
+        lax.fori_loop(0, FREQS, body, 0, unroll=unroll)
 
 
 FREQS = 16
 
 
-def work(numbers, sources, fills, sums=(), total=None, after=(), unroll=2):
+def work(numbers, sources, fills, sums=(), total=None, after=(), unroll=4, guarded=False):
     columns, spots, own, other = sources
     variations = own.shape[1]
     args, aliases = [numbers], {}
@@ -262,7 +321,7 @@
         shapes.append(jax.ShapeDtypeStruct((FREQS, 2, sums[0][0][0].shape[2] // 2, variations), jnp.float32))
     shapes.append(TOKEN)
     return pl.pallas_call(
-        functools.partial(work_kernel, fills, len(sums), total is not None, unroll),
+        functools.partial(work_kernel, fills, len(sums), total is not None, unroll, guarded),
         out_shape=tuple(shapes),
         in_specs=[SMEM] + [VMEM] * (len(args) - 1) + [ANY] * len(after),
         out_specs=(VMEM,) * len(shapes),
@@ -312,15 +371,14 @@
     shape = jax.ShapeDtypeStruct(total.shape, jnp.float32)
     return pl.pallas_call(
         functools.partial(finish_kernel, len(sums), unroll),
-        out_shape=(shape, shape),
+        out_shape=shape,
         in_specs=[VMEM] * len(args),
-        out_specs=(ANY, VMEM),
-        scratch_shapes=[pltpu.SemaphoreType.DMA((FREQS,))],
-        input_output_aliases={len(args) - 1: 1},
-        compiler_params=SMALL,
+        out_specs=ANY,
+        scratch_shapes=[pltpu.VMEM(total.shape, jnp.float32), pltpu.SemaphoreType.DMA((FREQS,))],
+        compiler_params=LARGE,
         cost_estimate=cost(4),
         name="finish",
-    )(*args)[0]
+    )(*args)
 
 
 def swap(array, axis):
@@ -359,24 +417,25 @@
         place = lax.axis_index("var")
         block = jnp.concatenate([own_part, received], axis=1)
         pieces = [block, exchange(block, 2), exchange(block, 6)]
-        numbers = jnp.stack([place % 2] + [(place // 2) ^ s for s in (0, 1, 3, 2)]).astype(jnp.int32)
+        early = place // 2 == UNITS - 1
+        numbers = jnp.stack([place % 2] + [(place // 2) ^ s for s in (0, 1, 3, 2)] + [early]).astype(jnp.int32)
     else:
         whole = [lax.all_gather(piece, "var", axis=1, tiled=True) for piece in (own_part, received)]
         pieces = [
             jnp.concatenate([part[:, i * rows : (i + 1) * rows] for part in whole], axis=1) for i in range(2 * UNITS)
         ]
         pairs = [(pieces[2 * i], pieces[2 * i + 1]) for i in range(UNITS)]
-        numbers = jnp.arange(-1, UNITS, dtype=jnp.int32) * (jnp.arange(1 + UNITS, dtype=jnp.int32) > 0)
+        numbers = jnp.asarray([0, *range(UNITS), 0], jnp.int32)
 
     own, other, columns, spots, token = prepare(
         fault_points, hypocenter, velocity, member_mask, slip_amount, *swapped, pieces[0]
     )
     step = functools.partial(work, numbers, (columns, spots, own, other))
-    slips_0, token = step((0,), after=(token,))
+    slips_0, slips_1, token = step((0, 1), after=(token,), guarded=True)
     if routed:
         pieces[1] = gate(pieces[1], token)
         pairs = [(piece, exchange(piece, 1)) for piece in pieces[:2]]
-    slips_1, token = step((1,), after=pieces[1:2])
+    slips_1, token = late_fill(numbers, (columns, spots, own, other), 1, slips_1, after=pieces[1:2])
     if routed:
         pieces[2] = gate(pieces[2], token)
         pairs.append((pieces[2], exchange(pieces[2], 1)))

time: 42.5 us -> 42 us (0.988)
  Pallas kernels: 25.4 us -> 23.9 us
  waiting for transfers between devices: 3.61 us -> 4.52 us
    pallas_call x4 -> x3, Pallas kernels: 14.9 us -> 11.2 us  [work(): pl.pallas_call(functools.partial(work_kernel, fills, len(sums), total is...]
    pallas_call x0 -> x1, Pallas kernels: none -> 3.03 us  [late_fill(): pl.pallas_call(functools.partial(late_fill_kernel, unit), out_shape=(jax....]
    ppermute x7, waiting for transfers between devices: 3.4 us -> 4.32 us  [exchange(): return lax.ppermute(piece, 'var', [(i, i ^ bits) for i in range(2 * UNITS)])]
    pallas_call x1, Pallas kernels: 5.15 us -> 4.64 us  [finish(): pl.pallas_call(functools.partial(finish_kernel, len(sums), unroll), out_s...]
  transfers between devices with their start and end apart: 10 -> 10, of which waited for: 3 -> 3; matrix products, arithmetic and copies ran while one was open for 2% -> 2% of each run, Pallas kernels for 48% -> 46%
where the time goes in v6:
time: 42 us; the launch traced here: 41.8 us
  Pallas kernels  23.9 us (57%)
  starting transfers between devices  12.2 us (29%)
  waiting for transfers between devices  4.52 us (11%)
  local copies, waits for them, and re-layouts  1.04 us (2%)
    pallas_call x3, Pallas kernels, work(): pl.pallas_call(functools.partial(work_kernel, fills, len(sums), total is...  11.2 us
    ppermute x7, starting transfers between devices, exchange(): return lax.ppermute(piece, 'var', [(i, i ^ bits) for i in range(2 * UNITS)])  11.1 us
    pallas_call x1, Pallas kernels, finish(): pl.pallas_call(functools.partial(finish_kernel, len(sums), unroll), out_s...  4.64 us
    ppermute x7, waiting for transfers between devices, exchange(): return lax.ppermute(piece, 'var', [(i, i ^ bits) for i in range(2 * UNITS)])  4.32 us
    pallas_call x1, Pallas kernels, late_fill(): pl.pallas_call(functools.partial(late_fill_kernel, unit), out_shape=(jax....  3.03 us
    pallas_call x1, Pallas kernels, rotate(): pl.pallas_call(rotate_kernel, out_shape=(piece, piece), in_specs=[ANY] *...  3 us
    pallas_call x1, Pallas kernels, prepare(): pl.pallas_call(prepare_kernel, out_shape=(out, out, columns, spots, TOKEN...  2.01 us
    ppermute x3, starting transfers between devices, swap(): return lax.ppermute(array, axis, [(0, 1), (1, 0)])  1.12 us
  transfers between devices with their start and end apart: 10, of which 3 were waited for; matrix products, arithmetic and copies ran while one was open for 2% of the time, Pallas kernels for 46%

profile of v6, /device:TPU:0, one launch (start us, length us, event | category | flops | bytes accessed | tf_op | source)
XLA Modules:
  0.0 41.8 jit_solution(4978521819320032354)
XLA Ops:
  0.0 0.5 %collective-permute-start.2 = (s32[1024,256]{1,0:T(8,128)}, s32[1024,256]{1,0:T(8,128)}, u32[]{:S(2)}, u32[]{:S(2)}) collective-permute-start(s32[1024,256]{1,0:T(8,128)} %own_mask.1), channel_id=1, source_target_pairs={{0,1},{1,0},{2,3},{3,2},{4,5},{5,4},{6,7},{7,6},{8,9},{9,8},{10,11... | collective-permute-start | bytes 3145736 | tf_op jit(solution)/shard_map/ppermute | solution.py:385
  0.5 0.1 collective-permute-start.3
  0.6 3.0 %rotate.1 = (bf16[16,32,128]{2,1,0:T(8,128)(2,1)}, bf16[16,32,128]{2,1,0:T(8,128)(2,1)}) custom-call(bf16[2,6,32,16,128]{4,3,2,1,0:T(8,128)(2,1)} %bitcast.14, f32[6,256]{1,0:T(8,128)} %tensor_hbm.1, s32[1,128]{1,0:T(1,128)} %bitcast.15), custom_call_target="tpu_custom_call" | custom-call | flops 3300000000 | bytes 9000000 | tf_op jit(solution)/shard_map/rotate/pallas_call | solution.py:83
  3.6 0.5 %collective-permute-start = (bf16[16,32,128]{2,1,0:T(8,128)(2,1)}, bf16[16,32,128]{2,1,0:T(8,128)(2,1)S(1)}, u32[]{:S(2)}, u32[]{:S(2)}) collective-permute-start(bf16[16,32,128]{2,1,0:T(8,128)(2,1)} %get-tuple-element.22), channel_id=1, source_target_pairs={{0,1},{1,0},{2,3},{3,2},{4,5},{5,4},{6,7},{7,6},{8,9},{9,8},{10,11... | collective-permute-start | bytes 393224 | tf_op jit(solution)/shard_map/ppermute | solution.py:385
  4.1 0.1 stack.31.numbers_ref
  4.2 0.9 %constant_dynamic-update-slice_fusion.1 = bf16[16,64,128]{2,1,0:T(8,128)(2,1)S(1)} fusion(bf16[16,32,128]{2,1,0:T(8,128)(2,1)} %get-tuple-element.21), kind=kLoop, calls=%fused_computation.1 | loop fusion | bytes 262144
  5.1 0.2 collective-permute-done
  5.4 3.0 %collective-permute-start.4 = (bf16[16,64,128]{2,1,0:T(8,128)(2,1)S(1)}, bf16[16,64,128]{2,1,0:T(8,128)(2,1)S(1)}, u32[]{:S(2)}, u32[]{:S(2)}) collective-permute-start(bf16[16,64,128]{2,1,0:T(8,128)(2,1)S(1)} %constant_dynamic-update-slice_fusion.after_ref.refs_4_), channel_id=1, source_target_pairs={{0,4},{2,6},{4,0},{6,2},{8,12},{10,14},{12,8},{14,10},{1,5},{3,7},... | collective-permute-start | bytes 786440 | tf_op jit(solution)/shard_map/ppermute | solution.py:389
  8.4 2.5 %collective-permute-start.1 = (bf16[16,64,128]{2,1,0:T(8,128)(2,1)S(1)}, bf16[16,64,128]{2,1,0:T(8,128)(2,1)S(1)}, u32[]{:S(2)}, u32[]{:S(2)}) collective-permute-start(bf16[16,64,128]{2,1,0:T(8,128)(2,1)S(1)} %constant_dynamic-update-slice_fusion.after_ref.refs_4_), channel_id=1, source_target_pairs={{0,12},{2,14},{4,8},{6,10},{8,4},{10,6},{12,0},{14,2},{1,13},{3,15... | collective-permute-start | bytes 786440 | tf_op jit(solution)/shard_map/ppermute | solution.py:389
  10.8 1.5 %collective-permute-start.8 = (bf16[16,64,128]{2,1,0:T(8,128)(2,1)S(1)}, bf16[16,64,128]{2,1,0:T(8,128)(2,1)S(1)}, u32[]{:S(2)}, u32[]{:S(2)}) collective-permute-start(bf16[16,64,128]{2,1,0:T(8,128)(2,1)S(1)} %constant_dynamic-update-slice_fusion.after_ref.refs_4_), channel_id=1, source_target_pairs={{0,2},{2,0},{4,6},{6,4},{8,10},{10,8},{12,14},{14,12},{1,3},{3,1},... | collective-permute-start | bytes 786440 | tf_op jit(solution)/shard_map/ppermute | solution.py:389
  12.4 2.0 %prepare.1 = (f32[256,1024]{1,0:T(8,128)S(1)}, f32[256,1024]{1,0:T(8,128)S(1)}, f32[2,512,128]{2,1,0:T(8,128)S(1)}, f32[8,1024]{1,0:T(8,128)S(1)}, f32[8,128]{1,0:T(8,128)S(1)}) custom-call(f32[2,512]{1,0:T(2,128)S(1)} %copy-done.3, s32[1,1024]{1,0:T(1,128)S(1)} %bitcast.12, f32[1,1024]{1,0:T(1,128)S(1)} %bitcast.13, s32[1024,256]{1,0:T(8,128)S(1)} %copy-done.1, ...), custom_call_target="tpu_custom_call" | custom-call | flops 3300000000 | bytes 9000000 | tf_op jit(solution)/shard_map/prepare/pallas_call | solution.py:157
  14.4 3.0 %fillfill.1 = (bf16[16,8,256,128]{3,2,1,0:T(8,128)(2,1)S(1)}, bf16[16,8,256,128]{3,2,1,0:T(8,128)(2,1)S(1)}, f32[8,128]{1,0:T(8,128)S(1)}) custom-call(s32[6]{0:T(128)S(1)} %stack.31.numbers_ref, f32[2,512,128]{2,1,0:T(8,128)S(1)} %get-tuple-element.23.refs_0_.columns, f32[8,1024]{1,0:T(8,128)S(1)} %get-tuple-element.24.refs_1_.spots, ...), custom_call_target="tpu_custom_call" | custom-call | flops 3300000000 | bytes 9000000 | tf_op jit(solution)/shard_map/fillfill/pallas_call | solution.py:323
  17.5 0.0 collective-permute-done.4.array_ref
  17.5 0.6 %collective-permute-start.9 = (bf16[16,64,128]{2,1,0:T(8,128)(2,1)S(1)}, bf16[16,64,128]{2,1,0:T(8,128)(2,1)S(1)}, u32[]{:S(2)}, u32[]{:S(2)}) collective-permute-start(bf16[16,64,128]{2,1,0:T(8,128)(2,1)S(1)} %gate.2.refs_0_.refs_7_), channel_id=1, source_target_pairs={{0,2},{2,0},{4,6},{6,4},{8,10},{10,8},{12,14},{14,12},{1,3},{3,1},... | collective-permute-start | bytes 786440 | tf_op jit(solution)/shard_map/ppermute | solution.py:389
  18.1 3.0 %late_fill.1 = (bf16[16,8,256,128]{3,2,1,0:T(8,128)(2,1)S(1)}, f32[8,128]{1,0:T(8,128)S(1)}) custom-call(s32[6]{0:T(128)S(1)} %stack.31.numbers_ref, f32[2,512,128]{2,1,0:T(8,128)S(1)} %get-tuple-element.23.refs_0_.columns, f32[8,1024]{1,0:T(8,128)S(1)} %get-tuple-element.24.refs_1_.spots, ...), custom_call_target="tpu_custom_call", output_to_operand_aliasing={{0}: (5, {})} | custom-call | flops 3300000000 | bytes 9000000 | tf_op jit(solution)/shard_map/late_fill/pallas_call | solution.py:249
  21.1 1.8 %collective-permute-done.1.array_ref = bf16[16,64,128]{2,1,0:T(8,128)(2,1)S(1)} collective-permute-done((bf16[16,64,128]{2,1,0:T(8,128)(2,1)S(1)}, bf16[16,64,128]{2,1,0:T(8,128)(2,1)S(1)}, u32[]{:S(2)}, u32[]{:S(2)}) %collective-permute-start.1) | collective-permute-done | bytes 262176 | tf_op jit(solution)/shard_map/ppermute | solution.py:389
  22.9 1.5 %collective-permute-start.5 = (bf16[16,64,128]{2,1,0:T(8,128)(2,1)S(1)}, bf16[16,64,128]{2,1,0:T(8,128)(2,1)S(1)}, u32[]{:S(2)}, u32[]{:S(2)}) collective-permute-start(bf16[16,64,128]{2,1,0:T(8,128)(2,1)S(1)} %gate.3.refs_4_.refs_0_), channel_id=1, source_target_pairs={{0,2},{2,0},{4,6},{6,4},{8,10},{10,8},{12,14},{14,12},{1,3},{3,1},... | collective-permute-start | bytes 786440 | tf_op jit(solution)/shard_map/ppermute | solution.py:389
  24.4 0.6 %collective-permute-start.6 = (bf16[16,64,128]{2,1,0:T(8,128)(2,1)S(1)}, bf16[16,64,128]{2,1,0:T(8,128)(2,1)S(1)}, u32[]{:S(2)}, u32[]{:S(2)}) collective-permute-start(bf16[16,64,128]{2,1,0:T(8,128)(2,1)S(1)} %gate.3.refs_4_.refs_0_), channel_id=1, source_target_pairs={{0,4},{2,6},{4,0},{6,2},{8,12},{10,14},{12,8},{14,10},{1,5},{3,7},... | collective-permute-start | bytes 786440 | tf_op jit(solution)/shard_map/ppermute | solution.py:389
  25.0 1.4 %collective-permute-start.7 = (bf16[16,64,128]{2,1,0:T(8,128)(2,1)S(1)}, bf16[16,64,128]{2,1,0:T(8,128)(2,1)S(1)}, u32[]{:S(2)}, u32[]{:S(2)}) collective-permute-start(bf16[16,64,128]{2,1,0:T(8,128)(2,1)S(1)} %gate.3.refs_4_.refs_0_), channel_id=1, source_target_pairs={{0,6},{2,4},{4,2},{6,0},{8,14},{10,12},{12,10},{14,8},{1,7},{3,5},... | collective-permute-start | bytes 786440 | tf_op jit(solution)/shard_map/ppermute | solution.py:389
  26.4 3.0 %fill.1 = (bf16[16,8,256,128]{3,2,1,0:T(8,128)(2,1)S(1)}, f32[8,128]{1,0:T(8,128)S(1)}) custom-call(s32[6]{0:T(128)S(1)} %stack.31.numbers_ref, f32[2,512,128]{2,1,0:T(8,128)S(1)} %get-tuple-element.23.refs_0_.columns, f32[8,1024]{1,0:T(8,128)S(1)} %get-tuple-element.24.refs_1_.spots, f32[256,1024]{1,0:T(8,128)S(1)} %get-tuple-element.25.refs_2_.own_ref, ...), custom_call_target="tpu_custom_call" | custom-call | flops 3300000000 | bytes 9000000 | tf_op jit(solution)/shard_map/fill/pallas_call | solution.py:323
  29.4 0.0 copy-start
  29.5 5.2 %fillsumsum.1 = (bf16[16,8,256,128]{3,2,1,0:T(8,128)(2,1)S(1)}, f32[16,2,64,1024]{3,2,1,0:T(8,128)S(1)}, f32[8,128]{1,0:T(8,128)}) custom-call(s32[6]{0:T(128)S(1)} %stack.31.numbers_ref, f32[2,512,128]{2,1,0:T(8,128)S(1)} %get-tuple-element.23.refs_0_.columns, f32[8,1024]{1,0:T(8,128)S(1)} %get-tuple-element.24.refs_1_.spots, ...), custom_call_target="tpu_custom_call" | custom-call | flops 3300000000 | bytes 9000000 | tf_op jit(solution)/shard_map/fillsumsum/pallas_call | solution.py:323
  34.6 2.5 %collective-permute-done.7.refs_4_ = bf16[16,64,128]{2,1,0:T(8,128)(2,1)S(1)} collective-permute-done((bf16[16,64,128]{2,1,0:T(8,128)(2,1)S(1)}, bf16[16,64,128]{2,1,0:T(8,128)(2,1)S(1)}, u32[]{:S(2)}, u32[]{:S(2)}) %collective-permute-start.7) | collective-permute-done | bytes 262176 | tf_op jit(solution)/shard_map/ppermute | solution.py:389
  37.2 4.6 %finish.1 = f32[16,2,64,1024]{3,2,1,0:T(8,128)} custom-call(f32[1,1024]{1,0:T(1,128)S(1)} %bitcast.11, bf16[16,64,128]{2,1,0:T(8,128)(2,1)S(1)} %gate.3.refs_4_.refs_0_, bf16[16,64,128]{2,1,0:T(8,128)(2,1)S(1)} %collective-permute-done.5.refs_1_, bf16[16,8,256,128]{3,2,1,0:T(8,128)(2,1)S(1)} %get-tuple-element.31.refs_2_, ...), custom_call_target="tpu_custom_call" | custom-call | flops 4400000000 | bytes 12000000 | tf_op jit(solution)/shard_map/finish/pallas_call | solution.py:372
  (20 shorter events, 0.1 us)
Async XLA Ops:
  0.0 12.4 %copy-start.1 = (s32[1024,256]{1,0:T(8,128)S(1)}, s32[1024,256]{1,0:T(8,128)}, u32[]{:S(2)}) copy-start(s32[1024,256]{1,0:T(8,128)} %own_mask.1) | copy-start | bytes 3145732
  0.0 12.4 %copy-start.2 = (f32[1024,256]{1,0:T(8,128)S(1)}, f32[1024,256]{1,0:T(8,128)}, u32[]{:S(2)}) copy-start(f32[1024,256]{1,0:T(8,128)} %own_slip.1) | copy-start | bytes 3145732
  0.0 12.4 %copy-start.5 = (f32[1024]{0:T(1024)S(1)}, f32[1024]{0:T(1024)}, u32[]{:S(2)}) copy-start(f32[1024]{0:T(1024)} %param.11) | copy-start | bytes 12292
  0.0 12.4 %copy-start.4 = (s32[1024]{0:T(1024)S(1)}, s32[1024]{0:T(1024)}, u32[]{:S(2)}) copy-start(s32[1024]{0:T(1024)} %param.10) | copy-start | bytes 12292
  0.0 12.4 %copy-start.3 = (f32[2,512]{1,0:T(2,128)S(1)}, f32[2,512]{1,0:T(2,128)}, u32[]{:S(2)}) copy-start(f32[2,512]{1,0:T(2,128)} %points_ref.1) | copy-start | bytes 12292
  0.0 12.4 %collective-permute-start.2 = (s32[1024,256]{1,0:T(8,128)}, s32[1024,256]{1,0:T(8,128)}, u32[]{:S(2)}, u32[]{:S(2)}) collective-permute-start(s32[1024,256]{1,0:T(8,128)} %own_mask.1), channel_id=1, source_target_pairs={{0,1},{1,0},{2,3},{3,2},{4,5},{5,4},{6,7},{7,6},{8,9},{9,8},{10,11... | collective-permute-start | bytes 3145736 | tf_op jit(solution)/shard_map/ppermute | solution.py:385
  0.5 11.8 %collective-permute-start.3 = (f32[1024,256]{1,0:T(8,128)}, f32[1024,256]{1,0:T(8,128)}, u32[]{:S(2)}, u32[]{:S(2)}) collective-permute-start(f32[1024,256]{1,0:T(8,128)} %own_slip.1), channel_id=1, source_target_pairs={{0,1},{1,0},{2,3},{3,2},{4,5},{5,4},{6,7},{7,6},{8,9},{9,8},{10,11... | collective-permute-start | bytes 3145736 | tf_op jit(solution)/shard_map/ppermute | solution.py:385
  3.6 1.7 %collective-permute-start = (bf16[16,32,128]{2,1,0:T(8,128)(2,1)}, bf16[16,32,128]{2,1,0:T(8,128)(2,1)S(1)}, u32[]{:S(2)}, u32[]{:S(2)}) collective-permute-start(bf16[16,32,128]{2,1,0:T(8,128)(2,1)} %get-tuple-element.22), channel_id=1, source_target_pairs={{0,1},{1,0},{2,3},{3,2},{4,5},{5,4},{6,7},{7,6},{8,9},{9,8},{10,11... | collective-permute-start | bytes 393224 | tf_op jit(solution)/shard_map/ppermute | solution.py:385
  5.4 12.1 %collective-permute-start.4 = (bf16[16,64,128]{2,1,0:T(8,128)(2,1)S(1)}, bf16[16,64,128]{2,1,0:T(8,128)(2,1)S(1)}, u32[]{:S(2)}, u32[]{:S(2)}) collective-permute-start(bf16[16,64,128]{2,1,0:T(8,128)(2,1)S(1)} %constant_dynamic-update-slice_fusion.after_ref.refs_4_), channel_id=1, source_target_pairs={{0,4},{2,6},{4,0},{6,2},{8,12},{10,14},{12,8},{14,10},{1,5},{3,7},... | collective-permute-start | bytes 786440 | tf_op jit(solution)/shard_map/ppermute | solution.py:389
  8.4 14.5 %collective-permute-start.1 = (bf16[16,64,128]{2,1,0:T(8,128)(2,1)S(1)}, bf16[16,64,128]{2,1,0:T(8,128)(2,1)S(1)}, u32[]{:S(2)}, u32[]{:S(2)}) collective-permute-start(bf16[16,64,128]{2,1,0:T(8,128)(2,1)S(1)} %constant_dynamic-update-slice_fusion.after_ref.refs_4_), channel_id=1, source_target_pairs={{0,12},{2,14},{4,8},{6,10},{8,4},{10,6},{12,0},{14,2},{1,13},{3,15... | collective-permute-start | bytes 786440 | tf_op jit(solution)/shard_map/ppermute | solution.py:389
  10.8 18.6 %collective-permute-start.8 = (bf16[16,64,128]{2,1,0:T(8,128)(2,1)S(1)}, bf16[16,64,128]{2,1,0:T(8,128)(2,1)S(1)}, u32[]{:S(2)}, u32[]{:S(2)}) collective-permute-start(bf16[16,64,128]{2,1,0:T(8,128)(2,1)S(1)} %constant_dynamic-update-slice_fusion.after_ref.refs_4_), channel_id=1, source_target_pairs={{0,2},{2,0},{4,6},{6,4},{8,10},{10,8},{12,14},{14,12},{1,3},{3,1},... | collective-permute-start | bytes 786440 | tf_op jit(solution)/shard_map/ppermute | solution.py:389
  17.5 11.9 %collective-permute-start.9 = (bf16[16,64,128]{2,1,0:T(8,128)(2,1)S(1)}, bf16[16,64,128]{2,1,0:T(8,128)(2,1)S(1)}, u32[]{:S(2)}, u32[]{:S(2)}) collective-permute-start(bf16[16,64,128]{2,1,0:T(8,128)(2,1)S(1)} %gate.2.refs_0_.refs_7_), channel_id=1, source_target_pairs={{0,2},{2,0},{4,6},{6,4},{8,10},{10,8},{12,14},{14,12},{1,3},{3,1},... | collective-permute-start | bytes 786440 | tf_op jit(solution)/shard_map/ppermute | solution.py:389
  22.9 11.7 %collective-permute-start.5 = (bf16[16,64,128]{2,1,0:T(8,128)(2,1)S(1)}, bf16[16,64,128]{2,1,0:T(8,128)(2,1)S(1)}, u32[]{:S(2)}, u32[]{:S(2)}) collective-permute-start(bf16[16,64,128]{2,1,0:T(8,128)(2,1)S(1)} %gate.3.refs_4_.refs_0_), channel_id=1, source_target_pairs={{0,2},{2,0},{4,6},{6,4},{8,10},{10,8},{12,14},{14,12},{1,3},{3,1},... | collective-permute-start | bytes 786440 | tf_op jit(solution)/shard_map/ppermute | solution.py:389
  24.4 10.2 %collective-permute-start.6 = (bf16[16,64,128]{2,1,0:T(8,128)(2,1)S(1)}, bf16[16,64,128]{2,1,0:T(8,128)(2,1)S(1)}, u32[]{:S(2)}, u32[]{:S(2)}) collective-permute-start(bf16[16,64,128]{2,1,0:T(8,128)(2,1)S(1)} %gate.3.refs_4_.refs_0_), channel_id=1, source_target_pairs={{0,4},{2,6},{4,0},{6,2},{8,12},{10,14},{12,8},{14,10},{1,5},{3,7},... | collective-permute-start | bytes 786440 | tf_op jit(solution)/shard_map/ppermute | solution.py:389
  25.0 12.2 %collective-permute-start.7 = (bf16[16,64,128]{2,1,0:T(8,128)(2,1)S(1)}, bf16[16,64,128]{2,1,0:T(8,128)(2,1)S(1)}, u32[]{:S(2)}, u32[]{:S(2)}) collective-permute-start(bf16[16,64,128]{2,1,0:T(8,128)(2,1)S(1)} %gate.3.refs_4_.refs_0_), channel_id=1, source_target_pairs={{0,6},{2,4},{4,2},{6,0},{8,14},{10,12},{12,10},{14,8},{1,7},{3,5},... | collective-permute-start | bytes 786440 | tf_op jit(solution)/shard_map/ppermute | solution.py:389
  29.4 7.7 %copy-start = (f32[1024]{0:T(1024)S(1)}, f32[1024]{0:T(1024)}, u32[]{:S(2)}) copy-start(f32[1024]{0:T(1024)} %param.12) | copy-start | bytes 12292

commit v7 on v6

--- a/solution.py
+++ b/solution.py
@@ -79,7 +79,7 @@
 
 def rotate(green, tensor, station_ids):
     _, _, count, freqs, stations = green.shape
-    piece = jax.ShapeDtypeStruct((freqs, count, stations), jnp.bfloat16)
+    piece = pltpu.VMEM((freqs, count, stations), jnp.bfloat16)
     return pl.pallas_call(
         rotate_kernel,
         out_shape=(piece, piece),

time: 42 us -> 41.1 us (0.979)
  local copies, waits for them, and re-layouts: 1.04 us -> 0.14 us
  waiting for transfers between devices: 4.52 us -> 5.26 us
  Pallas kernels: 23.9 us -> 23.2 us
    unnamed x13, local copies, waits for them, and re-layouts: 0.94 us -> 0.03 us
    ppermute x3, waiting for transfers between devices: 0.2 us -> 0.96 us  [swap(): return lax.ppermute(array, axis, [(0, 1), (1, 0)])]
    pallas_call x1, Pallas kernels: 3 us -> 2.32 us  [rotate(): pl.pallas_call(rotate_kernel, out_shape=(piece, piece), in_specs=[ANY] *...]
  transfers between devices with their start and end apart: 10 -> 10, of which waited for: 3 -> 3; matrix products, arithmetic and copies ran while one was open for 2% -> 0% of each run, Pallas kernels for 46% -> 45%
where the time goes in v7:
time: 41.1 us; the launch traced here: 41 us
  Pallas kernels  23.2 us (56%)
  starting transfers between devices  12.2 us (30%)
  waiting for transfers between devices  5.26 us (13%)
    pallas_call x3, Pallas kernels, work(): pl.pallas_call(functools.partial(work_kernel, fills, len(sums), total is...  11.2 us
    ppermute x7, starting transfers between devices, exchange(): return lax.ppermute(piece, 'var', [(i, i ^ bits) for i in range(2 * UNITS)])  11.1 us
    pallas_call x1, Pallas kernels, finish(): pl.pallas_call(functools.partial(finish_kernel, len(sums), unroll), out_s...  4.63 us
    ppermute x7, waiting for transfers between devices, exchange(): return lax.ppermute(piece, 'var', [(i, i ^ bits) for i in range(2 * UNITS)])  4.3 us
    pallas_call x1, Pallas kernels, late_fill(): pl.pallas_call(functools.partial(late_fill_kernel, unit), out_shape=(jax....  3.03 us
    pallas_call x1, Pallas kernels, rotate(): pl.pallas_call(rotate_kernel, out_shape=(piece, piece), in_specs=[ANY] *...  2.32 us
    pallas_call x1, Pallas kernels, prepare(): pl.pallas_call(prepare_kernel, out_shape=(out, out, columns, spots, TOKEN...  2.01 us
    ppermute x3, starting transfers between devices, swap(): return lax.ppermute(array, axis, [(0, 1), (1, 0)])  1.12 us
  transfers between devices with their start and end apart: 10, of which 3 were waited for; matrix products, arithmetic and copies ran while one was open for 0% of the time, Pallas kernels for 45%

profile of v7, /device:TPU:0, one launch (start us, length us, event | category | flops | bytes accessed | tf_op | source)
XLA Modules:
  0.0 41.0 jit_solution(6891893012239516793)
XLA Ops:
  0.0 0.5 %collective-permute-start.2 = (s32[1024,256]{1,0:T(8,128)}, s32[1024,256]{1,0:T(8,128)}, u32[]{:S(2)}, u32[]{:S(2)}) collective-permute-start(s32[1024,256]{1,0:T(8,128)} %own_mask.1), channel_id=1, source_target_pairs={{0,1},{1,0},{2,3},{3,2},{4,5},{5,4},{6,7},{7,6},{8,9},{9,8},{10,11... | collective-permute-start | bytes 3145736 | tf_op jit(solution)/shard_map/ppermute | solution.py:385
  0.5 0.1 collective-permute-start.3
  0.6 2.3 %rotate.1 = (bf16[16,32,128]{2,1,0:T(8,128)(2,1)S(1)}, bf16[16,32,128]{2,1,0:T(8,128)(2,1)S(1)}) custom-call(bf16[2,6,32,16,128]{4,3,2,1,0:T(8,128)(2,1)} %bitcast.14, f32[6,256]{1,0:T(8,128)} %tensor_hbm.1, s32[1,128]{1,0:T(1,128)} %bitcast.15), custom_call_target="tpu_custom_call" | custom-call | flops 3300000000 | bytes 9000000 | tf_op jit(solution)/shard_map/rotate/pallas_call | solution.py:83
  3.0 0.5 %collective-permute-start = (bf16[16,32,128]{2,1,0:T(8,128)(2,1)S(1)}, bf16[16,32,128]{2,1,0:T(8,128)(2,1)S(1)}, u32[]{:S(2)}, u32[]{:S(2)}) collective-permute-start(bf16[16,32,128]{2,1,0:T(8,128)(2,1)S(1)} %get-tuple-element.22), channel_id=1, source_target_pairs={{0,1},{1,0},{2,3},{3,2},{4,5},{5,4},{6,7},{7,6},{8,9},{9,8},{10,11... | collective-permute-start | bytes 393224 | tf_op jit(solution)/shard_map/ppermute | solution.py:385
  3.5 0.1 stack.31.numbers_ref
  3.6 1.0 %collective-permute-done = bf16[16,32,128]{2,1,0:T(8,128)(2,1)S(1)} collective-permute-done((bf16[16,32,128]{2,1,0:T(8,128)(2,1)S(1)}, bf16[16,32,128]{2,1,0:T(8,128)(2,1)S(1)}, u32[]{:S(2)}, u32[]{:S(2)}) %collective-permute-start) | collective-permute-done | bytes 131104 | tf_op jit(solution)/shard_map/ppermute | solution.py:385
  4.5 3.0 %collective-permute-start.4 = (bf16[16,64,128]{2,1,0:T(8,128)(2,1)S(1)}, bf16[16,64,128]{2,1,0:T(8,128)(2,1)S(1)}, u32[]{:S(2)}, u32[]{:S(2)}) collective-permute-start(bf16[16,64,128]{2,1,0:T(8,128)(2,1)S(1)} %constant_dynamic-update-slice_fusion.after_ref.refs_4_), channel_id=1, source_target_pairs={{0,4},{2,6},{4,0},{6,2},{8,12},{10,14},{12,8},{14,10},{1,5},{3,7},... | collective-permute-start | bytes 786440 | tf_op jit(solution)/shard_map/ppermute | solution.py:389
  7.6 2.5 %collective-permute-start.1 = (bf16[16,64,128]{2,1,0:T(8,128)(2,1)S(1)}, bf16[16,64,128]{2,1,0:T(8,128)(2,1)S(1)}, u32[]{:S(2)}, u32[]{:S(2)}) collective-permute-start(bf16[16,64,128]{2,1,0:T(8,128)(2,1)S(1)} %constant_dynamic-update-slice_fusion.after_ref.refs_4_), channel_id=1, source_target_pairs={{0,12},{2,14},{4,8},{6,10},{8,4},{10,6},{12,0},{14,2},{1,13},{3,15... | collective-permute-start | bytes 786440 | tf_op jit(solution)/shard_map/ppermute | solution.py:389
  10.0 1.5 %collective-permute-start.8 = (bf16[16,64,128]{2,1,0:T(8,128)(2,1)S(1)}, bf16[16,64,128]{2,1,0:T(8,128)(2,1)S(1)}, u32[]{:S(2)}, u32[]{:S(2)}) collective-permute-start(bf16[16,64,128]{2,1,0:T(8,128)(2,1)S(1)} %constant_dynamic-update-slice_fusion.after_ref.refs_4_), channel_id=1, source_target_pairs={{0,2},{2,0},{4,6},{6,4},{8,10},{10,8},{12,14},{14,12},{1,3},{3,1},... | collective-permute-start | bytes 786440 | tf_op jit(solution)/shard_map/ppermute | solution.py:389
  11.6 0.0 collective-permute-done.3.slip_hbm
  11.6 2.0 %prepare.1 = (f32[256,1024]{1,0:T(8,128)S(1)}, f32[256,1024]{1,0:T(8,128)S(1)}, f32[2,512,128]{2,1,0:T(8,128)S(1)}, f32[8,1024]{1,0:T(8,128)S(1)}, f32[8,128]{1,0:T(8,128)S(1)}) custom-call(f32[2,512]{1,0:T(2,128)S(1)} %copy-done.3, s32[1,1024]{1,0:T(1,128)S(1)} %bitcast.12, f32[1,1024]{1,0:T(1,128)S(1)} %bitcast.13, s32[1024,256]{1,0:T(8,128)S(1)} %copy-done.1, ...), custom_call_target="tpu_custom_call" | custom-call | flops 3300000000 | bytes 9000000 | tf_op jit(solution)/shard_map/prepare/pallas_call | solution.py:157
  13.6 3.0 %fillfill.1 = (bf16[16,8,256,128]{3,2,1,0:T(8,128)(2,1)S(1)}, bf16[16,8,256,128]{3,2,1,0:T(8,128)(2,1)S(1)}, f32[8,128]{1,0:T(8,128)S(1)}) custom-call(s32[6]{0:T(128)S(1)} %stack.31.numbers_ref, f32[2,512,128]{2,1,0:T(8,128)S(1)} %get-tuple-element.23.refs_0_.columns, f32[8,1024]{1,0:T(8,128)S(1)} %get-tuple-element.24.refs_1_.spots, ...), custom_call_target="tpu_custom_call" | custom-call | flops 3300000000 | bytes 9000000 | tf_op jit(solution)/shard_map/fillfill/pallas_call | solution.py:323
  16.7 0.0 collective-permute-done.4.array_ref
  16.7 0.6 %collective-permute-start.9 = (bf16[16,64,128]{2,1,0:T(8,128)(2,1)S(1)}, bf16[16,64,128]{2,1,0:T(8,128)(2,1)S(1)}, u32[]{:S(2)}, u32[]{:S(2)}) collective-permute-start(bf16[16,64,128]{2,1,0:T(8,128)(2,1)S(1)} %gate.2.refs_0_.refs_7_), channel_id=1, source_target_pairs={{0,2},{2,0},{4,6},{6,4},{8,10},{10,8},{12,14},{14,12},{1,3},{3,1},... | collective-permute-start | bytes 786440 | tf_op jit(solution)/shard_map/ppermute | solution.py:389
  17.3 3.0 %late_fill.1 = (bf16[16,8,256,128]{3,2,1,0:T(8,128)(2,1)S(1)}, f32[8,128]{1,0:T(8,128)S(1)}) custom-call(s32[6]{0:T(128)S(1)} %stack.31.numbers_ref, f32[2,512,128]{2,1,0:T(8,128)S(1)} %get-tuple-element.23.refs_0_.columns, f32[8,1024]{1,0:T(8,128)S(1)} %get-tuple-element.24.refs_1_.spots, ...), custom_call_target="tpu_custom_call", output_to_operand_aliasing={{0}: (5, {})} | custom-call | flops 3300000000 | bytes 9000000 | tf_op jit(solution)/shard_map/late_fill/pallas_call | solution.py:249
  20.3 1.8 %collective-permute-done.1.array_ref = bf16[16,64,128]{2,1,0:T(8,128)(2,1)S(1)} collective-permute-done((bf16[16,64,128]{2,1,0:T(8,128)(2,1)S(1)}, bf16[16,64,128]{2,1,0:T(8,128)(2,1)S(1)}, u32[]{:S(2)}, u32[]{:S(2)}) %collective-permute-start.1) | collective-permute-done | bytes 262176 | tf_op jit(solution)/shard_map/ppermute | solution.py:389
  22.1 1.5 %collective-permute-start.5 = (bf16[16,64,128]{2,1,0:T(8,128)(2,1)S(1)}, bf16[16,64,128]{2,1,0:T(8,128)(2,1)S(1)}, u32[]{:S(2)}, u32[]{:S(2)}) collective-permute-start(bf16[16,64,128]{2,1,0:T(8,128)(2,1)S(1)} %gate.3.refs_4_.refs_0_), channel_id=1, source_target_pairs={{0,2},{2,0},{4,6},{6,4},{8,10},{10,8},{12,14},{14,12},{1,3},{3,1},... | collective-permute-start | bytes 786440 | tf_op jit(solution)/shard_map/ppermute | solution.py:389
  23.6 0.6 %collective-permute-start.6 = (bf16[16,64,128]{2,1,0:T(8,128)(2,1)S(1)}, bf16[16,64,128]{2,1,0:T(8,128)(2,1)S(1)}, u32[]{:S(2)}, u32[]{:S(2)}) collective-permute-start(bf16[16,64,128]{2,1,0:T(8,128)(2,1)S(1)} %gate.3.refs_4_.refs_0_), channel_id=1, source_target_pairs={{0,4},{2,6},{4,0},{6,2},{8,12},{10,14},{12,8},{14,10},{1,5},{3,7},... | collective-permute-start | bytes 786440 | tf_op jit(solution)/shard_map/ppermute | solution.py:389
  24.2 1.4 %collective-permute-start.7 = (bf16[16,64,128]{2,1,0:T(8,128)(2,1)S(1)}, bf16[16,64,128]{2,1,0:T(8,128)(2,1)S(1)}, u32[]{:S(2)}, u32[]{:S(2)}) collective-permute-start(bf16[16,64,128]{2,1,0:T(8,128)(2,1)S(1)} %gate.3.refs_4_.refs_0_), channel_id=1, source_target_pairs={{0,6},{2,4},{4,2},{6,0},{8,14},{10,12},{12,10},{14,8},{1,7},{3,5},... | collective-permute-start | bytes 786440 | tf_op jit(solution)/shard_map/ppermute | solution.py:389
  25.6 3.0 %fill.1 = (bf16[16,8,256,128]{3,2,1,0:T(8,128)(2,1)S(1)}, f32[8,128]{1,0:T(8,128)S(1)}) custom-call(s32[6]{0:T(128)S(1)} %stack.31.numbers_ref, f32[2,512,128]{2,1,0:T(8,128)S(1)} %get-tuple-element.23.refs_0_.columns, f32[8,1024]{1,0:T(8,128)S(1)} %get-tuple-element.24.refs_1_.spots, f32[256,1024]{1,0:T(8,128)S(1)} %get-tuple-element.25.refs_2_.own_ref, ...), custom_call_target="tpu_custom_call" | custom-call | flops 3300000000 | bytes 9000000 | tf_op jit(solution)/shard_map/fill/pallas_call | solution.py:323
  28.6 0.0 copy-start
  28.6 5.2 %fillsumsum.1 = (bf16[16,8,256,128]{3,2,1,0:T(8,128)(2,1)S(1)}, f32[16,2,64,1024]{3,2,1,0:T(8,128)S(1)}, f32[8,128]{1,0:T(8,128)}) custom-call(s32[6]{0:T(128)S(1)} %stack.31.numbers_ref, f32[2,512,128]{2,1,0:T(8,128)S(1)} %get-tuple-element.23.refs_0_.columns, f32[8,1024]{1,0:T(8,128)S(1)} %get-tuple-element.24.refs_1_.spots, ...), custom_call_target="tpu_custom_call" | custom-call | flops 3300000000 | bytes 9000000 | tf_op jit(solution)/shard_map/fillsumsum/pallas_call | solution.py:323
  33.8 2.5 %collective-permute-done.7.refs_4_ = bf16[16,64,128]{2,1,0:T(8,128)(2,1)S(1)} collective-permute-done((bf16[16,64,128]{2,1,0:T(8,128)(2,1)S(1)}, bf16[16,64,128]{2,1,0:T(8,128)(2,1)S(1)}, u32[]{:S(2)}, u32[]{:S(2)}) %collective-permute-start.7) | collective-permute-done | bytes 262176 | tf_op jit(solution)/shard_map/ppermute | solution.py:389
  36.3 4.6 %finish.1 = f32[16,2,64,1024]{3,2,1,0:T(8,128)} custom-call(f32[1,1024]{1,0:T(1,128)S(1)} %bitcast.11, bf16[16,64,128]{2,1,0:T(8,128)(2,1)S(1)} %gate.3.refs_4_.refs_0_, bf16[16,64,128]{2,1,0:T(8,128)(2,1)S(1)} %collective-permute-done.5.refs_1_, bf16[16,8,256,128]{3,2,1,0:T(8,128)(2,1)S(1)} %get-tuple-element.31.refs_2_, ...), custom_call_target="tpu_custom_call" | custom-call | flops 4400000000 | bytes 12000000 | tf_op jit(solution)/shard_map/finish/pallas_call | solution.py:372
  (20 shorter events, 0.1 us)
Async XLA Ops:
  0.0 11.6 %copy-start.1 = (s32[1024,256]{1,0:T(8,128)S(1)}, s32[1024,256]{1,0:T(8,128)}, u32[]{:S(2)}) copy-start(s32[1024,256]{1,0:T(8,128)} %own_mask.1) | copy-start | bytes 3145732
  0.0 11.6 %copy-start.2 = (f32[1024,256]{1,0:T(8,128)S(1)}, f32[1024,256]{1,0:T(8,128)}, u32[]{:S(2)}) copy-start(f32[1024,256]{1,0:T(8,128)} %own_slip.1) | copy-start | bytes 3145732
  0.0 11.6 %copy-start.5 = (f32[1024]{0:T(1024)S(1)}, f32[1024]{0:T(1024)}, u32[]{:S(2)}) copy-start(f32[1024]{0:T(1024)} %param.11) | copy-start | bytes 12292
  0.0 11.6 %copy-start.4 = (s32[1024]{0:T(1024)S(1)}, s32[1024]{0:T(1024)}, u32[]{:S(2)}) copy-start(s32[1024]{0:T(1024)} %param.10) | copy-start | bytes 12292
  0.0 11.6 %copy-start.3 = (f32[2,512]{1,0:T(2,128)S(1)}, f32[2,512]{1,0:T(2,128)}, u32[]{:S(2)}) copy-start(f32[2,512]{1,0:T(2,128)} %points_ref.1) | copy-start | bytes 12292
  0.0 11.5 %collective-permute-start.2 = (s32[1024,256]{1,0:T(8,128)}, s32[1024,256]{1,0:T(8,128)}, u32[]{:S(2)}, u32[]{:S(2)}) collective-permute-start(s32[1024,256]{1,0:T(8,128)} %own_mask.1), channel_id=1, source_target_pairs={{0,1},{1,0},{2,3},{3,2},{4,5},{5,4},{6,7},{7,6},{8,9},{9,8},{10,11... | collective-permute-start | bytes 3145736 | tf_op jit(solution)/shard_map/ppermute | solution.py:385
  0.5 11.0 %collective-permute-start.3 = (f32[1024,256]{1,0:T(8,128)}, f32[1024,256]{1,0:T(8,128)}, u32[]{:S(2)}, u32[]{:S(2)}) collective-permute-start(f32[1024,256]{1,0:T(8,128)} %own_slip.1), channel_id=1, source_target_pairs={{0,1},{1,0},{2,3},{3,2},{4,5},{5,4},{6,7},{7,6},{8,9},{9,8},{10,11... | collective-permute-start | bytes 3145736 | tf_op jit(solution)/shard_map/ppermute | solution.py:385
  3.0 1.6 %collective-permute-start = (bf16[16,32,128]{2,1,0:T(8,128)(2,1)S(1)}, bf16[16,32,128]{2,1,0:T(8,128)(2,1)S(1)}, u32[]{:S(2)}, u32[]{:S(2)}) collective-permute-start(bf16[16,32,128]{2,1,0:T(8,128)(2,1)S(1)} %get-tuple-element.22), channel_id=1, source_target_pairs={{0,1},{1,0},{2,3},{3,2},{4,5},{5,4},{6,7},{7,6},{8,9},{9,8},{10,11... | collective-permute-start | bytes 393224 | tf_op jit(solution)/shard_map/ppermute | solution.py:385
  4.5 12.1 %collective-permute-start.4 = (bf16[16,64,128]{2,1,0:T(8,128)(2,1)S(1)}, bf16[16,64,128]{2,1,0:T(8,128)(2,1)S(1)}, u32[]{:S(2)}, u32[]{:S(2)}) collective-permute-start(bf16[16,64,128]{2,1,0:T(8,128)(2,1)S(1)} %constant_dynamic-update-slice_fusion.after_ref.refs_4_), channel_id=1, source_target_pairs={{0,4},{2,6},{4,0},{6,2},{8,12},{10,14},{12,8},{14,10},{1,5},{3,7},... | collective-permute-start | bytes 786440 | tf_op jit(solution)/shard_map/ppermute | solution.py:389
  7.6 14.5 %collective-permute-start.1 = (bf16[16,64,128]{2,1,0:T(8,128)(2,1)S(1)}, bf16[16,64,128]{2,1,0:T(8,128)(2,1)S(1)}, u32[]{:S(2)}, u32[]{:S(2)}) collective-permute-start(bf16[16,64,128]{2,1,0:T(8,128)(2,1)S(1)} %constant_dynamic-update-slice_fusion.after_ref.refs_4_), channel_id=1, source_target_pairs={{0,12},{2,14},{4,8},{6,10},{8,4},{10,6},{12,0},{14,2},{1,13},{3,15... | collective-permute-start | bytes 786440 | tf_op jit(solution)/shard_map/ppermute | solution.py:389
  10.0 18.6 %collective-permute-start.8 = (bf16[16,64,128]{2,1,0:T(8,128)(2,1)S(1)}, bf16[16,64,128]{2,1,0:T(8,128)(2,1)S(1)}, u32[]{:S(2)}, u32[]{:S(2)}) collective-permute-start(bf16[16,64,128]{2,1,0:T(8,128)(2,1)S(1)} %constant_dynamic-update-slice_fusion.after_ref.refs_4_), channel_id=1, source_target_pairs={{0,2},{2,0},{4,6},{6,4},{8,10},{10,8},{12,14},{14,12},{1,3},{3,1},... | collective-permute-start | bytes 786440 | tf_op jit(solution)/shard_map/ppermute | solution.py:389
  16.7 11.9 %collective-permute-start.9 = (bf16[16,64,128]{2,1,0:T(8,128)(2,1)S(1)}, bf16[16,64,128]{2,1,0:T(8,128)(2,1)S(1)}, u32[]{:S(2)}, u32[]{:S(2)}) collective-permute-start(bf16[16,64,128]{2,1,0:T(8,128)(2,1)S(1)} %gate.2.refs_0_.refs_7_), channel_id=1, source_target_pairs={{0,2},{2,0},{4,6},{6,4},{8,10},{10,8},{12,14},{14,12},{1,3},{3,1},... | collective-permute-start | bytes 786440 | tf_op jit(solution)/shard_map/ppermute | solution.py:389
  22.1 11.7 %collective-permute-start.5 = (bf16[16,64,128]{2,1,0:T(8,128)(2,1)S(1)}, bf16[16,64,128]{2,1,0:T(8,128)(2,1)S(1)}, u32[]{:S(2)}, u32[]{:S(2)}) collective-permute-start(bf16[16,64,128]{2,1,0:T(8,128)(2,1)S(1)} %gate.3.refs_4_.refs_0_), channel_id=1, source_target_pairs={{0,2},{2,0},{4,6},{6,4},{8,10},{10,8},{12,14},{14,12},{1,3},{3,1},... | collective-permute-start | bytes 786440 | tf_op jit(solution)/shard_map/ppermute | solution.py:389
  23.6 10.2 %collective-permute-start.6 = (bf16[16,64,128]{2,1,0:T(8,128)(2,1)S(1)}, bf16[16,64,128]{2,1,0:T(8,128)(2,1)S(1)}, u32[]{:S(2)}, u32[]{:S(2)}) collective-permute-start(bf16[16,64,128]{2,1,0:T(8,128)(2,1)S(1)} %gate.3.refs_4_.refs_0_), channel_id=1, source_target_pairs={{0,4},{2,6},{4,0},{6,2},{8,12},{10,14},{12,8},{14,10},{1,5},{3,7},... | collective-permute-start | bytes 786440 | tf_op jit(solution)/shard_map/ppermute | solution.py:389
  24.2 12.2 %collective-permute-start.7 = (bf16[16,64,128]{2,1,0:T(8,128)(2,1)S(1)}, bf16[16,64,128]{2,1,0:T(8,128)(2,1)S(1)}, u32[]{:S(2)}, u32[]{:S(2)}) collective-permute-start(bf16[16,64,128]{2,1,0:T(8,128)(2,1)S(1)} %gate.3.refs_4_.refs_0_), channel_id=1, source_target_pairs={{0,6},{2,4},{4,2},{6,0},{8,14},{10,12},{12,10},{14,8},{1,7},{3,5},... | collective-permute-start | bytes 786440 | tf_op jit(solution)/shard_map/ppermute | solution.py:389
  28.6 7.7 %copy-start = (f32[1024]{0:T(1024)S(1)}, f32[1024]{0:T(1024)}, u32[]{:S(2)}) copy-start(f32[1024]{0:T(1024)} %param.12) | copy-start | bytes 12292

commit v8 on v7

--- a/solution.py
+++ b/solution.py
@@ -442,7 +442,7 @@
         pairs.append((exchange(pieces[2], 2), exchange(pieces[2], 3)))
     slips_2, token = step((2,), after=pieces[2:3])
     slips_3, total, token = step((3,), ((pairs[0], slips_0), (pairs[1], slips_1)), after=(token,), unroll=8)
-    return finish(rise_time, ((pairs[2], slips_2), (pairs[3], slips_3)), total, unroll=8)
+    return finish(rise_time, ((pairs[2], slips_2), (pairs[3], slips_3)), total, unroll=16)
 
 
 def solution(mesh):

time: 41.1 us -> 41 us (level)
  transfers between devices with their start and end apart: 10 -> 10, of which waited for: 3 -> 3; matrix products, arithmetic and copies ran while one was open for 0% -> 0% of each run, Pallas kernels for 45% -> 46%
where the time goes in v8:
time: 41 us; the launch traced here: 40.9 us
  Pallas kernels  23.1 us (56%)
  starting transfers between devices  12.2 us (30%)
  waiting for transfers between devices  5.26 us (13%)
    pallas_call x3, Pallas kernels, work(): pl.pallas_call(functools.partial(work_kernel, fills, len(sums), total is...  11.2 us
    ppermute x7, starting transfers between devices, exchange(): return lax.ppermute(piece, 'var', [(i, i ^ bits) for i in range(2 * UNITS)])  11.1 us
    pallas_call x1, Pallas kernels, finish(): pl.pallas_call(functools.partial(finish_kernel, len(sums), unroll), out_s...  4.51 us
    ppermute x7, waiting for transfers between devices, exchange(): return lax.ppermute(piece, 'var', [(i, i ^ bits) for i in range(2 * UNITS)])  4.3 us
    pallas_call x1, Pallas kernels, late_fill(): pl.pallas_call(functools.partial(late_fill_kernel, unit), out_shape=(jax....  3.03 us
    pallas_call x1, Pallas kernels, rotate(): pl.pallas_call(rotate_kernel, out_shape=(piece, piece), in_specs=[ANY] *...  2.32 us
    pallas_call x1, Pallas kernels, prepare(): pl.pallas_call(prepare_kernel, out_shape=(out, out, columns, spots, TOKEN...  2.01 us
    ppermute x3, starting transfers between devices, swap(): return lax.ppermute(array, axis, [(0, 1), (1, 0)])  1.12 us
  transfers between devices with their start and end apart: 10, of which 3 were waited for; matrix products, arithmetic and copies ran while one was open for 0% of the time, Pallas kernels for 46%

profile of v8, /device:TPU:0, one launch (start us, length us, event | category | flops | bytes accessed | tf_op | source)
XLA Modules:
  0.0 40.9 jit_solution(9686614067854434125)
XLA Ops:
  0.0 0.5 %collective-permute-start.2 = (s32[1024,256]{1,0:T(8,128)}, s32[1024,256]{1,0:T(8,128)}, u32[]{:S(2)}, u32[]{:S(2)}) collective-permute-start(s32[1024,256]{1,0:T(8,128)} %own_mask.1), channel_id=1, source_target_pairs={{0,1},{1,0},{2,3},{3,2},{4,5},{5,4},{6,7},{7,6},{8,9},{9,8},{10,11... | collective-permute-start | bytes 3145736 | tf_op jit(solution)/shard_map/ppermute | solution.py:385
  0.5 0.1 collective-permute-start.3
  0.6 2.3 %rotate.1 = (bf16[16,32,128]{2,1,0:T(8,128)(2,1)S(1)}, bf16[16,32,128]{2,1,0:T(8,128)(2,1)S(1)}) custom-call(bf16[2,6,32,16,128]{4,3,2,1,0:T(8,128)(2,1)} %bitcast.14, f32[6,256]{1,0:T(8,128)} %tensor_hbm.1, s32[1,128]{1,0:T(1,128)} %bitcast.15), custom_call_target="tpu_custom_call" | custom-call | flops 3300000000 | bytes 9000000 | tf_op jit(solution)/shard_map/rotate/pallas_call | solution.py:83
  3.0 0.5 %collective-permute-start = (bf16[16,32,128]{2,1,0:T(8,128)(2,1)S(1)}, bf16[16,32,128]{2,1,0:T(8,128)(2,1)S(1)}, u32[]{:S(2)}, u32[]{:S(2)}) collective-permute-start(bf16[16,32,128]{2,1,0:T(8,128)(2,1)S(1)} %get-tuple-element.22), channel_id=1, source_target_pairs={{0,1},{1,0},{2,3},{3,2},{4,5},{5,4},{6,7},{7,6},{8,9},{9,8},{10,11... | collective-permute-start | bytes 393224 | tf_op jit(solution)/shard_map/ppermute | solution.py:385
  3.5 0.1 stack.31.numbers_ref
  3.6 1.0 %collective-permute-done = bf16[16,32,128]{2,1,0:T(8,128)(2,1)S(1)} collective-permute-done((bf16[16,32,128]{2,1,0:T(8,128)(2,1)S(1)}, bf16[16,32,128]{2,1,0:T(8,128)(2,1)S(1)}, u32[]{:S(2)}, u32[]{:S(2)}) %collective-permute-start) | collective-permute-done | bytes 131104 | tf_op jit(solution)/shard_map/ppermute | solution.py:385
  4.5 3.0 %collective-permute-start.4 = (bf16[16,64,128]{2,1,0:T(8,128)(2,1)S(1)}, bf16[16,64,128]{2,1,0:T(8,128)(2,1)S(1)}, u32[]{:S(2)}, u32[]{:S(2)}) collective-permute-start(bf16[16,64,128]{2,1,0:T(8,128)(2,1)S(1)} %constant_dynamic-update-slice_fusion.after_ref.refs_4_), channel_id=1, source_target_pairs={{0,4},{2,6},{4,0},{6,2},{8,12},{10,14},{12,8},{14,10},{1,5},{3,7},... | collective-permute-start | bytes 786440 | tf_op jit(solution)/shard_map/ppermute | solution.py:389
  7.6 2.5 %collective-permute-start.1 = (bf16[16,64,128]{2,1,0:T(8,128)(2,1)S(1)}, bf16[16,64,128]{2,1,0:T(8,128)(2,1)S(1)}, u32[]{:S(2)}, u32[]{:S(2)}) collective-permute-start(bf16[16,64,128]{2,1,0:T(8,128)(2,1)S(1)} %constant_dynamic-update-slice_fusion.after_ref.refs_4_), channel_id=1, source_target_pairs={{0,12},{2,14},{4,8},{6,10},{8,4},{10,6},{12,0},{14,2},{1,13},{3,15... | collective-permute-start | bytes 786440 | tf_op jit(solution)/shard_map/ppermute | solution.py:389
  10.0 1.5 %collective-permute-start.8 = (bf16[16,64,128]{2,1,0:T(8,128)(2,1)S(1)}, bf16[16,64,128]{2,1,0:T(8,128)(2,1)S(1)}, u32[]{:S(2)}, u32[]{:S(2)}) collective-permute-start(bf16[16,64,128]{2,1,0:T(8,128)(2,1)S(1)} %constant_dynamic-update-slice_fusion.after_ref.refs_4_), channel_id=1, source_target_pairs={{0,2},{2,0},{4,6},{6,4},{8,10},{10,8},{12,14},{14,12},{1,3},{3,1},... | collective-permute-start | bytes 786440 | tf_op jit(solution)/shard_map/ppermute | solution.py:389
  11.6 2.0 %prepare.1 = (f32[256,1024]{1,0:T(8,128)S(1)}, f32[256,1024]{1,0:T(8,128)S(1)}, f32[2,512,128]{2,1,0:T(8,128)S(1)}, f32[8,1024]{1,0:T(8,128)S(1)}, f32[8,128]{1,0:T(8,128)S(1)}) custom-call(f32[2,512]{1,0:T(2,128)S(1)} %copy-done.3, s32[1,1024]{1,0:T(1,128)S(1)} %bitcast.12, f32[1,1024]{1,0:T(1,128)S(1)} %bitcast.13, s32[1024,256]{1,0:T(8,128)S(1)} %copy-done.1, ...), custom_call_target="tpu_custom_call" | custom-call | flops 3300000000 | bytes 9000000 | tf_op jit(solution)/shard_map/prepare/pallas_call | solution.py:157
  13.6 3.0 %fillfill.1 = (bf16[16,8,256,128]{3,2,1,0:T(8,128)(2,1)S(1)}, bf16[16,8,256,128]{3,2,1,0:T(8,128)(2,1)S(1)}, f32[8,128]{1,0:T(8,128)S(1)}) custom-call(s32[6]{0:T(128)S(1)} %stack.31.numbers_ref, f32[2,512,128]{2,1,0:T(8,128)S(1)} %get-tuple-element.23.refs_0_.columns, f32[8,1024]{1,0:T(8,128)S(1)} %get-tuple-element.24.refs_1_.spots, ...), custom_call_target="tpu_custom_call" | custom-call | flops 3300000000 | bytes 9000000 | tf_op jit(solution)/shard_map/fillfill/pallas_call | solution.py:323
  16.7 0.6 %collective-permute-start.9 = (bf16[16,64,128]{2,1,0:T(8,128)(2,1)S(1)}, bf16[16,64,128]{2,1,0:T(8,128)(2,1)S(1)}, u32[]{:S(2)}, u32[]{:S(2)}) collective-permute-start(bf16[16,64,128]{2,1,0:T(8,128)(2,1)S(1)} %gate.2.refs_0_.refs_7_), channel_id=1, source_target_pairs={{0,2},{2,0},{4,6},{6,4},{8,10},{10,8},{12,14},{14,12},{1,3},{3,1},... | collective-permute-start | bytes 786440 | tf_op jit(solution)/shard_map/ppermute | solution.py:389
  17.3 3.0 %late_fill.1 = (bf16[16,8,256,128]{3,2,1,0:T(8,128)(2,1)S(1)}, f32[8,128]{1,0:T(8,128)S(1)}) custom-call(s32[6]{0:T(128)S(1)} %stack.31.numbers_ref, f32[2,512,128]{2,1,0:T(8,128)S(1)} %get-tuple-element.23.refs_0_.columns, f32[8,1024]{1,0:T(8,128)S(1)} %get-tuple-element.24.refs_1_.spots, ...), custom_call_target="tpu_custom_call", output_to_operand_aliasing={{0}: (5, {})} | custom-call | flops 3300000000 | bytes 9000000 | tf_op jit(solution)/shard_map/late_fill/pallas_call | solution.py:249
  20.3 1.8 %collective-permute-done.1.array_ref = bf16[16,64,128]{2,1,0:T(8,128)(2,1)S(1)} collective-permute-done((bf16[16,64,128]{2,1,0:T(8,128)(2,1)S(1)}, bf16[16,64,128]{2,1,0:T(8,128)(2,1)S(1)}, u32[]{:S(2)}, u32[]{:S(2)}) %collective-permute-start.1) | collective-permute-done | bytes 262176 | tf_op jit(solution)/shard_map/ppermute | solution.py:389
  22.1 1.5 %collective-permute-start.5 = (bf16[16,64,128]{2,1,0:T(8,128)(2,1)S(1)}, bf16[16,64,128]{2,1,0:T(8,128)(2,1)S(1)}, u32[]{:S(2)}, u32[]{:S(2)}) collective-permute-start(bf16[16,64,128]{2,1,0:T(8,128)(2,1)S(1)} %gate.3.refs_4_.refs_0_), channel_id=1, source_target_pairs={{0,2},{2,0},{4,6},{6,4},{8,10},{10,8},{12,14},{14,12},{1,3},{3,1},... | collective-permute-start | bytes 786440 | tf_op jit(solution)/shard_map/ppermute | solution.py:389
  23.6 0.6 %collective-permute-start.6 = (bf16[16,64,128]{2,1,0:T(8,128)(2,1)S(1)}, bf16[16,64,128]{2,1,0:T(8,128)(2,1)S(1)}, u32[]{:S(2)}, u32[]{:S(2)}) collective-permute-start(bf16[16,64,128]{2,1,0:T(8,128)(2,1)S(1)} %gate.3.refs_4_.refs_0_), channel_id=1, source_target_pairs={{0,4},{2,6},{4,0},{6,2},{8,12},{10,14},{12,8},{14,10},{1,5},{3,7},... | collective-permute-start | bytes 786440 | tf_op jit(solution)/shard_map/ppermute | solution.py:389
  24.2 1.4 %collective-permute-start.7 = (bf16[16,64,128]{2,1,0:T(8,128)(2,1)S(1)}, bf16[16,64,128]{2,1,0:T(8,128)(2,1)S(1)}, u32[]{:S(2)}, u32[]{:S(2)}) collective-permute-start(bf16[16,64,128]{2,1,0:T(8,128)(2,1)S(1)} %gate.3.refs_4_.refs_0_), channel_id=1, source_target_pairs={{0,6},{2,4},{4,2},{6,0},{8,14},{10,12},{12,10},{14,8},{1,7},{3,5},... | collective-permute-start | bytes 786440 | tf_op jit(solution)/shard_map/ppermute | solution.py:389
  25.6 3.0 %fill.1 = (bf16[16,8,256,128]{3,2,1,0:T(8,128)(2,1)S(1)}, f32[8,128]{1,0:T(8,128)S(1)}) custom-call(s32[6]{0:T(128)S(1)} %stack.31.numbers_ref, f32[2,512,128]{2,1,0:T(8,128)S(1)} %get-tuple-element.23.refs_0_.columns, f32[8,1024]{1,0:T(8,128)S(1)} %get-tuple-element.24.refs_1_.spots, f32[256,1024]{1,0:T(8,128)S(1)} %get-tuple-element.25.refs_2_.own_ref, ...), custom_call_target="tpu_custom_call" | custom-call | flops 3300000000 | bytes 9000000 | tf_op jit(solution)/shard_map/fill/pallas_call | solution.py:323
  28.6 0.0 collective-permute-done.8.refs_5_
  28.6 0.0 copy-start
  28.6 5.2 %fillsumsum.1 = (bf16[16,8,256,128]{3,2,1,0:T(8,128)(2,1)S(1)}, f32[16,2,64,1024]{3,2,1,0:T(8,128)S(1)}, f32[8,128]{1,0:T(8,128)}) custom-call(s32[6]{0:T(128)S(1)} %stack.31.numbers_ref, f32[2,512,128]{2,1,0:T(8,128)S(1)} %get-tuple-element.23.refs_0_.columns, f32[8,1024]{1,0:T(8,128)S(1)} %get-tuple-element.24.refs_1_.spots, ...), custom_call_target="tpu_custom_call" | custom-call | flops 3300000000 | bytes 9000000 | tf_op jit(solution)/shard_map/fillsumsum/pallas_call | solution.py:323
  33.8 0.0 collective-permute-done.6.refs_3_
  33.8 2.5 %collective-permute-done.7.refs_4_ = bf16[16,64,128]{2,1,0:T(8,128)(2,1)S(1)} collective-permute-done((bf16[16,64,128]{2,1,0:T(8,128)(2,1)S(1)}, bf16[16,64,128]{2,1,0:T(8,128)(2,1)S(1)}, u32[]{:S(2)}, u32[]{:S(2)}) %collective-permute-start.7) | collective-permute-done | bytes 262176 | tf_op jit(solution)/shard_map/ppermute | solution.py:389
  36.3 4.5 %finish.1 = f32[16,2,64,1024]{3,2,1,0:T(8,128)} custom-call(f32[1,1024]{1,0:T(1,128)S(1)} %bitcast.11, bf16[16,64,128]{2,1,0:T(8,128)(2,1)S(1)} %gate.3.refs_4_.refs_0_, bf16[16,64,128]{2,1,0:T(8,128)(2,1)S(1)} %collective-permute-done.5.refs_1_, bf16[16,8,256,128]{3,2,1,0:T(8,128)(2,1)S(1)} %get-tuple-element.31.refs_2_, ...), custom_call_target="tpu_custom_call" | custom-call | flops 4400000000 | bytes 12000000 | tf_op jit(solution)/shard_map/finish/pallas_call | solution.py:372
  (20 shorter events, 0.1 us)
Async XLA Ops:
  0.0 11.6 %copy-start.1 = (s32[1024,256]{1,0:T(8,128)S(1)}, s32[1024,256]{1,0:T(8,128)}, u32[]{:S(2)}) copy-start(s32[1024,256]{1,0:T(8,128)} %own_mask.1) | copy-start | bytes 3145732
  0.0 11.6 %copy-start.2 = (f32[1024,256]{1,0:T(8,128)S(1)}, f32[1024,256]{1,0:T(8,128)}, u32[]{:S(2)}) copy-start(f32[1024,256]{1,0:T(8,128)} %own_slip.1) | copy-start | bytes 3145732
  0.0 11.6 %copy-start.5 = (f32[1024]{0:T(1024)S(1)}, f32[1024]{0:T(1024)}, u32[]{:S(2)}) copy-start(f32[1024]{0:T(1024)} %param.11) | copy-start | bytes 12292
  0.0 11.6 %copy-start.4 = (s32[1024]{0:T(1024)S(1)}, s32[1024]{0:T(1024)}, u32[]{:S(2)}) copy-start(s32[1024]{0:T(1024)} %param.10) | copy-start | bytes 12292
  0.0 11.6 %copy-start.3 = (f32[2,512]{1,0:T(2,128)S(1)}, f32[2,512]{1,0:T(2,128)}, u32[]{:S(2)}) copy-start(f32[2,512]{1,0:T(2,128)} %points_ref.1) | copy-start | bytes 12292
  0.0 11.5 %collective-permute-start.2 = (s32[1024,256]{1,0:T(8,128)}, s32[1024,256]{1,0:T(8,128)}, u32[]{:S(2)}, u32[]{:S(2)}) collective-permute-start(s32[1024,256]{1,0:T(8,128)} %own_mask.1), channel_id=1, source_target_pairs={{0,1},{1,0},{2,3},{3,2},{4,5},{5,4},{6,7},{7,6},{8,9},{9,8},{10,11... | collective-permute-start | bytes 3145736 | tf_op jit(solution)/shard_map/ppermute | solution.py:385
  0.5 11.0 %collective-permute-start.3 = (f32[1024,256]{1,0:T(8,128)}, f32[1024,256]{1,0:T(8,128)}, u32[]{:S(2)}, u32[]{:S(2)}) collective-permute-start(f32[1024,256]{1,0:T(8,128)} %own_slip.1), channel_id=1, source_target_pairs={{0,1},{1,0},{2,3},{3,2},{4,5},{5,4},{6,7},{7,6},{8,9},{9,8},{10,11... | collective-permute-start | bytes 3145736 | tf_op jit(solution)/shard_map/ppermute | solution.py:385
  3.0 1.6 %collective-permute-start = (bf16[16,32,128]{2,1,0:T(8,128)(2,1)S(1)}, bf16[16,32,128]{2,1,0:T(8,128)(2,1)S(1)}, u32[]{:S(2)}, u32[]{:S(2)}) collective-permute-start(bf16[16,32,128]{2,1,0:T(8,128)(2,1)S(1)} %get-tuple-element.22), channel_id=1, source_target_pairs={{0,1},{1,0},{2,3},{3,2},{4,5},{5,4},{6,7},{7,6},{8,9},{9,8},{10,11... | collective-permute-start | bytes 393224 | tf_op jit(solution)/shard_map/ppermute | solution.py:385
  4.5 12.1 %collective-permute-start.4 = (bf16[16,64,128]{2,1,0:T(8,128)(2,1)S(1)}, bf16[16,64,128]{2,1,0:T(8,128)(2,1)S(1)}, u32[]{:S(2)}, u32[]{:S(2)}) collective-permute-start(bf16[16,64,128]{2,1,0:T(8,128)(2,1)S(1)} %constant_dynamic-update-slice_fusion.after_ref.refs_4_), channel_id=1, source_target_pairs={{0,4},{2,6},{4,0},{6,2},{8,12},{10,14},{12,8},{14,10},{1,5},{3,7},... | collective-permute-start | bytes 786440 | tf_op jit(solution)/shard_map/ppermute | solution.py:389
  7.6 14.5 %collective-permute-start.1 = (bf16[16,64,128]{2,1,0:T(8,128)(2,1)S(1)}, bf16[16,64,128]{2,1,0:T(8,128)(2,1)S(1)}, u32[]{:S(2)}, u32[]{:S(2)}) collective-permute-start(bf16[16,64,128]{2,1,0:T(8,128)(2,1)S(1)} %constant_dynamic-update-slice_fusion.after_ref.refs_4_), channel_id=1, source_target_pairs={{0,12},{2,14},{4,8},{6,10},{8,4},{10,6},{12,0},{14,2},{1,13},{3,15... | collective-permute-start | bytes 786440 | tf_op jit(solution)/shard_map/ppermute | solution.py:389
  10.0 18.6 %collective-permute-start.8 = (bf16[16,64,128]{2,1,0:T(8,128)(2,1)S(1)}, bf16[16,64,128]{2,1,0:T(8,128)(2,1)S(1)}, u32[]{:S(2)}, u32[]{:S(2)}) collective-permute-start(bf16[16,64,128]{2,1,0:T(8,128)(2,1)S(1)} %constant_dynamic-update-slice_fusion.after_ref.refs_4_), channel_id=1, source_target_pairs={{0,2},{2,0},{4,6},{6,4},{8,10},{10,8},{12,14},{14,12},{1,3},{3,1},... | collective-permute-start | bytes 786440 | tf_op jit(solution)/shard_map/ppermute | solution.py:389
  16.7 11.9 %collective-permute-start.9 = (bf16[16,64,128]{2,1,0:T(8,128)(2,1)S(1)}, bf16[16,64,128]{2,1,0:T(8,128)(2,1)S(1)}, u32[]{:S(2)}, u32[]{:S(2)}) collective-permute-start(bf16[16,64,128]{2,1,0:T(8,128)(2,1)S(1)} %gate.2.refs_0_.refs_7_), channel_id=1, source_target_pairs={{0,2},{2,0},{4,6},{6,4},{8,10},{10,8},{12,14},{14,12},{1,3},{3,1},... | collective-permute-start | bytes 786440 | tf_op jit(solution)/shard_map/ppermute | solution.py:389
  22.1 11.7 %collective-permute-start.5 = (bf16[16,64,128]{2,1,0:T(8,128)(2,1)S(1)}, bf16[16,64,128]{2,1,0:T(8,128)(2,1)S(1)}, u32[]{:S(2)}, u32[]{:S(2)}) collective-permute-start(bf16[16,64,128]{2,1,0:T(8,128)(2,1)S(1)} %gate.3.refs_4_.refs_0_), channel_id=1, source_target_pairs={{0,2},{2,0},{4,6},{6,4},{8,10},{10,8},{12,14},{14,12},{1,3},{3,1},... | collective-permute-start | bytes 786440 | tf_op jit(solution)/shard_map/ppermute | solution.py:389
  23.6 10.2 %collective-permute-start.6 = (bf16[16,64,128]{2,1,0:T(8,128)(2,1)S(1)}, bf16[16,64,128]{2,1,0:T(8,128)(2,1)S(1)}, u32[]{:S(2)}, u32[]{:S(2)}) collective-permute-start(bf16[16,64,128]{2,1,0:T(8,128)(2,1)S(1)} %gate.3.refs_4_.refs_0_), channel_id=1, source_target_pairs={{0,4},{2,6},{4,0},{6,2},{8,12},{10,14},{12,8},{14,10},{1,5},{3,7},... | collective-permute-start | bytes 786440 | tf_op jit(solution)/shard_map/ppermute | solution.py:389
  24.2 12.2 %collective-permute-start.7 = (bf16[16,64,128]{2,1,0:T(8,128)(2,1)S(1)}, bf16[16,64,128]{2,1,0:T(8,128)(2,1)S(1)}, u32[]{:S(2)}, u32[]{:S(2)}) collective-permute-start(bf16[16,64,128]{2,1,0:T(8,128)(2,1)S(1)} %gate.3.refs_4_.refs_0_), channel_id=1, source_target_pairs={{0,6},{2,4},{4,2},{6,0},{8,14},{10,12},{12,10},{14,8},{1,7},{3,5},... | collective-permute-start | bytes 786440 | tf_op jit(solution)/shard_map/ppermute | solution.py:389
  28.6 7.7 %copy-start = (f32[1024]{0:T(1024)S(1)}, f32[1024]{0:T(1024)}, u32[]{:S(2)}) copy-start(f32[1024]{0:T(1024)} %param.12) | copy-start | bytes 12292
